TPU v7x, 256 devices: a whole 4x4x8 slice. The times are simulated.
256 devices in a mesh: section: 8 (over z), dp: 32 (over x, y, core).
Axes of the slice: x: 4, y: 4, z: 8, core: 2. Of those that a mesh axis runs over, the one named last changes fastest.
Arguments:
- out_grad: bfloat16 [2, 2048, 6144], P(None, 'dp'), may hold values from -6 to 6
- x_rows: bfloat16 [8, 2, 64, 6144], P('section'), may hold values from -6 to 6
- saved_u: bfloat16 [8, 2, 64, 5376], P('section', None, None, 'dp'), may hold values from -6 to 6
- w_up_t: bfloat16 [8, 5376, 6144], P('section', 'dp'), may hold values from -0.078125 to 0.078125
- w_down: bfloat16 [8, 5376, 6144], P('section', 'dp'), may hold values from -0.078125 to 0.078125
- gate: float32 [8, 2, 64], P('section', None, 'dp'), may hold values from 0.2 to 1
- route_tokens: int32 [8, 2, 64], P('section', None, 'dp'), may hold values from 0 to 63
- route_count: int32 [8, 2, 32], P('section', None, 'dp'), may hold values from 1 to 2, as said below
Outputs:
- in_grad: bfloat16 [8, 2, 2048, 6144], P('section', None, 'dp')
- grad_up_t: bfloat16 [8, 5376, 6144], P('section', 'dp')
- grad_down: bfloat16 [8, 5376, 6144], P('section', 'dp')
Inputs may be any that keep to these rules, and one draw needn't show every extreme that they name: `route_tokens`: a token index within the micro-batch rows of the slot's dp index. `route_count`: in every layer and micro-batch some dp index has all 2 slots live.
All inputs are finite; a program needn't handle non-finite values.
Results may differ from a plain program's by a relative error of at most 0.0059.
Values may be sent and summed in bfloat16 or wider, within the bound.
No kernel may reach another device: no remote copies, remote signals or barrier semaphores. Data moves between devices by JAX's collectives and lax.ppermute only.
A program may use at most 64 MiB of HBM per device.

v0:
```python
import jax
import jax.numpy as jnp
from jax import lax
from jax.sharding import PartitionSpec as P


def from_behind(block, axis, distance):
    devices = range(lax.axis_size(axis))
    route = [(i - distance, i) for i in devices if i - distance in devices]
    return lax.ppermute(block, axis, route)


def silu_pair(pre_activation):
    sigmoid_v = jax.nn.sigmoid(pre_activation)
    return (pre_activation * sigmoid_v, sigmoid_v * (1.0 + pre_activation * (1.0 - sigmoid_v)))


def per_device(out_grad, x_rows, saved_u, w_up_t, w_down, gate, route_tokens, route_count):
    section_count = lax.axis_size("section")
    dp_count = lax.axis_size("dp")
    section_index = lax.axis_index("section")
    micro_count = out_grad.shape[0]
    tok_rows = out_grad.shape[1]
    feature_count = out_grad.shape[2]
    slot_count = gate.shape[2]
    hid_rows = w_down.shape[1]
    tick_count = micro_count + section_count - 1
    down_proj = w_down[0]
    up_weights = w_up_t[0]
    is_top = section_index == section_count - 1
    incoming = jnp.zeros((tok_rows, feature_count), jnp.bfloat16)
    init_state = (
        incoming,
        jnp.zeros((micro_count, tok_rows, feature_count), jnp.bfloat16),
        jnp.zeros((hid_rows, feature_count), jnp.float32),
        jnp.zeros((hid_rows, feature_count), jnp.float32),
    )

    def tick_step(tick_index, loop_state):
        received, in_grad, grad_down, grad_up = loop_state
        micro_index = tick_index - (section_count - 1 - section_index)
        valid_tick = (micro_index >= 0) & (micro_index < micro_count)
        micro_pick = jnp.clip(micro_index, 0, micro_count - 1)
        top_grad = out_grad[micro_pick]
        grad_slab = jnp.where(is_top, top_grad, received)
        grad_slab = jnp.where(valid_tick, grad_slab, jnp.zeros_like(grad_slab))
        token_ids = route_tokens[0, micro_pick]
        live_count = route_count[0, micro_pick, 0]
        live_slots = jnp.arange(slot_count) < live_count
        weights = jnp.where(live_slots & valid_tick, gate[0, micro_pick], jnp.float32(0.0))
        scaled = (weights[:, None] * grad_slab[token_ids].astype(jnp.float32)).astype(jnp.bfloat16)
        activation_f, slope_factor = silu_pair(saved_u[0, micro_pick].astype(jnp.float32))
        activation = activation_f.astype(jnp.bfloat16)
        row_piece = lax.all_gather(scaled, "dp", axis=0, tiled=True)
        down_total = grad_down
        product = jnp.einsum("rd,hd->rh", row_piece, down_proj, preferred_element_type=jnp.float32)
        hidden_back = product
        down_total = down_total + jnp.einsum(
            "rh,rd->hd", activation, row_piece, preferred_element_type=jnp.float32
        )
        hidden_back, grad_down = (hidden_back, down_total)
        hidden_grad = (hidden_back * slope_factor).astype(jnp.bfloat16)
        grad_up = grad_up + jnp.einsum(
            "rh,rd->hd", hidden_grad, x_rows[0, micro_pick], preferred_element_type=jnp.float32
        )
        partial_value = jnp.dot(hidden_grad, up_weights, preferred_element_type=jnp.float32)
        partial_value = partial_value.reshape(dp_count, slot_count, feature_count)
        swapped = lax.all_to_all(partial_value, "dp", split_axis=0, concat_axis=0, tiled=True)
        own_rows = jnp.sum(swapped, axis=0)
        new_slab = grad_slab.astype(jnp.float32).at[token_ids].add(own_rows).astype(jnp.bfloat16)
        in_grad = jnp.where(
            valid_tick, lax.dynamic_update_index_in_dim(in_grad, new_slab, micro_pick, 0), in_grad
        )
        outgoing = from_behind(new_slab, "section", -1)
        return (outgoing, in_grad, grad_down, grad_up)

    final_state = lax.fori_loop(0, tick_count, tick_step, init_state)
    in_grad = final_state[1]
    grad_down = final_state[2]
    grad_up = final_state[3]
    return (in_grad[None], grad_up.astype(jnp.bfloat16)[None], grad_down.astype(jnp.bfloat16)[None])


def solution(mesh):
    return jax.shard_map(
        per_device,
        mesh=mesh,
        in_specs=(
            P(None, "dp", None),
            P("section", None, None, None),
            P("section", None, None, "dp"),
            P("section", "dp", None),
            P("section", "dp", None),
            P("section", None, "dp"),
            P("section", None, "dp"),
            P("section", None, "dp"),
        ),
        out_specs=(
            P("section", None, "dp", None),
            P("section", "dp", None),
            P("section", "dp", None),
        ),
        check_vma=False,
    )
```

profile of v0, /device:TPU:8, one launch (start us, length us, event | category | flops | bytes accessed | tf_op | source)
XLA Modules:
  0.0 813.2 jit_solution(1662078892205412703)
XLA Ops:
  2.1 805.1 %while.22 = (s32[]{:T(128)}, bf16[64,6144]{1,0:T(8,128)(2,1)S(1)}, bf16[2,64,6144]{2,1,0:T(8,128)(2,1)}, f32[168,6144]{1,0:T(8,128)}, f32[168,6144]{1,0:T(8,128)...) while((s32[]{:T(128)}, bf16[64,6144]{1,0:T(8,128)(2,1)S(1)}, ...), condition=%wide.region_3.4_spmd.clone, body=%wide.region_0.3_spmd.clone.sunk | while | flops 535180288 | bytes 95415840 | solution.py:77
  5.3 24.8 %all-gather.3 = bf16[32,2,6144]{2,1,0:T(2,128)(2,1)S(1)} all-gather(bf16[1,2,6144]{2,1,0:T(2,128)(2,1)S(1)} %fusion.55), channel_id=1, replica_groups=mesh['section'=8,'dp'=32] {'dp'}, dimensions={0}, use_global_device_ids=true | all-gather | bytes 811008 | tf_op jit(solution)/shard_map/while/body/eval_jaxpr/all_gather | solution.py:54
  30.5 2.5 fusion.56
  34.8 3.1 reshape.104
  37.9 5.8 all-to-all-start
  43.7 21.1 %all-to-all-done = f32[32,2,6144]{2,1,0:T(2,128)} async-done(((f32[32,2,6144]{2,1,0:T(2,128)}), f32[32,2,6144]{2,1,0:T(2,128)}, u32[]{:S(2)}, u32[]{:S(2)}) %all-to-all-start) | async-done | bytes 1572896 | tf_op jit(solution)/shard_map/while/body/eval_jaxpr/all_to_all | solution.py:68
  71.6 2.7 convolution_add_fusion.5
  76.4 15.0 %collective-permute-done = bf16[64,6144]{1,0:T(8,128)(2,1)S(1)} collective-permute-done((bf16[64,6144]{1,0:T(8,128)(2,1)S(1)}, bf16[64,6144]{1,0:T(8,128)(2,1)S(1)}, u32[]{:S(2)}, u32[]{:S(2)}) %collective-permute-start) | collective-permute-done | bytes 786464 | tf_op jit(solution)/shard_map/while/body/eval_jaxpr/ppermute | solution.py:10
  94.7 24.3 %all-gather.3 = bf16[32,2,6144]{2,1,0:T(2,128)(2,1)S(1)} all-gather(bf16[1,2,6144]{2,1,0:T(2,128)(2,1)S(1)} %fusion.55), channel_id=1, replica_groups=mesh['section'=8,'dp'=32] {'dp'}, dimensions={0}, use_global_device_ids=true | all-gather | bytes 811008 | tf_op jit(solution)/shard_map/while/body/eval_jaxpr/all_gather | solution.py:54
  119.3 2.5 fusion.56
  123.6 3.1 reshape.104
  126.8 5.6 all-to-all-start
  132.4 21.1 %all-to-all-done = f32[32,2,6144]{2,1,0:T(2,128)} async-done(((f32[32,2,6144]{2,1,0:T(2,128)}), f32[32,2,6144]{2,1,0:T(2,128)}, u32[]{:S(2)}, u32[]{:S(2)}) %all-to-all-start) | async-done | bytes 1572896 | tf_op jit(solution)/shard_map/while/body/eval_jaxpr/all_to_all | solution.py:68
  160.3 5.0 convolution_add_fusion.5
  166.8 13.4 %collective-permute-done = bf16[64,6144]{1,0:T(8,128)(2,1)S(1)} collective-permute-done((bf16[64,6144]{1,0:T(8,128)(2,1)S(1)}, bf16[64,6144]{1,0:T(8,128)(2,1)S(1)}, u32[]{:S(2)}, u32[]{:S(2)}) %collective-permute-start) | collective-permute-done | bytes 786464 | tf_op jit(solution)/shard_map/while/body/eval_jaxpr/ppermute | solution.py:10
  183.4 24.3 %all-gather.3 = bf16[32,2,6144]{2,1,0:T(2,128)(2,1)S(1)} all-gather(bf16[1,2,6144]{2,1,0:T(2,128)(2,1)S(1)} %fusion.55), channel_id=1, replica_groups=mesh['section'=8,'dp'=32] {'dp'}, dimensions={0}, use_global_device_ids=true | all-gather | bytes 811008 | tf_op jit(solution)/shard_map/while/body/eval_jaxpr/all_gather | solution.py:54
  208.0 2.5 fusion.56
  212.3 3.1 reshape.104
  215.5 5.6 all-to-all-start
  221.1 21.1 %all-to-all-done = f32[32,2,6144]{2,1,0:T(2,128)} async-done(((f32[32,2,6144]{2,1,0:T(2,128)}), f32[32,2,6144]{2,1,0:T(2,128)}, u32[]{:S(2)}, u32[]{:S(2)}) %all-to-all-start) | async-done | bytes 1572896 | tf_op jit(solution)/shard_map/while/body/eval_jaxpr/all_to_all | solution.py:68
  249.0 5.0 convolution_add_fusion.5
  255.4 13.4 %collective-permute-done = bf16[64,6144]{1,0:T(8,128)(2,1)S(1)} collective-permute-done((bf16[64,6144]{1,0:T(8,128)(2,1)S(1)}, bf16[64,6144]{1,0:T(8,128)(2,1)S(1)}, u32[]{:S(2)}, u32[]{:S(2)}) %collective-permute-start) | collective-permute-done | bytes 786464 | tf_op jit(solution)/shard_map/while/body/eval_jaxpr/ppermute | solution.py:10
  272.1 24.3 %all-gather.3 = bf16[32,2,6144]{2,1,0:T(2,128)(2,1)S(1)} all-gather(bf16[1,2,6144]{2,1,0:T(2,128)(2,1)S(1)} %fusion.55), channel_id=1, replica_groups=mesh['section'=8,'dp'=32] {'dp'}, dimensions={0}, use_global_device_ids=true | all-gather | bytes 811008 | tf_op jit(solution)/shard_map/while/body/eval_jaxpr/all_gather | solution.py:54
  296.7 2.5 fusion.56
  301.0 3.1 reshape.104
  304.1 5.6 all-to-all-start
  309.8 21.1 %all-to-all-done = f32[32,2,6144]{2,1,0:T(2,128)} async-done(((f32[32,2,6144]{2,1,0:T(2,128)}), f32[32,2,6144]{2,1,0:T(2,128)}, u32[]{:S(2)}, u32[]{:S(2)}) %all-to-all-start) | async-done | bytes 1572896 | tf_op jit(solution)/shard_map/while/body/eval_jaxpr/all_to_all | solution.py:68
  337.7 5.0 convolution_add_fusion.5
  344.1 14.6 %collective-permute-done = bf16[64,6144]{1,0:T(8,128)(2,1)S(1)} collective-permute-done((bf16[64,6144]{1,0:T(8,128)(2,1)S(1)}, bf16[64,6144]{1,0:T(8,128)(2,1)S(1)}, u32[]{:S(2)}, u32[]{:S(2)}) %collective-permute-start) | collective-permute-done | bytes 786464 | tf_op jit(solution)/shard_map/while/body/eval_jaxpr/ppermute | solution.py:10
  362.0 24.3 %all-gather.3 = bf16[32,2,6144]{2,1,0:T(2,128)(2,1)S(1)} all-gather(bf16[1,2,6144]{2,1,0:T(2,128)(2,1)S(1)} %fusion.55), channel_id=1, replica_groups=mesh['section'=8,'dp'=32] {'dp'}, dimensions={0}, use_global_device_ids=true | all-gather | bytes 811008 | tf_op jit(solution)/shard_map/while/body/eval_jaxpr/all_gather | solution.py:54
  390.9 3.1 reshape.104
  394.0 5.6 all-to-all-start
  399.6 21.1 %all-to-all-done = f32[32,2,6144]{2,1,0:T(2,128)} async-done(((f32[32,2,6144]{2,1,0:T(2,128)}), f32[32,2,6144]{2,1,0:T(2,128)}, u32[]{:S(2)}, u32[]{:S(2)}) %all-to-all-start) | async-done | bytes 1572896 | tf_op jit(solution)/shard_map/while/body/eval_jaxpr/all_to_all | solution.py:68
  427.5 5.0 convolution_add_fusion.5
  434.0 14.4 %collective-permute-done = bf16[64,6144]{1,0:T(8,128)(2,1)S(1)} collective-permute-done((bf16[64,6144]{1,0:T(8,128)(2,1)S(1)}, bf16[64,6144]{1,0:T(8,128)(2,1)S(1)}, u32[]{:S(2)}, u32[]{:S(2)}) %collective-permute-start) | collective-permute-done | bytes 786464 | tf_op jit(solution)/shard_map/while/body/eval_jaxpr/ppermute | solution.py:10
  451.7 24.3 %all-gather.3 = bf16[32,2,6144]{2,1,0:T(2,128)(2,1)S(1)} all-gather(bf16[1,2,6144]{2,1,0:T(2,128)(2,1)S(1)} %fusion.55), channel_id=1, replica_groups=mesh['section'=8,'dp'=32] {'dp'}, dimensions={0}, use_global_device_ids=true | all-gather | bytes 811008 | tf_op jit(solution)/shard_map/while/body/eval_jaxpr/all_gather | solution.py:54
  476.3 2.5 fusion.56
  480.6 3.1 reshape.104
  483.7 5.6 all-to-all-start
  489.3 21.1 %all-to-all-done = f32[32,2,6144]{2,1,0:T(2,128)} async-done(((f32[32,2,6144]{2,1,0:T(2,128)}), f32[32,2,6144]{2,1,0:T(2,128)}, u32[]{:S(2)}, u32[]{:S(2)}) %all-to-all-start) | async-done | bytes 1572896 | tf_op jit(solution)/shard_map/while/body/eval_jaxpr/all_to_all | solution.py:68
  517.3 5.0 convolution_add_fusion.5
  523.7 14.4 %collective-permute-done = bf16[64,6144]{1,0:T(8,128)(2,1)S(1)} collective-permute-done((bf16[64,6144]{1,0:T(8,128)(2,1)S(1)}, bf16[64,6144]{1,0:T(8,128)(2,1)S(1)}, u32[]{:S(2)}, u32[]{:S(2)}) %collective-permute-start) | collective-permute-done | bytes 786464 | tf_op jit(solution)/shard_map/while/body/eval_jaxpr/ppermute | solution.py:10
  541.4 24.3 %all-gather.3 = bf16[32,2,6144]{2,1,0:T(2,128)(2,1)S(1)} all-gather(bf16[1,2,6144]{2,1,0:T(2,128)(2,1)S(1)} %fusion.55), channel_id=1, replica_groups=mesh['section'=8,'dp'=32] {'dp'}, dimensions={0}, use_global_device_ids=true | all-gather | bytes 811008 | tf_op jit(solution)/shard_map/while/body/eval_jaxpr/all_gather | solution.py:54
  566.0 2.5 fusion.56
  570.3 3.1 reshape.104
  573.4 5.6 all-to-all-start
  579.0 21.1 %all-to-all-done = f32[32,2,6144]{2,1,0:T(2,128)} async-done(((f32[32,2,6144]{2,1,0:T(2,128)}), f32[32,2,6144]{2,1,0:T(2,128)}, u32[]{:S(2)}, u32[]{:S(2)}) %all-to-all-start) | async-done | bytes 1572896 | tf_op jit(solution)/shard_map/while/body/eval_jaxpr/all_to_all | solution.py:68
  607.0 5.0 convolution_add_fusion.5
  613.4 14.4 %collective-permute-done = bf16[64,6144]{1,0:T(8,128)(2,1)S(1)} collective-permute-done((bf16[64,6144]{1,0:T(8,128)(2,1)S(1)}, bf16[64,6144]{1,0:T(8,128)(2,1)S(1)}, u32[]{:S(2)}, u32[]{:S(2)}) %collective-permute-start) | collective-permute-done | bytes 786464 | tf_op jit(solution)/shard_map/while/body/eval_jaxpr/ppermute | solution.py:10
  631.1 24.3 %all-gather.3 = bf16[32,2,6144]{2,1,0:T(2,128)(2,1)S(1)} all-gather(bf16[1,2,6144]{2,1,0:T(2,128)(2,1)S(1)} %fusion.55), channel_id=1, replica_groups=mesh['section'=8,'dp'=32] {'dp'}, dimensions={0}, use_global_device_ids=true | all-gather | bytes 811008 | tf_op jit(solution)/shard_map/while/body/eval_jaxpr/all_gather | solution.py:54
  655.7 2.5 fusion.56
  660.0 3.1 reshape.104
  663.1 5.6 all-to-all-start
  668.8 21.1 %all-to-all-done = f32[32,2,6144]{2,1,0:T(2,128)} async-done(((f32[32,2,6144]{2,1,0:T(2,128)}), f32[32,2,6144]{2,1,0:T(2,128)}, u32[]{:S(2)}, u32[]{:S(2)}) %all-to-all-start) | async-done | bytes 1572896 | tf_op jit(solution)/shard_map/while/body/eval_jaxpr/all_to_all | solution.py:68
  696.7 5.0 convolution_add_fusion.5
  703.1 14.4 %collective-permute-done = bf16[64,6144]{1,0:T(8,128)(2,1)S(1)} collective-permute-done((bf16[64,6144]{1,0:T(8,128)(2,1)S(1)}, bf16[64,6144]{1,0:T(8,128)(2,1)S(1)}, u32[]{:S(2)}, u32[]{:S(2)}) %collective-permute-start) | collective-permute-done | bytes 786464 | tf_op jit(solution)/shard_map/while/body/eval_jaxpr/ppermute | solution.py:10
  720.8 24.3 %all-gather.3 = bf16[32,2,6144]{2,1,0:T(2,128)(2,1)S(1)} all-gather(bf16[1,2,6144]{2,1,0:T(2,128)(2,1)S(1)} %fusion.55), channel_id=1, replica_groups=mesh['section'=8,'dp'=32] {'dp'}, dimensions={0}, use_global_device_ids=true | all-gather | bytes 811008 | tf_op jit(solution)/shard_map/while/body/eval_jaxpr/all_gather | solution.py:54
  745.4 2.5 fusion.56
  749.7 3.1 reshape.104
  752.8 5.6 all-to-all-start
  758.5 21.1 %all-to-all-done = f32[32,2,6144]{2,1,0:T(2,128)} async-done(((f32[32,2,6144]{2,1,0:T(2,128)}), f32[32,2,6144]{2,1,0:T(2,128)}, u32[]{:S(2)}, u32[]{:S(2)}) %all-to-all-start) | async-done | bytes 1572896 | tf_op jit(solution)/shard_map/while/body/eval_jaxpr/all_to_all | solution.py:68
  786.4 5.0 convolution_add_fusion.5
  792.8 14.4 %collective-permute-done = bf16[64,6144]{1,0:T(8,128)(2,1)S(1)} collective-permute-done((bf16[64,6144]{1,0:T(8,128)(2,1)S(1)}, bf16[64,6144]{1,0:T(8,128)(2,1)S(1)}, u32[]{:S(2)}, u32[]{:S(2)}) %collective-permute-start) | collective-permute-done | bytes 786464 | tf_op jit(solution)/shard_map/while/body/eval_jaxpr/ppermute | solution.py:10
  807.2 6.0 convert_bitcast_fusion
  (211 shorter events, 125.9 us)
Async XLA Ops:
  0.6 1.4 copy-start.7
  0.6 1.4 copy-start.6
  0.7 1.4 copy-start.5
  0.7 1.4 copy-start.4
  30.4 2.5 copy-start.2
  37.9 26.9 %all-to-all-start = ((f32[32,2,6144]{2,1,0:T(2,128)}), f32[32,2,6144]{2,1,0:T(2,128)}, u32[]{:S(2)}, u32[]{:S(2)}) async-start(f32[32,2,6144]{2,1,0:T(2,128)} %reshape.104), calls=%async_computation | async-start | bytes 3145728 | tf_op jit(solution)/shard_map/while/body/eval_jaxpr/all_to_all | solution.py:68
  68.0 3.6 copy-start.3
  70.3 21.1 %collective-permute-start = (bf16[64,6144]{1,0:T(8,128)(2,1)S(1)}, bf16[64,6144]{1,0:T(8,128)(2,1)S(1)}, u32[]{:S(2)}, u32[]{:S(2)}) collective-permute-start(bf16[64,6144]{1,0:T(8,128)(2,1)S(1)} %get-tuple-element.527), channel_id=1, source_target_pairs={{32,0},{64,32},{96,64},{128,96},{160,128},{192,160},{224,192},{33,... | collective-permute-start | bytes 2359304 | tf_op jit(solution)/shard_map/while/body/eval_jaxpr/ppermute | solution.py:10
  71.6 3.4 copy-start
  76.4 15.1 %copy-start.1 = (f32[168,6144]{1,0:T(8,128)}, f32[168,6144]{1,0:T(8,128)S(1)}, u32[]{:S(2)}) copy-start(f32[168,6144]{1,0:T(8,128)S(1)} %convolution_add_fusion.4) | copy-start | bytes 12386308 | tf_op jit(solution)/shard_map/while
  119.3 2.5 copy-start.2
  126.8 26.7 %all-to-all-start = ((f32[32,2,6144]{2,1,0:T(2,128)}), f32[32,2,6144]{2,1,0:T(2,128)}, u32[]{:S(2)}, u32[]{:S(2)}) async-start(f32[32,2,6144]{2,1,0:T(2,128)} %reshape.104), calls=%async_computation | async-start | bytes 3145728 | tf_op jit(solution)/shard_map/while/body/eval_jaxpr/all_to_all | solution.py:68
  156.7 3.6 copy-start.3
  159.0 21.2 %collective-permute-start = (bf16[64,6144]{1,0:T(8,128)(2,1)S(1)}, bf16[64,6144]{1,0:T(8,128)(2,1)S(1)}, u32[]{:S(2)}, u32[]{:S(2)}) collective-permute-start(bf16[64,6144]{1,0:T(8,128)(2,1)S(1)} %get-tuple-element.527), channel_id=1, source_target_pairs={{32,0},{64,32},{96,64},{128,96},{160,128},{192,160},{224,192},{33,... | collective-permute-start | bytes 2359304 | tf_op jit(solution)/shard_map/while/body/eval_jaxpr/ppermute | solution.py:10
  160.3 5.0 copy-start
  166.7 13.4 %copy-start.1 = (f32[168,6144]{1,0:T(8,128)}, f32[168,6144]{1,0:T(8,128)S(1)}, u32[]{:S(2)}) copy-start(f32[168,6144]{1,0:T(8,128)S(1)} %convolution_add_fusion.4) | copy-start | bytes 12386308 | tf_op jit(solution)/shard_map/while
  208.0 2.5 copy-start.2
  215.5 26.7 %all-to-all-start = ((f32[32,2,6144]{2,1,0:T(2,128)}), f32[32,2,6144]{2,1,0:T(2,128)}, u32[]{:S(2)}, u32[]{:S(2)}) async-start(f32[32,2,6144]{2,1,0:T(2,128)} %reshape.104), calls=%async_computation | async-start | bytes 3145728 | tf_op jit(solution)/shard_map/while/body/eval_jaxpr/all_to_all | solution.py:68
  245.4 3.6 copy-start.3
  247.7 21.2 %collective-permute-start = (bf16[64,6144]{1,0:T(8,128)(2,1)S(1)}, bf16[64,6144]{1,0:T(8,128)(2,1)S(1)}, u32[]{:S(2)}, u32[]{:S(2)}) collective-permute-start(bf16[64,6144]{1,0:T(8,128)(2,1)S(1)} %get-tuple-element.527), channel_id=1, source_target_pairs={{32,0},{64,32},{96,64},{128,96},{160,128},{192,160},{224,192},{33,... | collective-permute-start | bytes 2359304 | tf_op jit(solution)/shard_map/while/body/eval_jaxpr/ppermute | solution.py:10
  249.0 5.0 copy-start
  255.4 13.4 %copy-start.1 = (f32[168,6144]{1,0:T(8,128)}, f32[168,6144]{1,0:T(8,128)S(1)}, u32[]{:S(2)}) copy-start(f32[168,6144]{1,0:T(8,128)S(1)} %convolution_add_fusion.4) | copy-start | bytes 12386308 | tf_op jit(solution)/shard_map/while
  296.7 2.5 copy-start.2
  304.1 26.7 %all-to-all-start = ((f32[32,2,6144]{2,1,0:T(2,128)}), f32[32,2,6144]{2,1,0:T(2,128)}, u32[]{:S(2)}, u32[]{:S(2)}) async-start(f32[32,2,6144]{2,1,0:T(2,128)} %reshape.104), calls=%async_computation | async-start | bytes 3145728 | tf_op jit(solution)/shard_map/while/body/eval_jaxpr/all_to_all | solution.py:68
  334.0 3.6 copy-start.3
  336.4 22.4 %collective-permute-start = (bf16[64,6144]{1,0:T(8,128)(2,1)S(1)}, bf16[64,6144]{1,0:T(8,128)(2,1)S(1)}, u32[]{:S(2)}, u32[]{:S(2)}) collective-permute-start(bf16[64,6144]{1,0:T(8,128)(2,1)S(1)} %get-tuple-element.527), channel_id=1, source_target_pairs={{32,0},{64,32},{96,64},{128,96},{160,128},{192,160},{224,192},{33,... | collective-permute-start | bytes 2359304 | tf_op jit(solution)/shard_map/while/body/eval_jaxpr/ppermute | solution.py:10
  337.7 5.0 copy-start
  344.1 14.6 %copy-start.1 = (f32[168,6144]{1,0:T(8,128)}, f32[168,6144]{1,0:T(8,128)S(1)}, u32[]{:S(2)}) copy-start(f32[168,6144]{1,0:T(8,128)S(1)} %convolution_add_fusion.4) | copy-start | bytes 12386308 | tf_op jit(solution)/shard_map/while
  386.6 2.5 copy-start.2
  394.0 26.7 %all-to-all-start = ((f32[32,2,6144]{2,1,0:T(2,128)}), f32[32,2,6144]{2,1,0:T(2,128)}, u32[]{:S(2)}, u32[]{:S(2)}) async-start(f32[32,2,6144]{2,1,0:T(2,128)} %reshape.104), calls=%async_computation | async-start | bytes 3145728 | tf_op jit(solution)/shard_map/while/body/eval_jaxpr/all_to_all | solution.py:68
  423.9 3.6 copy-start.3
  426.2 22.2 %collective-permute-start = (bf16[64,6144]{1,0:T(8,128)(2,1)S(1)}, bf16[64,6144]{1,0:T(8,128)(2,1)S(1)}, u32[]{:S(2)}, u32[]{:S(2)}) collective-permute-start(bf16[64,6144]{1,0:T(8,128)(2,1)S(1)} %get-tuple-element.527), channel_id=1, source_target_pairs={{32,0},{64,32},{96,64},{128,96},{160,128},{192,160},{224,192},{33,... | collective-permute-start | bytes 2359304 | tf_op jit(solution)/shard_map/while/body/eval_jaxpr/ppermute | solution.py:10
  427.5 5.0 copy-start
  434.0 14.4 %copy-start.1 = (f32[168,6144]{1,0:T(8,128)}, f32[168,6144]{1,0:T(8,128)S(1)}, u32[]{:S(2)}) copy-start(f32[168,6144]{1,0:T(8,128)S(1)} %convolution_add_fusion.4) | copy-start | bytes 12386308 | tf_op jit(solution)/shard_map/while
  476.3 2.5 copy-start.2
  483.7 26.7 %all-to-all-start = ((f32[32,2,6144]{2,1,0:T(2,128)}), f32[32,2,6144]{2,1,0:T(2,128)}, u32[]{:S(2)}, u32[]{:S(2)}) async-start(f32[32,2,6144]{2,1,0:T(2,128)} %reshape.104), calls=%async_computation | async-start | bytes 3145728 | tf_op jit(solution)/shard_map/while/body/eval_jaxpr/all_to_all | solution.py:68
  513.6 3.6 copy-start.3
  515.9 22.2 %collective-permute-start = (bf16[64,6144]{1,0:T(8,128)(2,1)S(1)}, bf16[64,6144]{1,0:T(8,128)(2,1)S(1)}, u32[]{:S(2)}, u32[]{:S(2)}) collective-permute-start(bf16[64,6144]{1,0:T(8,128)(2,1)S(1)} %get-tuple-element.527), channel_id=1, source_target_pairs={{32,0},{64,32},{96,64},{128,96},{160,128},{192,160},{224,192},{33,... | collective-permute-start | bytes 2359304 | tf_op jit(solution)/shard_map/while/body/eval_jaxpr/ppermute | solution.py:10
  517.2 5.0 copy-start
  523.7 14.4 %copy-start.1 = (f32[168,6144]{1,0:T(8,128)}, f32[168,6144]{1,0:T(8,128)S(1)}, u32[]{:S(2)}) copy-start(f32[168,6144]{1,0:T(8,128)S(1)} %convolution_add_fusion.4) | copy-start | bytes 12386308 | tf_op jit(solution)/shard_map/while
  566.0 2.5 copy-start.2
  573.4 26.7 %all-to-all-start = ((f32[32,2,6144]{2,1,0:T(2,128)}), f32[32,2,6144]{2,1,0:T(2,128)}, u32[]{:S(2)}, u32[]{:S(2)}) async-start(f32[32,2,6144]{2,1,0:T(2,128)} %reshape.104), calls=%async_computation | async-start | bytes 3145728 | tf_op jit(solution)/shard_map/while/body/eval_jaxpr/all_to_all | solution.py:68
  603.3 3.6 copy-start.3
  605.6 22.2 %collective-permute-start = (bf16[64,6144]{1,0:T(8,128)(2,1)S(1)}, bf16[64,6144]{1,0:T(8,128)(2,1)S(1)}, u32[]{:S(2)}, u32[]{:S(2)}) collective-permute-start(bf16[64,6144]{1,0:T(8,128)(2,1)S(1)} %get-tuple-element.527), channel_id=1, source_target_pairs={{32,0},{64,32},{96,64},{128,96},{160,128},{192,160},{224,192},{33,... | collective-permute-start | bytes 2359304 | tf_op jit(solution)/shard_map/while/body/eval_jaxpr/ppermute | solution.py:10
  606.9 5.0 copy-start
  613.4 14.4 %copy-start.1 = (f32[168,6144]{1,0:T(8,128)}, f32[168,6144]{1,0:T(8,128)S(1)}, u32[]{:S(2)}) copy-start(f32[168,6144]{1,0:T(8,128)S(1)} %convolution_add_fusion.4) | copy-start | bytes 12386308 | tf_op jit(solution)/shard_map/while
  655.7 2.5 copy-start.2
  663.1 26.7 %all-to-all-start = ((f32[32,2,6144]{2,1,0:T(2,128)}), f32[32,2,6144]{2,1,0:T(2,128)}, u32[]{:S(2)}, u32[]{:S(2)}) async-start(f32[32,2,6144]{2,1,0:T(2,128)} %reshape.104), calls=%async_computation | async-start | bytes 3145728 | tf_op jit(solution)/shard_map/while/body/eval_jaxpr/all_to_all | solution.py:68
  693.0 3.6 copy-start.3
  695.3 22.2 %collective-permute-start = (bf16[64,6144]{1,0:T(8,128)(2,1)S(1)}, bf16[64,6144]{1,0:T(8,128)(2,1)S(1)}, u32[]{:S(2)}, u32[]{:S(2)}) collective-permute-start(bf16[64,6144]{1,0:T(8,128)(2,1)S(1)} %get-tuple-element.527), channel_id=1, source_target_pairs={{32,0},{64,32},{96,64},{128,96},{160,128},{192,160},{224,192},{33,... | collective-permute-start | bytes 2359304 | tf_op jit(solution)/shard_map/while/body/eval_jaxpr/ppermute | solution.py:10
  696.6 5.0 copy-start
  703.1 14.4 %copy-start.1 = (f32[168,6144]{1,0:T(8,128)}, f32[168,6144]{1,0:T(8,128)S(1)}, u32[]{:S(2)}) copy-start(f32[168,6144]{1,0:T(8,128)S(1)} %convolution_add_fusion.4) | copy-start | bytes 12386308 | tf_op jit(solution)/shard_map/while
  745.4 2.5 copy-start.2
  752.8 26.7 %all-to-all-start = ((f32[32,2,6144]{2,1,0:T(2,128)}), f32[32,2,6144]{2,1,0:T(2,128)}, u32[]{:S(2)}, u32[]{:S(2)}) async-start(f32[32,2,6144]{2,1,0:T(2,128)} %reshape.104), calls=%async_computation | async-start | bytes 3145728 | tf_op jit(solution)/shard_map/while/body/eval_jaxpr/all_to_all | solution.py:68
  782.7 3.6 copy-start.3
  785.0 22.2 %collective-permute-start = (bf16[64,6144]{1,0:T(8,128)(2,1)S(1)}, bf16[64,6144]{1,0:T(8,128)(2,1)S(1)}, u32[]{:S(2)}, u32[]{:S(2)}) collective-permute-start(bf16[64,6144]{1,0:T(8,128)(2,1)S(1)} %get-tuple-element.527), channel_id=1, source_target_pairs={{32,0},{64,32},{96,64},{128,96},{160,128},{192,160},{224,192},{33,... | collective-permute-start | bytes 2359304 | tf_op jit(solution)/shard_map/while/body/eval_jaxpr/ppermute | solution.py:10
  786.3 5.0 copy-start
  792.8 14.4 %copy-start.1 = (f32[168,6144]{1,0:T(8,128)}, f32[168,6144]{1,0:T(8,128)S(1)}, u32[]{:S(2)}) copy-start(f32[168,6144]{1,0:T(8,128)S(1)} %convolution_add_fusion.4) | copy-start | bytes 12386308 | tf_op jit(solution)/shard_map/while
where the time goes:
time: 821 us; the launch traced here: 813 us
  waiting for transfers between devices  318 us (39%)
  blocking collectives  219 us (27%)
  matrix products  94.3 us (11%)
  other arithmetic  73.6 us (9%)
  starting transfers between devices  62.3 us (8%)
  local copies, waits for them, and re-layouts  43.5 us (5%)
    all_gather x9, blocking collectives, tick_step(): row_piece = lax.all_gather(scaled, 'dp', axis=0, tiled=True)  219 us
    all_to_all x9, waiting for transfers between devices, tick_step(): lax.all_to_all(partial_value, 'dp', split_axis=0, concat_axis=0, tiled=True)  190 us
    ppermute x9, waiting for transfers between devices, from_behind(): return lax.ppermute(block, axis, route)  128 us
    all_to_all x9, starting transfers between devices, tick_step(): lax.all_to_all(partial_value, 'dp', split_axis=0, concat_axis=0, tiled=True)  50.8 us
    dot_general x9, matrix products, tick_step(): jnp.einsum('rh,rd->hd', hidden_grad, x_rows[0, micro_pick], preferred_ele...  42.7 us
    reshape x9, local copies, waits for them, and re-layouts, tick_step(): partial_value = partial_value.reshape(dp_count, slot_count, feature_count)  28.1 us
    dot_general x9, matrix products, tick_step(): jnp.einsum('rd,hd->rh', row_piece, down_proj, preferred_element_type=jnp....  22.8 us
    select_n x9, other arithmetic, tick_step(): jnp.where(valid_tick, lax.dynamic_update_index_in_dim(in_grad, new_slab,...  20.6 us
  transfers between devices with their start and end apart: 18, of which 18 were waited for; matrix products, arithmetic and copies ran while one was open for 7% of the time, Pallas kernels for 0%

commit v1 on v0

v1 whole, which is shorter than its diff:
```python
import jax
import jax.numpy as jnp
from jax import lax
from jax.sharding import PartitionSpec as P

BF = jnp.bfloat16
F32 = jnp.float32
LANES = 128


def per_device(out_grad, x_rows, saved_u, w_up_t, w_down, gate, route_tokens, route_count):
    section_count = lax.axis_size("section")
    dp_count = lax.axis_size("dp")
    section_index = lax.axis_index("section")
    core = lax.axis_index("dp") % 2
    micro_count, tok_rows, width = out_grad.shape
    cap = gate.shape[2]
    hid = w_down.shape[1]
    chips = dp_count // 2
    slots = micro_count * cap
    same_core = [[2 * chip + c for chip in range(chips)] for c in range(2)]
    sibling = [(i, i ^ 1) for i in range(dp_count)]
    down = w_down[0]
    up = w_up_t[0]

    def spread(block, axis, count, groups=None):
        sent = jnp.broadcast_to(block[None], (count,) + block.shape)
        return lax.all_to_all(sent, axis, 0, 0, tiled=True, axis_index_groups=groups)

    tokens = route_tokens[0]
    live = jnp.arange(cap)[None, :] < route_count[0]
    weights = jnp.where(live, gate[0], jnp.float32(0.0)).reshape(slots)
    slot_micro = jnp.arange(slots) // cap
    token_flat = tokens.reshape(slots)
    live_flat = live.reshape(slots)
    pick = (slot_micro * tok_rows + token_flat)[:, None] == jnp.arange(micro_count * tok_rows)[None, :]
    first_rows = jnp.dot(
        pick.astype(BF), out_grad.reshape(micro_count * tok_rows, width), preferred_element_type=F32
    )
    twin = (
        (slot_micro[:, None] == slot_micro[None, :])
        & (token_flat[:, None] == token_flat[None, :])
        & live_flat[None, :]
    ).astype(F32)

    view = saved_u[0].reshape(micro_count, chips, 2, cap, hid).transpose(2, 1, 0, 3, 4)
    view = jnp.where(core == 0, view, view[::-1]).reshape(dp_count * slots, hid).astype(F32)
    sigmoid_v = jax.nn.sigmoid(view)
    activation = (view * sigmoid_v).astype(BF)
    slope = sigmoid_v * (1.0 + view * (1.0 - sigmoid_v))

    lanes = jnp.arange(LANES)

    def one_round(row_in, dp_note, section_note):
        scaled = (weights[:, None] * row_in).astype(BF)
        sent = jnp.concatenate([scaled, dp_note], axis=1)
        own = spread(sent, "dp", chips, same_core)
        other = lax.ppermute(own, "dp", sibling)
        gathered = jnp.stack([own, other])
        rows = gathered[..., :width].reshape(dp_count * slots, width)
        back = jnp.einsum("rd,hd->rh", rows, down, preferred_element_type=F32)
        hidden_grad = (back * slope).astype(BF)
        partial = jnp.dot(hidden_grad, up, preferred_element_type=F32)
        partial = partial.reshape(2, chips, slots, width)
        arrived = lax.ppermute(partial[1].astype(BF), "dp", sibling)
        pair_sum = (partial[0] + arrived.astype(F32)).astype(BF)
        swapped = lax.all_to_all(pair_sum, "dp", 0, 0, tiled=True, axis_index_groups=same_core)
        row_grad = jnp.sum(swapped.astype(F32), axis=0)
        total = jnp.dot(twin, row_grad, precision=lax.Precision.HIGHEST)
        new_rows = (row_in + total).astype(BF)
        news = spread(jnp.concatenate([new_rows, section_note], axis=1), "section", section_count)
        return rows, hidden_grad, news, gathered[..., width:]

    blank = jnp.zeros((slots, LANES), BF)
    note = jnp.where(lanes[None, :] == 0, token_flat[:, None], jnp.where(lanes[None, :] == 1, live_flat[:, None], 0)).astype(BF)
    rows, hidden_grad, news, _ = one_round(first_rows, blank, note)

    all_tokens = news[:, :, width].astype(jnp.int32).reshape(section_count, micro_count, cap)
    all_live = news[:, :, width + 1].astype(jnp.int32).reshape(section_count, micro_count, cap) > 0
    layer = jnp.arange(section_count)

    token_ids = jnp.arange(tok_rows)
    touched = jnp.any(
        (all_tokens[..., None] == token_ids) & all_live[..., None], axis=2
    )
    depth = jnp.max(jnp.sum(touched.astype(jnp.int32), axis=0))

    def last_touch(allowed):
        ids = jnp.where(touched & allowed[:, None, None], layer[:, None, None], section_count)
        return jnp.min(ids, axis=0)

    above = last_touch(layer > section_index)
    upto = last_touch(layer >= section_index)

    def source(last):
        match = (
            (last[:, :, None, None] == layer[None, None, :, None])
            & (all_tokens.transpose(1, 0, 2)[:, None] == token_ids[None, :, None, None])
            & all_live.transpose(1, 0, 2)[:, None]
        )
        first = match & (jnp.cumsum(match.astype(jnp.int32), axis=3) == 1)
        return first.astype(BF)

    eye = jnp.eye(micro_count, dtype=BF)
    above_source = source(above)
    own_pick = pick.reshape(slots, micro_count, tok_rows).astype(BF)
    slot_source = jnp.einsum("rmt,mtls->rlms", own_pick, above_source).reshape(slots, section_count * slots)
    has_source = jnp.sum(slot_source.astype(F32), axis=1, keepdims=True) > 0

    def next_rows(news):
        table = news[..., :width].reshape(section_count * slots, width)
        return jnp.where(has_source, jnp.dot(slot_source, table, preferred_element_type=F32), first_rows)

    depth_note = jnp.broadcast_to(depth.astype(BF), (slots, LANES))
    rows, hidden_grad, news, notes = one_round(next_rows(news), depth_note, blank)
    rounds = jnp.max(notes.astype(F32)).astype(jnp.int32)

    def more(state):
        return state[0] < rounds

    def again(state):
        rows, hidden_grad, news, _ = one_round(next_rows(state[3]), blank, blank)
        return (state[0] + 1, rows, hidden_grad, news)

    _, rows, hidden_grad, news = lax.while_loop(more, again, (jnp.int32(2), rows, hidden_grad, news))

    upto_source = jnp.einsum("mtls,mn->mtlns", source(upto), eye).reshape(
        micro_count, tok_rows, section_count * slots
    )
    touched_here = upto < section_count
    table = news[..., :width].reshape(section_count * slots, width)
    moved = jnp.einsum("mtk,kd->mtd", upto_source, table, preferred_element_type=F32)
    in_grad = jnp.where(touched_here[:, :, None], moved.astype(BF), out_grad)

    grad_down = jnp.einsum("rh,rd->hd", activation, rows, preferred_element_type=F32).astype(BF)
    ordered = hidden_grad.reshape(2, chips, micro_count, cap, hid)
    ordered = jnp.where(core == 0, ordered, ordered[::-1]).transpose(2, 1, 0, 3, 4)
    grad_up = jnp.einsum(
        "rh,rd->hd",
        ordered.reshape(micro_count * dp_count * cap, hid),
        x_rows[0].reshape(micro_count * dp_count * cap, width),
        preferred_element_type=F32,
    ).astype(BF)
    return (in_grad[None], grad_up[None], grad_down[None])


def solution(mesh):
    return jax.shard_map(
        per_device,
        mesh=mesh,
        in_specs=(
            P(None, "dp", None),
            P("section", None, None, None),
            P("section", None, None, "dp"),
            P("section", "dp", None),
            P("section", "dp", None),
            P("section", None, "dp"),
            P("section", None, "dp"),
            P("section", None, "dp"),
        ),
        out_specs=(
            P("section", None, "dp", None),
            P("section", "dp", None),
            P("section", "dp", None),
        ),
        check_vma=False,
    )
```

time: 821 us -> 254 us (0.31)
  waiting for transfers between devices: 318 us -> 66.1 us
  blocking collectives: 219 us -> 71.3 us
  matrix products: 94.3 us -> 24.2 us
  other arithmetic: 73.6 us -> 22.7 us
  starting transfers between devices: 62.3 us -> 26.4 us
    all_gather x9 -> x0, blocking collectives: 219 us -> none  [tick_step(): row_piece = lax.all_gather(scaled, 'dp', axis=0, tiled=True)]
    all_to_all x9 -> x5, waiting for transfers between devices: 190 us -> 59.5 us  [the longest x3 34.1 us: spread(): lax.all_to_all(sent, axis, 0, 0, tiled=True, axis_index_groups=groups)]
    ppermute x9 -> x6, waiting for transfers between devices: 128 us -> 6.61 us  [the longest x3 6.61 us: one_round(): other = lax.ppermute(own, 'dp', sibling)]
    all_to_all x0 -> x4, blocking collectives: none -> 71.3 us  [the longest x3 53.5 us: spread(): lax.all_to_all(sent, axis, 0, 0, tiled=True, axis_index_groups=groups)]
    dot_general x36 -> x15, matrix products: 94.3 us -> 24.2 us  [the longest x3 7.59 us: one_round(): partial = jnp.dot(hidden_grad, up, preferred_element_type=F32)]
    select_n x27 -> x3, other arithmetic: 26.6 us -> 0.08 us  [the longest x2 0.08 us: per_device(): weights = jnp.where(live, gate[0], jnp.float32(0.0)).reshape(slots)]
    all_to_all x9 -> x5, starting transfers between devices: 50.8 us -> 25.9 us  [the longest x3 15.4 us: spread(): lax.all_to_all(sent, axis, 0, 0, tiled=True, axis_index_groups=groups)]
    reshape x9, local copies, waits for them, and re-layouts: 28.1 us -> 10.5 us  [the longest x3 5.35 us: one_round(): rows = gathered[..., :width].reshape(dp_count * slots, width)]
  transfers between devices with their start and end apart: 18 -> 11, of which waited for: 18 -> 8; matrix products, arithmetic and copies ran while one was open for 7% -> 5% of each run, Pallas kernels for 0% -> 0%
where the time goes in v1:
time: 254 us; the launch traced here: 252 us
  blocking collectives  71.3 us (28%)
  waiting for transfers between devices  66.1 us (26%)
  local copies, waits for them, and re-layouts  39.1 us (15%)
  starting transfers between devices  26.4 us (10%)
  matrix products  24.2 us (10%)
  other arithmetic  22.7 us (9%)
    all_to_all x3, blocking collectives, spread(): lax.all_to_all(sent, axis, 0, 0, tiled=True, axis_index_groups=groups)  53.5 us
    all_to_all x3, waiting for transfers between devices, spread(): lax.all_to_all(sent, axis, 0, 0, tiled=True, axis_index_groups=groups)  34.1 us
    all_to_all x2, waiting for transfers between devices, one_round(): lax.all_to_all(pair_sum, 'dp', 0, 0, tiled=True, axis_index_groups=same_c...  25.4 us
    all_to_all x1, blocking collectives, one_round(): lax.all_to_all(pair_sum, 'dp', 0, 0, tiled=True, axis_index_groups=same_c...  17.9 us
    all_to_all x3, starting transfers between devices, spread(): lax.all_to_all(sent, axis, 0, 0, tiled=True, axis_index_groups=groups)  15.4 us
    all_to_all x2, starting transfers between devices, one_round(): lax.all_to_all(pair_sum, 'dp', 0, 0, tiled=True, axis_index_groups=same_c...  10.6 us
    convert_element_type x3, other arithmetic, one_round(): pair_sum = (partial[0] + arrived.astype(F32)).astype(BF)  7.95 us
    dot_general x3, matrix products, one_round(): partial = jnp.dot(hidden_grad, up, preferred_element_type=F32)  7.59 us
  transfers between devices with their start and end apart: 11, of which 8 were waited for; matrix products, arithmetic and copies ran while one was open for 5% of the time, Pallas kernels for 0%

profile of v1, /device:TPU:8, one launch (start us, length us, event | category | flops | bytes accessed | tf_op | source)
XLA Modules:
  0.0 252.3 jit_solution(11119165050799688797)
XLA Ops:
  0.6 0.9 reshape_squeeze.9
  1.5 0.7 iota_compare_fusion.6
  2.3 0.8 squeeze.26
  3.1 1.8 multiply_convert_fusion.2
  5.1 19.9 %all_to_all.54 = bf16[16,4,6272]{2,1,0:T(4,128)(2,1)S(1)} all-to-all(bf16[16,4,6272]{2,1,0:T(4,128)(2,1)S(1)} %broadcast_in_dim.111), channel_id=1, replica_groups={{0,2,4,6,8,10,12,14,16,18,20,22,24,26,28,30},{1,3,5,7,9,11,13,15,17,19,..., dimensions={0} | all-to-all | bytes 1605632 | tf_op jit(solution)/shard_map/all_to_all | solution.py:28
  25.5 2.0 collective-permute-done.2
  27.5 2.4 pad_maximum_fusion.1
  29.9 1.3 reshape.232
  31.2 6.4 %fusion.24 = f32[128,6144]{1,0:T(8,128)} fusion(bf16[128,6144]{1,0:T(8,128)(2,1)} %reshape.232, bf16[1,168,6144]{2,1,0:T(8,128)(2,1)} %param.13, bf16[1,168,6144]{2,1,0:T(8,128)(2,1)} %param.14, f32[128,168]{0,1:T(8,128)S(1)} %copy.78), kind=kOutput, calls=%fused_computation.48 | convolution fusion | flops 528675840 | bytes 8933376 | tf_op jit(solution)/shard_map/dot_general | solution.py:63
  37.6 1.5 slice.90
  39.1 1.2 convert_element_type.148
  40.4 1.3 slice-done.2
  41.7 1.6 squeeze.29
  43.3 2.9 %add_convert_fusion.2 = bf16[16,4,6144]{2,1,0:T(4,128)(2,1)} fusion(f32[16,4,6144]{2,1,0:T(4,128)} %squeeze.29, bf16[16,4,6144]{2,1,0:T(4,128)(2,1)} %collective-permute-done.3), kind=kLoop, calls=%fused_computation.43 | loop fusion | flops 1179648 | bytes 3145728 | tf_op jit(solution)/shard_map/convert_element_type | solution.py:66
  46.2 5.2 %all-to-all-start.4 = ((bf16[16,4,6144]{2,1,0:T(4,128)(2,1)}), bf16[16,4,6144]{2,1,0:T(4,128)(2,1)S(1)}, u32[]{:S(2)}, u32[]{:S(2)}) async-start(bf16[16,4,6144]{2,1,0:T(4,128)(2,1)} %add_convert_fusion.2), calls=%async_computation.4 | async-start | bytes 1572864 | tf_op jit(solution)/shard_map/all_to_all | solution.py:67
  51.6 13.6 %all-to-all-done.4 = bf16[16,4,6144]{2,1,0:T(4,128)(2,1)S(1)} async-done(((bf16[16,4,6144]{2,1,0:T(4,128)(2,1)}), bf16[16,4,6144]{2,1,0:T(4,128)(2,1)S(1)}, u32[]{:S(2)}, u32[]{:S(2)}) %all-to-all-start.4) | async-done | bytes 786464 | tf_op jit(solution)/shard_map/all_to_all | solution.py:67
  65.8 0.9 broadcast_in_dim.166
  66.7 8.5 %all-to-all-start.5 = ((bf16[8,4,6272]{2,1,0:T(4,128)(2,1)}), bf16[8,4,6272]{2,1,0:T(4,128)(2,1)S(1)}, u32[]{:S(2)}, u32[]{:S(2)}) async-start(bf16[8,4,6272]{2,1,0:T(4,128)(2,1)} %broadcast_in_dim.166), calls=%async_computation.5 | async-start | bytes 802816 | tf_op jit(solution)/shard_map/all_to_all | solution.py:28
  75.2 12.7 %all-to-all-done.5 = bf16[8,4,6272]{2,1,0:T(4,128)(2,1)S(1)} async-done(((bf16[8,4,6272]{2,1,0:T(4,128)(2,1)}), bf16[8,4,6272]{2,1,0:T(4,128)(2,1)S(1)}, u32[]{:S(2)}, u32[]{:S(2)}) %all-to-all-start.5) | async-done | bytes 401440 | tf_op jit(solution)/shard_map/all_to_all | solution.py:28
  92.0 16.3 %all_to_all.55 = bf16[16,4,6272]{2,1,0:T(4,128)(2,1)S(1)} all-to-all(bf16[16,4,6272]{2,1,0:T(4,128)(2,1)S(1)} %broadcast_in_dim.172), channel_id=1, replica_groups={{0,2,4,6,8,10,12,14,16,18,20,22,24,26,28,30},{1,3,5,7,9,11,13,15,17,19,..., dimensions={0} | all-to-all | bytes 1605632 | tf_op jit(solution)/shard_map/all_to_all | solution.py:28
  108.3 2.3 collective-permute-done.4
  110.6 0.9 copy-done.13
  111.5 2.1 fusion.21
  113.6 2.7 %reshape.236 = bf16[128,6144]{1,0:T(8,128)(2,1)S(1)} reshape(bf16[2,16,4,6144]{3,2,1,0:T(4,128)(2,1)} %fusion.21) | data formatting | bytes 3145728 | tf_op jit(solution)/shard_map/reshape | solution.py:60
  116.3 2.9 %fusion.23 = bf16[128,168]{0,1:T(8,128)(2,1)S(1)} fusion(bf16[128,6144]{1,0:T(8,128)(2,1)S(1)} %reshape.236, bf16[1,168,6144]{2,1,0:T(8,128)(2,1)} %param.14, f32[128,168]{0,1:T(8,128)S(1)} %copy.78), kind=kOutput, calls=%fused_computation.47 | convolution fusion | flops 264434688 | bytes 3766272 | tf_op jit(solution)/shard_map/rd,hd->rh/dot_general | solution.py:61
  119.9 1.6 copy-done.6
  121.6 1.2 convert_element_type.165
  122.9 1.3 slice-done.1
  124.2 1.6 squeeze.30
  125.8 3.0 %add_convert_fusion.1 = bf16[16,4,6144]{2,1,0:T(4,128)(2,1)} fusion(f32[16,4,6144]{2,1,0:T(4,128)} %squeeze.30, bf16[16,4,6144]{2,1,0:T(4,128)(2,1)} %collective-permute-done.5), kind=kLoop, calls=%fused_computation.41 | loop fusion | flops 1179648 | bytes 3145728 | tf_op jit(solution)/shard_map/convert_element_type | solution.py:66
  128.7 5.3 %all-to-all-start.7 = ((bf16[16,4,6144]{2,1,0:T(4,128)(2,1)}), bf16[16,4,6144]{2,1,0:T(4,128)(2,1)S(1)}, u32[]{:S(2)}, u32[]{:S(2)}) async-start(bf16[16,4,6144]{2,1,0:T(4,128)(2,1)} %add_convert_fusion.1), calls=%async_computation.7 | async-start | bytes 1572864 | tf_op jit(solution)/shard_map/all_to_all | solution.py:67
  136.1 11.7 %all-to-all-done.7 = bf16[16,4,6144]{2,1,0:T(4,128)(2,1)S(1)} async-done(((bf16[16,4,6144]{2,1,0:T(4,128)(2,1)}), bf16[16,4,6144]{2,1,0:T(4,128)(2,1)S(1)}, u32[]{:S(2)}, u32[]{:S(2)}) %all-to-all-start.7) | async-done | bytes 786464 | tf_op jit(solution)/shard_map/all_to_all | solution.py:67
  148.5 0.9 broadcast_in_dim.173
  149.4 3.5 %all-to-all-start.8 = ((bf16[8,4,6272]{2,1,0:T(4,128)(2,1)}), bf16[8,4,6272]{2,1,0:T(4,128)(2,1)S(1)}, u32[]{:S(2)}, u32[]{:S(2)}) async-start(bf16[8,4,6272]{2,1,0:T(4,128)(2,1)} %broadcast_in_dim.173), calls=%async_computation.8 | async-start | bytes 802816 | tf_op jit(solution)/shard_map/all_to_all | solution.py:28
  154.2 0.8 fusion.27
  155.7 0.7 broadcast_multiply_fusion
  156.4 1.4 fusion.31
  158.4 7.3 %all-to-all-done.8 = bf16[8,4,6272]{2,1,0:T(4,128)(2,1)S(1)} async-done(((bf16[8,4,6272]{2,1,0:T(4,128)(2,1)}), bf16[8,4,6272]{2,1,0:T(4,128)(2,1)S(1)}, u32[]{:S(2)}, u32[]{:S(2)}) %all-to-all-start.8) | async-done | bytes 401440 | tf_op jit(solution)/shard_map/all_to_all | solution.py:28
  165.7 71.8 %while.16 = (s32[]{:T(128)}, bf16[128,6144]{1,0:T(8,128)(2,1)}, bf16[128,168]{0,1:T(8,128)(2,1)}, bf16[8,4,6272]{2,1,0:T(4,128)(2,1)S(1)}, s32[]{:T(128)}, /*ind...) while((s32[]{:T(128)}, bf16[128,6144]{1,0:T(8,128)(2,1)}, ...), condition=%wide.wide.region_13.14_spmd.clone, body=%wide.wide.region_11.13_spmd.clone.sunk | while | flops 536488000 | bytes 66835332 | solution.py:125
  166.0 0.9 multiply_convert_fusion.7
  167.1 17.3 %all_to_all.56 = bf16[16,4,6272]{2,1,0:T(4,128)(2,1)S(1)} all-to-all(bf16[16,4,6272]{2,1,0:T(4,128)(2,1)S(1)} %broadcast_in_dim.203), channel_id=1, replica_groups={{0,2,4,6,8,10,12,14,16,18,20,22,24,26,28,30},{1,3,5,7,9,11,13,15,17,19,..., dimensions={0} | all-to-all | bytes 1605632 | tf_op jit(solution)/shard_map/while/body/all_to_all | solution.py:28
  184.4 2.3 collective-permute-done
  186.7 0.9 pad_maximum_fusion.6
  187.6 1.3 reshape.252
  188.9 2.9 %fusion.113 = bf16[128,168]{0,1:T(8,128)(2,1)S(1)} fusion(f32[128,168]{0,1:T(8,128)S(1)} %copy-done.15, bf16[128,6144]{1,0:T(8,128)(2,1)} %reshape.252, bf16[168,6144]{1,0:T(8,128)(2,1)} %get-tuple-element.451), kind=kOutput, calls=%fused_computation.10.clone.clone.1 | convolution fusion | flops 264284160 | bytes 3766272 | tf_op jit(solution)/shard_map/while/body/rd,hd->rh/dot_general | solution.py:61
  192.5 1.6 copy-done.1
  194.2 1.2 convert_element_type.256
  195.5 1.3 slice-done
  196.8 1.6 squeeze.35
  198.4 2.1 add_convert_fusion.5
  200.5 17.9 %all_to_all.57 = bf16[16,4,6144]{2,1,0:T(4,128)(2,1)S(1)} all-to-all(bf16[16,4,6144]{2,1,0:T(4,128)(2,1)S(1)} %add_convert_fusion.5), channel_id=1, replica_groups={{0,2,4,6,8,10,12,14,16,18,20,22,24,26,28,30},{1,3,5,7,9,11,13,15,17,19,..., dimensions={0} | all-to-all | bytes 1572864 | tf_op jit(solution)/shard_map/while/body/all_to_all | solution.py:67
  219.1 0.9 broadcast_in_dim.204
  219.9 3.5 %all-to-all-start.2 = ((bf16[8,4,6272]{2,1,0:T(4,128)(2,1)}), bf16[8,4,6272]{2,1,0:T(4,128)(2,1)S(1)}, u32[]{:S(2)}, u32[]{:S(2)}) async-start(bf16[8,4,6272]{2,1,0:T(4,128)(2,1)} %broadcast_in_dim.204), calls=%async_computation.2 | async-start | bytes 802816 | tf_op jit(solution)/shard_map/while/body/all_to_all | solution.py:28
  223.4 14.1 %all-to-all-done.2 = bf16[8,4,6272]{2,1,0:T(4,128)(2,1)S(1)} async-done(((bf16[8,4,6272]{2,1,0:T(4,128)(2,1)}), bf16[8,4,6272]{2,1,0:T(4,128)(2,1)S(1)}, u32[]{:S(2)}, u32[]{:S(2)}) %all-to-all-start.2) | async-done | bytes 401440 | tf_op jit(solution)/shard_map/while/body/all_to_all | solution.py:28
  237.5 0.9 slice.64
  238.4 1.1 reshape.245
  239.5 1.5 copy.85
  241.0 1.5 reshape.238
  242.5 0.8 copy.87
  243.4 0.7 copy.88
  244.1 1.5 reshape.239
  245.6 2.9 %fusion.15 = bf16[1,168,6144]{2,1,0:T(8,128)(2,1)} fusion(bf16[128,6144]{1,0:T(8,128)(2,1)S(1)} %copy-done.5, f32[128,168]{0,1:T(8,128)} %copy-done.18), kind=kOutput, calls=%fused_computation.25 | convolution fusion | flops 265380864 | bytes 3723264 | tf_op jit(solution)/shard_map/rh,rd->hd/dot_general | solution.py:135
  248.6 2.0 fusion.16
  250.6 1.7 fusion.18
  (140 shorter events, 12.6 us)
Async XLA Ops:
  0.6 247.9 %copy-start = (bf16[1,2,64,6144]{3,2,1,0:T(8,128)(2,1)S(1)}, bf16[1,2,64,6144]{3,2,1,0:T(8,128)(2,1)}, u32[]{:S(2)}) copy-start(bf16[1,2,64,6144]{3,2,1,0:T(8,128)(2,1)} %param.11) | copy-start | bytes 4718596
  1.5 146.6 %copy-start.28 = (s32[4]{0:T(128)}, s32[4]{0:T(128)S(1)}, u32[]{:S(2)}) copy-start(s32[4]{0:T(128)S(1)} %reshape_squeeze.9) | copy-start | bytes 52
  2.3 145.8 %copy-start.30 = (pred[4]{0:T(512)(128)(4,1)}, pred[4]{0:T(512)(128)(4,1)S(1)}, u32[]{:S(2)}) copy-start(pred[4]{0:T(512)(128)(4,1)S(1)} %lt.53) | copy-start | bytes 16
  4.9 86.7 %copy-start.10 = (f32[4,6144]{1,0:T(4,128)}, f32[4,6144]{1,0:T(4,128)S(1)}, u32[]{:S(2)}) copy-start(f32[4,6144]{1,0:T(4,128)S(1)} %get-tuple-element.414) | copy-start | bytes 294916
  4.9 20.2 %copy-start.21 = (bf16[1,2,64,168]{3,2,1,0:T(8,128)(2,1)S(1)}, bf16[1,2,64,168]{3,2,1,0:T(8,128)(2,1)}, u32[]{:S(2)}) copy-start(bf16[1,2,64,168]{3,2,1,0:T(8,128)(2,1)} %param.12) | copy-start | bytes 129028
  25.1 2.4 copy-start.14
  25.1 2.4 collective-permute-start.2
  25.5 109.9 %copy-start.18 = (f32[128,168]{0,1:T(8,128)}, f32[128,168]{0,1:T(8,128)S(1)}, u32[]{:S(2)}) copy-start(f32[128,168]{0,1:T(8,128)S(1)} %copy.78) | copy-start | bytes 258052
  40.3 1.4 slice-start.2
  40.3 3.0 %collective-permute-start.3 = (bf16[16,4,6144]{2,1,0:T(4,128)(2,1)}, bf16[16,4,6144]{2,1,0:T(4,128)(2,1)}, u32[]{:S(2)}, u32[]{:S(2)}) collective-permute-start(bf16[16,4,6144]{2,1,0:T(4,128)(2,1)} %convert_element_type.148), channel_id=1, source_target_pairs={{0,1},{1,0},{2,3},{3,2},{4,5},{5,4},{6,7},{7,6},{8,9},{9,8},{10,11... | collective-permute-start | bytes 2359304 | tf_op jit(solution)/shard_map/ppermute | solution.py:65
  46.2 19.0 %all-to-all-start.4 = ((bf16[16,4,6144]{2,1,0:T(4,128)(2,1)}), bf16[16,4,6144]{2,1,0:T(4,128)(2,1)S(1)}, u32[]{:S(2)}, u32[]{:S(2)}) async-start(bf16[16,4,6144]{2,1,0:T(4,128)(2,1)} %add_convert_fusion.2), calls=%async_computation.4 | async-start | bytes 1572864 | tf_op jit(solution)/shard_map/all_to_all | solution.py:67
  51.5 96.7 %copy-start.32 = (s32[4]{0:T(128)}, s32[4]{0:T(128)S(1)}, u32[]{:S(2)}) copy-start(s32[4]{0:T(128)S(1)} %and_select_fusion) | copy-start | bytes 52
  66.7 21.2 %all-to-all-start.5 = ((bf16[8,4,6272]{2,1,0:T(4,128)(2,1)}), bf16[8,4,6272]{2,1,0:T(4,128)(2,1)S(1)}, u32[]{:S(2)}, u32[]{:S(2)}) async-start(bf16[8,4,6272]{2,1,0:T(4,128)(2,1)} %broadcast_in_dim.166), calls=%async_computation.5 | async-start | bytes 802816 | tf_op jit(solution)/shard_map/all_to_all | solution.py:28
  88.1 4.0 %copy-start.22 = (s32[2,8,2]{1,2,0:T(2,128)}, s32[2,8,2]{1,2,0:T(2,128)S(1)}, u32[]{:S(2)}) copy-start(s32[2,8,2]{1,2,0:T(2,128)S(1)} %convert_bitcast_fusion) | copy-start | bytes 388
  88.5 3.1 %copy-start.23 = (pred[8,2,2]{0,2,1:T(4,128)(4,1)}, pred[8,2,2]{0,2,1:T(4,128)(4,1)S(1)}, u32[]{:S(2)}) copy-start(pred[8,2,2]{0,2,1:T(4,128)(4,1)S(1)} %gt.38) | copy-start | bytes 100
  108.3 2.3 copy-start.7
  108.3 2.3 collective-permute-start.4
  110.6 0.9 copy-start.13
  116.3 2.9 %copy-start.4 = (bf16[128,6144]{1,0:T(8,128)(2,1)}, bf16[128,6144]{1,0:T(8,128)(2,1)S(1)}, u32[]{:S(2)}) copy-start(bf16[128,6144]{1,0:T(8,128)(2,1)S(1)} %reshape.236) | copy-start | bytes 4718596
  116.3 2.9 %copy-start.2 = (bf16[1,168,6144]{2,1,0:T(8,128)(2,1)S(1)}, bf16[1,168,6144]{2,1,0:T(8,128)(2,1)}, u32[]{:S(2)}) copy-start(bf16[1,168,6144]{2,1,0:T(8,128)(2,1)} %param.13) | copy-start | bytes 6193156
  119.2 0.6 copy-start.16
  119.8 1.6 copy-start.6
  122.8 1.4 slice-start.1
  122.8 3.0 %collective-permute-start.5 = (bf16[16,4,6144]{2,1,0:T(4,128)(2,1)}, bf16[16,4,6144]{2,1,0:T(4,128)(2,1)}, u32[]{:S(2)}, u32[]{:S(2)}) collective-permute-start(bf16[16,4,6144]{2,1,0:T(4,128)(2,1)} %convert_element_type.165), channel_id=1, source_target_pairs={{0,1},{1,0},{2,3},{3,2},{4,5},{5,4},{6,7},{7,6},{8,9},{9,8},{10,11... | collective-permute-start | bytes 2359304 | tf_op jit(solution)/shard_map/ppermute | solution.py:65
  128.7 5.3 %copy-start.24 = (f32[1,2,2]{2,1,0:T(2,128)S(1)}, f32[1,2,2]{2,1,0:T(2,128)}, u32[]{:S(2)}) copy-start(f32[1,2,2]{2,1,0:T(2,128)} %param.15) | copy-start | bytes 52
  128.7 5.3 %copy-start.26 = (s32[1,2,1]{1,2,0:T(1,128)S(1)}, s32[1,2,1]{1,2,0:T(1,128)}, u32[]{:S(2)}) copy-start(s32[1,2,1]{1,2,0:T(1,128)} %param.17) | copy-start | bytes 28
  128.7 19.1 %all-to-all-start.7 = ((bf16[16,4,6144]{2,1,0:T(4,128)(2,1)}), bf16[16,4,6144]{2,1,0:T(4,128)(2,1)S(1)}, u32[]{:S(2)}, u32[]{:S(2)}) async-start(bf16[16,4,6144]{2,1,0:T(4,128)(2,1)} %add_convert_fusion.1), calls=%async_computation.7 | async-start | bytes 1572864 | tf_op jit(solution)/shard_map/all_to_all | solution.py:67
  134.1 22.3 %copy-start.8 = (bf16[16,4,6272]{2,1,0:T(4,128)(2,1)S(1)}, bf16[16,4,6272]{2,1,0:T(4,128)(2,1)}, u32[]{:S(2)}) copy-start(bf16[16,4,6272]{2,1,0:T(4,128)(2,1)} %copy-done.7) | copy-start | bytes 2408452
  134.1 1.9 copy-start.25
  148.1 7.6 %copy-start.27 = (bf16[2,2]{1,0:T(2,128)(2,1)S(1)}, bf16[2,2]{1,0:T(2,128)(2,1)}, u32[]{:S(2)}) copy-start(bf16[2,2]{1,0:T(2,128)(2,1)} %compare_convert_fusion) | copy-start | bytes 28
  148.5 17.3 %copy-start.11 = (f32[4,6144]{1,0:T(4,128)S(1)}, f32[4,6144]{1,0:T(4,128)}, u32[]{:S(2)}) copy-start(f32[4,6144]{1,0:T(4,128)} %copy-done.10) | copy-start | bytes 294916
  149.4 16.4 %all-to-all-start.8 = ((bf16[8,4,6272]{2,1,0:T(4,128)(2,1)}), bf16[8,4,6272]{2,1,0:T(4,128)(2,1)S(1)}, u32[]{:S(2)}, u32[]{:S(2)}) async-start(bf16[8,4,6272]{2,1,0:T(4,128)(2,1)} %broadcast_in_dim.173), calls=%async_computation.8 | async-start | bytes 802816 | tf_op jit(solution)/shard_map/all_to_all | solution.py:28
  154.2 11.5 %copy-start.29 = (s32[4]{0:T(128)S(1)}, s32[4]{0:T(128)}, u32[]{:S(2)}) copy-start(s32[4]{0:T(128)} %copy-done.28) | copy-start | bytes 52
  184.4 2.3 collective-permute-start
  187.6 1.3 copy-start.15
  188.9 2.9 %copy-start.3 = (bf16[168,6144]{1,0:T(8,128)(2,1)S(1)}, bf16[168,6144]{1,0:T(8,128)(2,1)}, u32[]{:S(2)}) copy-start(bf16[168,6144]{1,0:T(8,128)(2,1)} %get-tuple-element.453) | copy-start | bytes 6193156 | tf_op jit(solution)/shard_map/while
  191.8 0.6 copy-start.17
  192.5 1.6 copy-start.1
  195.4 1.4 slice-start
  195.4 3.0 %collective-permute-start.1 = (bf16[16,4,6144]{2,1,0:T(4,128)(2,1)}, bf16[16,4,6144]{2,1,0:T(4,128)(2,1)}, u32[]{:S(2)}, u32[]{:S(2)}) collective-permute-start(bf16[16,4,6144]{2,1,0:T(4,128)(2,1)} %convert_element_type.256), channel_id=1, source_target_pairs={{0,1},{1,0},{2,3},{3,2},{4,5},{5,4},{6,7},{7,6},{8,9},{9,8},{10,11... | collective-permute-start | bytes 2359304 | tf_op jit(solution)/shard_map/while/body/ppermute | solution.py:65
  200.4 18.2 %copy-start.31 = (pred[4]{0:T(512)(128)(4,1)S(1)}, pred[4]{0:T(512)(128)(4,1)}, u32[]{:S(2)}) copy-start(pred[4]{0:T(512)(128)(4,1)} %get-tuple-element.456) | copy-start | bytes 16 | tf_op jit(solution)/shard_map/while
  200.4 18.2 %copy-start.33 = (s32[4]{0:T(128)S(1)}, s32[4]{0:T(128)}, u32[]{:S(2)}) copy-start(s32[4]{0:T(128)} %get-tuple-element.454) | copy-start | bytes 52 | tf_op jit(solution)/shard_map/while
  218.3 19.2 %copy-start.12 = (f32[4,6144]{1,0:T(4,128)S(1)}, f32[4,6144]{1,0:T(4,128)}, u32[]{:S(2)}) copy-start(f32[4,6144]{1,0:T(4,128)} %get-tuple-element.484) | copy-start | bytes 294916 | tf_op jit(solution)/shard_map/while
  219.9 17.6 %all-to-all-start.2 = ((bf16[8,4,6272]{2,1,0:T(4,128)(2,1)}), bf16[8,4,6272]{2,1,0:T(4,128)(2,1)S(1)}, u32[]{:S(2)}, u32[]{:S(2)}) async-start(bf16[8,4,6272]{2,1,0:T(4,128)(2,1)} %broadcast_in_dim.204), calls=%async_computation.2 | async-start | bytes 802816 | tf_op jit(solution)/shard_map/while/body/all_to_all | solution.py:28
  237.5 8.1 %copy-start.5 = (bf16[128,6144]{1,0:T(8,128)(2,1)S(1)}, bf16[128,6144]{1,0:T(8,128)(2,1)}, u32[]{:S(2)}) copy-start(bf16[128,6144]{1,0:T(8,128)(2,1)} %get-tuple-element.467) | copy-start | bytes 4718596
  245.6 2.9 %copy-start.19 = (bf16[128,168]{1,0:T(8,128)(2,1)S(1)}, bf16[128,168]{1,0:T(8,128)(2,1)}, u32[]{:S(2)}) copy-start(bf16[128,168]{1,0:T(8,128)(2,1)} %reshape.239) | copy-start | bytes 129028
  248.6 2.0 copy-start.9
  248.6 2.0 copy-start.20

commit v2 on v1

v2 whole, which is shorter than its diff:
```python
import jax
import jax.numpy as jnp
from jax import lax
from jax.experimental import pallas as pl
from jax.experimental.pallas import tpu as pltpu
from jax.sharding import PartitionSpec as P

BF = jnp.bfloat16
F32 = jnp.float32
I32 = jnp.int32
LANES = 128
LATE = 2


def plan_kernel(sections, cap, tok_rows, info_ref, place_ref, round_ref, own_ref, source_ref, ready_ref, last_ref):
    slots = 2 * cap
    place = place_ref[0]
    rows = 2 * tok_rows

    def clear(t, carry):
        ready_ref[t] = 1
        last_ref[t] = -1
        return carry

    lax.fori_loop(0, rows, clear, 0)
    row_ids = lax.broadcasted_iota(I32, source_ref.shape, 0)
    source_ref[...] = jnp.full(source_ref.shape, -1, I32)

    def layer_step(step, most):
        layer = sections - 1 - step
        at = (layer ^ place) * (2 * slots)
        token = [info_ref[at + i] + (i // cap) * tok_rows for i in range(slots)]
        live = [info_ref[at + slots + i] for i in range(slots)]
        own = layer == place
        for i in range(slots):
            prior = last_ref[token[i]]
            own_ref[i] = jnp.where(own, prior, own_ref[i])
        given = []
        for i in range(slots):
            twin_before = jnp.int32(0)
            twin_after = jnp.int32(0)
            for k in range((i // cap) * cap, (i // cap) * cap + cap):
                same = jnp.where((token[k] == token[i]) & (live[k] > 0), 1, 0)
                if k < i:
                    twin_before = jnp.maximum(twin_before, same * given[k])
                elif k > i:
                    twin_after = twin_after + same
            when = ready_ref[token[i]]
            size = 1 + twin_after
            for _ in range(slots - 1):
                taken = jnp.int32(0)
                for k in range(i):
                    taken = taken + jnp.where(given[k] == when, 1, 0)
                when = jnp.where((when >= 2) & (taken + size > LATE), when + 1, when)
            when = jnp.where(twin_before > 0, twin_before, when)
            when = jnp.where(live[i] > 0, when, 0)
            given.append(when)
        for i in range(slots):
            round_ref[layer * slots + i] = given[i]
            most = jnp.maximum(most, given[i])
            ready_ref[token[i]] = jnp.where(live[i] > 0, given[i] + 1, ready_ref[token[i]])
            last_ref[token[i]] = jnp.where(live[i] > 0, layer * slots + i, last_ref[token[i]])
            hit = (row_ids == token[i]) & ((live[i] > 0) & (layer >= place))
            source_ref[...] = jnp.where(hit, layer * slots + i, source_ref[...])
        return most

    for i in range(slots):
        own_ref[i] = -1
    own_ref[slots] = lax.fori_loop(0, sections, layer_step, jnp.int32(1))


def plan(info, place, sections, cap, tok_rows):
    slots = 2 * cap
    smem = pl.BlockSpec(memory_space=pltpu.SMEM)
    return pl.pallas_call(
        lambda *refs: plan_kernel(sections, cap, tok_rows, *refs),
        in_specs=[smem, smem],
        out_specs=[smem, smem, pl.BlockSpec(memory_space=pltpu.VMEM)],
        out_shape=[
            jax.ShapeDtypeStruct((sections * slots,), I32),
            jax.ShapeDtypeStruct((slots + 1,), I32),
            jax.ShapeDtypeStruct((2 * tok_rows, LANES), I32),
        ],
        scratch_shapes=[pltpu.SMEM((2 * tok_rows,), I32), pltpu.SMEM((2 * tok_rows,), I32)],
        cost_estimate=pl.CostEstimate(flops=100000, bytes_accessed=70000, transcendentals=0),
    )(info, place)


def per_device(out_grad, x_rows, saved_u, w_up_t, w_down, gate, route_tokens, route_count):
    section_count = lax.axis_size("section")
    dp_count = lax.axis_size("dp")
    section_index = lax.axis_index("section")
    core = lax.axis_index("dp") % 2
    micro_count, tok_rows, width = out_grad.shape
    cap = gate.shape[2]
    hid = w_down.shape[1]
    chips = dp_count // 2
    slots = micro_count * cap
    same_core = [[2 * chip + c for chip in range(chips)] for c in range(2)]
    sibling = [(i, i ^ 1) for i in range(dp_count)]
    down = w_down[0]
    up = w_up_t[0]
    flat_out = out_grad.reshape(micro_count * tok_rows, width)

    def spread(block, axis, count, groups=None):
        sent = jnp.broadcast_to(block[None], (count,) + block.shape)
        return lax.all_to_all(sent, axis, 0, 0, tiled=True, axis_index_groups=groups)

    token_flat = route_tokens[0].reshape(slots)
    live = (jnp.arange(cap)[None, :] < route_count[0]).reshape(slots)
    weights = jnp.where(live, gate[0].reshape(slots), jnp.float32(0.0))
    slot_micro = jnp.arange(slots) // cap

    info = jnp.concatenate([token_flat, live.astype(I32)])[None]
    hop = 1
    while hop < section_count:
        arrived = lax.ppermute(info, "section", [(i, i ^ hop) for i in range(section_count)])
        info = jnp.concatenate([info, arrived])
        hop *= 2
    rounds_of, own_plan, source = plan(info.reshape(-1), section_index.reshape(1), section_count, cap, tok_rows)
    own_round = lax.dynamic_slice(rounds_of, (section_index * slots,), (slots,))
    own_source = own_plan[:slots]

    pick = (slot_micro * tok_rows + token_flat)[:, None] == jnp.arange(micro_count * tok_rows)[None, :]
    first_rows = jnp.dot(pick.astype(BF), flat_out, preferred_element_type=F32)
    twin = (
        (slot_micro[:, None] == slot_micro[None, :]) & (token_flat[:, None] == token_flat[None, :]) & live[None, :]
    ).astype(F32)

    view = saved_u[0].reshape(micro_count, chips, 2, cap, hid).transpose(2, 1, 0, 3, 4)
    view = jnp.where(core == 0, view, view[::-1]).reshape(dp_count, slots, hid).astype(F32)
    sigmoid_v = jax.nn.sigmoid(view)
    activation = (view * sigmoid_v).astype(BF)
    slope = sigmoid_v * (1.0 + view * (1.0 - sigmoid_v))

    def gather(sent):
        own = spread(sent, "dp", chips, same_core)
        other = lax.ppermute(own, "dp", sibling)
        return jnp.concatenate([own, other])

    def layer_pass(rows, slopes):
        count = rows.shape[1]
        back = jnp.einsum("rd,hd->rh", rows.reshape(dp_count * count, width), down, preferred_element_type=F32)
        hidden_grad = (back.reshape(dp_count, count, hid) * slopes).astype(BF)
        partial = jnp.dot(hidden_grad.reshape(dp_count * count, hid), up, preferred_element_type=F32)
        partial = partial.reshape(2, chips, count, width)
        arrived = lax.ppermute(partial[1].astype(BF), "dp", sibling)
        pair_sum = (partial[0] + arrived.astype(F32)).astype(BF)
        swapped = lax.all_to_all(pair_sum, "dp", 0, 0, tiled=True, axis_index_groups=same_core)
        return hidden_grad, jnp.sum(swapped.astype(F32), axis=0)

    rows = gather((weights[:, None] * first_rows).astype(BF))
    hidden_grad, row_grad = layer_pass(rows, slope)
    total = jnp.sum(twin[:, :, None] * row_grad[None], axis=1)
    new_rows = (first_rows + total).astype(BF)
    table = spread(new_rows, "section", section_count).reshape(section_count * slots, width)
    first_bf = first_rows.astype(BF)

    lanes = jnp.arange(LANES)
    late = jnp.arange(LATE)
    table_ids = jnp.arange(section_count * slots)

    def chosen(rounds, now):
        mine = rounds == now
        rank = jnp.cumsum(mine.astype(I32), axis=-1) - 1
        return mine[..., None, :] & (rank[..., None, :] == late[:, None])

    def send_rows(now, table):
        which = chosen(own_round, now)
        weight = jnp.sum(jnp.where(which, weights, 0.0), axis=1)
        from_table = jnp.any(which[:, :, None] & (own_source[:, None] == table_ids)[None], axis=1)
        from_first = which & (own_source < 0)[None, :]
        row_in = jnp.dot(from_table.astype(BF), table, preferred_element_type=F32) + jnp.dot(
            from_first.astype(BF), first_bf, preferred_element_type=F32
        )
        return which, row_in, (weight[:, None] * row_in).astype(BF)

    def finish(now, which, row_in, late_rows, all_rounds, rows, hidden_grad):
        taken = chosen(all_rounds, now)
        late_slope = jnp.sum(jnp.where(taken[..., None], slope[:, None], 0.0), axis=2)
        late_hidden, row_grad = layer_pass(late_rows, late_slope)
        for c in range(LATE):
            rows = jnp.where(taken[:, c, :, None], late_rows[:, c : c + 1], rows)
            hidden_grad = jnp.where(taken[:, c, :, None], late_hidden[:, c : c + 1], hidden_grad)
        paired = jnp.any(which[:, None, :, None] & which[None, :, None, :] & (twin > 0)[None, None], axis=(2, 3))
        new_rows = row_in
        for c in range(LATE):
            new_rows = new_rows + jnp.where(paired[:, c : c + 1], row_grad[c : c + 1], 0.0)
        return new_rows.astype(BF), rows, hidden_grad

    def take_in(now, new_rows, table):
        news = spread(new_rows, "section", section_count)
        sent = chosen(rounds_of.reshape(section_count, slots), now)
        table = table.reshape(section_count, slots, width)
        for c in range(LATE):
            table = jnp.where(sent[:, c, :, None], news[:, c : c + 1], table)
        return table.reshape(section_count * slots, width)

    which, row_in, scaled = send_rows(2, table)
    word = jnp.sum(jnp.where(lanes[None, :] == jnp.arange(slots + 1)[:, None], jnp.concatenate([own_round, own_plan[slots:]])[:, None], 0), axis=0)
    word = jnp.broadcast_to(word.astype(BF), (LATE, LANES))
    got = gather(jnp.concatenate([scaled, word], axis=1))
    words = got[:, 0, width:].astype(F32).astype(I32)
    all_rounds = words[:, :slots]
    rounds = jnp.max(words[:, slots])
    new_rows, rows, hidden_grad = finish(2, which, row_in, got[..., :width], all_rounds, rows, hidden_grad)

    def more(state):
        return state[0] < rounds

    def again(state):
        done, new_rows, table, rows, hidden_grad = state
        table = take_in(done, new_rows, table)
        now = done + 1
        which, row_in, scaled = send_rows(now, table)
        late_rows = gather(scaled)
        new_rows, rows, hidden_grad = finish(now, which, row_in, late_rows, all_rounds, rows, hidden_grad)
        return now, new_rows, table, rows, hidden_grad

    done, new_rows, table, rows, hidden_grad = lax.while_loop(
        more, again, (jnp.int32(2), new_rows, table, rows, hidden_grad)
    )
    table = take_in(done, new_rows, table)

    grad_down = jnp.einsum(
        "rh,rd->hd",
        activation.reshape(dp_count * slots, hid),
        rows.reshape(dp_count * slots, width),
        preferred_element_type=F32,
    ).astype(BF)
    ordered = hidden_grad.reshape(2, chips, micro_count, cap, hid)
    ordered = jnp.where(core == 0, ordered, ordered[::-1]).transpose(2, 1, 0, 3, 4)
    grad_up = jnp.einsum(
        "rh,rd->hd",
        ordered.reshape(micro_count * dp_count * cap, hid),
        x_rows[0].reshape(micro_count * dp_count * cap, width),
        preferred_element_type=F32,
    ).astype(BF)
    moved = jnp.dot(
        (source[:, : section_count * slots] == table_ids[None, :]).astype(BF), table, preferred_element_type=F32
    )
    in_grad = jnp.where(source[:, :1] >= 0, moved.astype(BF), flat_out).reshape(out_grad.shape)
    return (in_grad[None], grad_up[None], grad_down[None])


def solution(mesh):
    return jax.shard_map(
        per_device,
        mesh=mesh,
        in_specs=(
            P(None, "dp", None),
            P("section", None, None, None),
            P("section", None, None, "dp"),
            P("section", "dp", None),
            P("section", "dp", None),
            P("section", None, "dp"),
            P("section", None, "dp"),
            P("section", None, "dp"),
        ),
        out_specs=(
            P("section", None, "dp", None),
            P("section", "dp", None),
            P("section", "dp", None),
        ),
        check_vma=False,
    )
```

time: 254 us -> 250 us (0.984)
  blocking collectives: 71.3 us -> 32 us
  starting transfers between devices: 26.4 us -> 49.5 us
  local copies, waits for them, and re-layouts: 39.1 us -> 51.2 us
  waiting for transfers between devices: 66.1 us -> 55.4 us
  other arithmetic: 22.7 us -> 30.4 us
  Pallas kernels: 0 us -> 2.87 us
    all_to_all x3 -> x2, blocking collectives: 53.5 us -> 32 us  [spread(): lax.all_to_all(sent, axis, 0, 0, tiled=True, axis_index_groups=groups)]
    all_to_all x1 -> x0, blocking collectives: 17.9 us -> none  [one_round(): lax.all_to_all(pair_sum, 'dp', 0, 0, tiled=True, axis_index_groups=same_c...]
    ppermute x6 -> x9, starting transfers between devices: 0.42 us -> 13.5 us  [the longest x3 12.2 us: per_device(): lax.ppermute(info, 'section', [(i, i ^ hop) for i in range(section_count)])]
    broadcast_in_dim x0 -> x22, local copies, waits for them, and re-layouts: none -> 13 us  [the longest x14 7.87 us: take_in(): table = jnp.where(sent[:, c, :, None], news[:, c:c + 1], table)]
    all_to_all x3 -> x4, waiting for transfers between devices: 34.1 us -> 27.7 us  [spread(): lax.all_to_all(sent, axis, 0, 0, tiled=True, axis_index_groups=groups)]
    select_n x2 -> x6, other arithmetic: 0.08 us -> 6.11 us  [the longest x2 5.64 us: finish(): rows = jnp.where(taken[:, c, :, None], late_rows[:, c:c + 1], rows)]
    another operation x6 -> x7, other arithmetic: 6.83 us -> 0.94 us  [the longest x4 0.51 us: chosen(): rank = jnp.cumsum(mine.astype(I32), axis=-1) - 1]
    all_to_all x2 -> x3, starting transfers between devices: 10.6 us -> 16.2 us  [layer_pass(): lax.all_to_all(pair_sum, 'dp', 0, 0, tiled=True, axis_index_groups=same_c...]
  transfers between devices with their start and end apart: 11 -> 16, of which waited for: 8 -> 11; matrix products, arithmetic and copies ran while one was open for 5% -> 16% of each run, Pallas kernels for 0% -> 1%
where the time goes in v2:
time: 250 us; the launch traced here: 248 us
  waiting for transfers between devices  55.4 us (22%)
  local copies, waits for them, and re-layouts  51.2 us (20%)
  starting transfers between devices  49.5 us (20%)
  blocking collectives  32 us (13%)
  other arithmetic  30.4 us (12%)
  matrix products  23.7 us (9%)
  Pallas kernels  2.87 us (1%)
    all_to_all x2, blocking collectives, spread(): lax.all_to_all(sent, axis, 0, 0, tiled=True, axis_index_groups=groups)  32 us
    all_to_all x4, waiting for transfers between devices, spread(): lax.all_to_all(sent, axis, 0, 0, tiled=True, axis_index_groups=groups)  27.7 us
    all_to_all x3, waiting for transfers between devices, layer_pass(): lax.all_to_all(pair_sum, 'dp', 0, 0, tiled=True, axis_index_groups=same_c...  20.5 us
    all_to_all x4, starting transfers between devices, spread(): lax.all_to_all(sent, axis, 0, 0, tiled=True, axis_index_groups=groups)  19.8 us
    all_to_all x3, starting transfers between devices, layer_pass(): lax.all_to_all(pair_sum, 'dp', 0, 0, tiled=True, axis_index_groups=same_c...  16.2 us
    ppermute x3, starting transfers between devices, per_device(): lax.ppermute(info, 'section', [(i, i ^ hop) for i in range(section_count)])  12.2 us
    broadcast_in_dim x14, local copies, waits for them, and re-layouts, take_in(): table = jnp.where(sent[:, c, :, None], news[:, c:c + 1], table)  7.87 us
    unnamed x60, local copies, waits for them, and re-layouts  7.58 us
  transfers between devices with their start and end apart: 16, of which 11 were waited for; matrix products, arithmetic and copies ran while one was open for 16% of the time, Pallas kernels for 1%

profile of v2, /device:TPU:8, one launch (start us, length us, event | category | flops | bytes accessed | tf_op | source)
XLA Modules:
  0.0 247.8 jit_solution(14436796191964777526)
XLA Ops:
  3.1 1.8 multiply_convert_fusion.2
  5.2 19.8 %all_to_all.66 = bf16[16,4,6144]{2,1,0:T(4,128)(2,1)S(1)} all-to-all(bf16[16,4,6144]{2,1,0:T(4,128)(2,1)S(1)} %broadcast_in_dim.595), channel_id=1, replica_groups={{0,2,4,6,8,10,12,14,16,18,20,22,24,26,28,30},{1,3,5,7,9,11,13,15,17,19,..., dimensions={0} | all-to-all | bytes 1572864 | tf_op jit(solution)/shard_map/all_to_all | solution.py:107
  25.0 1.4 fusion.65
  26.5 2.5 collective-permute-done.5
  29.0 1.2 constant_dynamic-update-slice_fusion.2
  31.4 2.2 fusion.56
  33.6 1.6 copy-done.4
  35.3 1.2 convert_element_type.210
  36.7 1.9 collective-permute-start.2
  38.7 1.5 collective-permute-done.2
  40.3 3.4 %collective-permute-start.3 = (s32[2,8]{1,0:T(2,128)S(1)}, s32[2,8]{1,0:T(2,128)S(1)}, u32[]{:S(2)}, u32[]{:S(2)}) collective-permute-start(s32[2,8]{1,0:T(2,128)S(1)} %pad_add_fusion.2), channel_id=1, source_target_pairs={{0,64},{32,96},{64,0},{96,32},{128,192},{160,224},{192,128},{224,1... | collective-permute-start | bytes 200 | tf_op jit(solution)/shard_map/ppermute | solution.py:117
  43.6 1.5 collective-permute-done.3
  45.2 6.9 %collective-permute-start.4 = (s32[4,8]{1,0:T(4,128)S(1)}, s32[4,8]{1,0:T(4,128)S(1)}, u32[]{:S(2)}, u32[]{:S(2)}) collective-permute-start(s32[4,8]{1,0:T(4,128)S(1)} %pad_add_fusion.1), channel_id=1, source_target_pairs={{0,128},{32,160},{64,192},{96,224},{128,0},{160,32},{192,64},{224,... | collective-permute-start | bytes 392 | tf_op jit(solution)/shard_map/ppermute | solution.py:117
  52.1 1.6 collective-permute-done.4
  54.3 2.9 %shard_map.103 = (s32[32]{0:T(128)S(1)}, s32[5]{0:T(128)S(1)}, s32[128,128]{1,0:T(8,128)}) custom-call(s32[64]{0:T(128)} %reshape.787.refs_0_, s32[1]{0:T(128)} %bitcast.2.refs_1_), custom_call_target="tpu_custom_call" | custom-call | flops 100000 | bytes 70000 | tf_op jit(solution)/shard_map/pallas_call | solution.py:75
  57.8 1.4 slice-done
  59.2 1.6 squeeze.37
  60.8 2.9 %add_convert_fusion.2 = bf16[16,4,6144]{2,1,0:T(4,128)(2,1)} fusion(f32[16,4,6144]{2,1,0:T(4,128)} %squeeze.37, bf16[16,4,6144]{2,1,0:T(4,128)(2,1)} %collective-permute-done.6), kind=kLoop, calls=%fused_computation.65 | loop fusion | flops 1179648 | bytes 3145728 | tf_op jit(solution)/shard_map/convert_element_type | solution.py:148
  63.7 5.2 %all-to-all-start.4 = ((bf16[16,4,6144]{2,1,0:T(4,128)(2,1)}), bf16[16,4,6144]{2,1,0:T(4,128)(2,1)S(1)}, u32[]{:S(2)}, u32[]{:S(2)}) async-start(bf16[16,4,6144]{2,1,0:T(4,128)(2,1)} %add_convert_fusion.2), calls=%async_computation.4 | async-start | bytes 1572864 | tf_op jit(solution)/shard_map/all_to_all | solution.py:149
  70.1 9.3 %all-to-all-done.4 = bf16[16,4,6144]{2,1,0:T(4,128)(2,1)S(1)} async-done(((bf16[16,4,6144]{2,1,0:T(4,128)(2,1)}), bf16[16,4,6144]{2,1,0:T(4,128)(2,1)S(1)}, u32[]{:S(2)}, u32[]{:S(2)}) %all-to-all-start.4) | async-done | bytes 786464 | tf_op jit(solution)/shard_map/all_to_all | solution.py:149
  81.0 7.0 %all-to-all-start.5 = ((bf16[8,4,6144]{2,1,0:T(4,128)(2,1)}), bf16[8,4,6144]{2,1,0:T(4,128)(2,1)S(1)}, u32[]{:S(2)}, u32[]{:S(2)}) async-start(bf16[8,4,6144]{2,1,0:T(4,128)(2,1)} %broadcast_in_dim.596), calls=%async_computation.5 | async-start | bytes 786432 | tf_op jit(solution)/shard_map/all_to_all | solution.py:107
  88.2 11.6 %all-to-all-done.5 = bf16[8,4,6144]{2,1,0:T(4,128)(2,1)S(1)} async-done(((bf16[8,4,6144]{2,1,0:T(4,128)(2,1)}), bf16[8,4,6144]{2,1,0:T(4,128)(2,1)S(1)}, u32[]{:S(2)}, u32[]{:S(2)}) %all-to-all-start.5) | async-done | bytes 393248 | tf_op jit(solution)/shard_map/all_to_all | solution.py:107
  101.2 12.2 %all_to_all.67 = bf16[16,2,6272]{2,1,0:T(2,128)(2,1)S(1)} all-to-all(bf16[16,2,6272]{2,1,0:T(2,128)(2,1)S(1)} %broadcast_in_dim.604), channel_id=1, replica_groups={{0,2,4,6,8,10,12,14,16,18,20,22,24,26,28,30},{1,3,5,7,9,11,13,15,17,19,..., dimensions={0} | all-to-all | bytes 802816 | tf_op jit(solution)/shard_map/all_to_all | solution.py:107
  116.0 0.9 slice_bitcast_fusion.7
  117.9 1.0 select_reduce_fusion.2
  118.9 2.4 fusion.36
  122.0 2.2 fusion.54
  124.2 1.1 copy-done.8
  125.4 1.0 convert_element_type.223
  126.9 2.0 select_select_fusion.3
  129.0 0.9 slice.282
  129.9 2.5 squeeze.38
  132.4 2.4 add_convert_fusion.3
  134.8 5.7 %all-to-all-start.7 = ((bf16[16,2,6144]{2,1,0:T(2,128)(2,1)}), bf16[16,2,6144]{2,1,0:T(2,128)(2,1)}, u32[]{:S(2)}, u32[]{:S(2)}) async-start(bf16[16,2,6144]{2,1,0:T(2,128)(2,1)} %add_convert_fusion.3), calls=%async_computation.7 | async-start | bytes 786432 | tf_op jit(solution)/shard_map/all_to_all | solution.py:149
  140.4 1.3 slice_bitcast_fusion.9
  142.5 2.4 copy.174
  146.4 3.0 %all-to-all-done.7 = bf16[16,2,6144]{2,1,0:T(2,128)(2,1)} async-done(((bf16[16,2,6144]{2,1,0:T(2,128)(2,1)}), bf16[16,2,6144]{2,1,0:T(2,128)(2,1)}, u32[]{:S(2)}, u32[]{:S(2)}) %all-to-all-start.7) | async-done | bytes 393248 | tf_op jit(solution)/shard_map/all_to_all | solution.py:149
  149.3 1.3 convert_reduce_fusion.2
  151.6 67.1 %while.21 = (s32[]{:T(128)}, bf16[2,6144]{1,0:T(2,128)(2,1)S(1)}, bf16[32,6144]{1,0:T(8,128)(2,1)S(1)}, bf16[32,4,6144]{2,1,0:T(4,128)(2,1)}, bf16[32,4,168]{2,1...) while((s32[]{:T(128)}, bf16[2,6144]{1,0:T(2,128)(2,1)S(1)}, ...), condition=%wide.region_20.21_spmd.clone.clone, body=%wide.region_11.20_spmd.clone.clone.sunk | while | flops 268303328 | bytes 42804900 | solution.py:220
  153.1 3.4 %all-to-all-start = ((bf16[8,2,6144]{2,1,0:T(2,128)(2,1)}), bf16[8,2,6144]{2,1,0:T(2,128)(2,1)S(1)}, u32[]{:S(2)}, u32[]{:S(2)}) async-start(bf16[8,2,6144]{2,1,0:T(2,128)(2,1)} %broadcast_in_dim.820), calls=%async_computation | async-start | bytes 393216 | tf_op jit(solution)/shard_map/while/body/all_to_all | solution.py:107
  160.8 5.8 %all-to-all-done = bf16[8,2,6144]{2,1,0:T(2,128)(2,1)S(1)} async-done(((bf16[8,2,6144]{2,1,0:T(2,128)(2,1)}), bf16[8,2,6144]{2,1,0:T(2,128)(2,1)S(1)}, u32[]{:S(2)}, u32[]{:S(2)}) %all-to-all-start) | async-done | bytes 196640 | tf_op jit(solution)/shard_map/while/body/all_to_all | solution.py:107
  168.8 0.9 broadcast_in_dim.827
  169.7 5.2 %all-to-all-start.1 = ((bf16[16,2,6144]{2,1,0:T(2,128)(2,1)}), bf16[16,2,6144]{2,1,0:T(2,128)(2,1)S(1)}, u32[]{:S(2)}, u32[]{:S(2)}) async-start(bf16[16,2,6144]{2,1,0:T(2,128)(2,1)} %broadcast_in_dim.827), calls=%async_computation.1 | async-start | bytes 786432 | tf_op jit(solution)/shard_map/while/body/all_to_all | solution.py:107
  175.5 6.9 %all-to-all-done.1 = bf16[16,2,6144]{2,1,0:T(2,128)(2,1)S(1)} async-done(((bf16[16,2,6144]{2,1,0:T(2,128)(2,1)}), bf16[16,2,6144]{2,1,0:T(2,128)(2,1)S(1)}, u32[]{:S(2)}, u32[]{:S(2)}) %all-to-all-start.1) | async-done | bytes 393248 | tf_op jit(solution)/shard_map/while/body/all_to_all | solution.py:107
  184.1 1.0 and_reduce_fusion.7
  185.8 1.0 select_reduce_fusion.8
  186.9 0.9 slice_bitcast_fusion.16
  189.9 2.2 fusion.121
  192.9 2.0 convert_element_type.321
  195.4 3.6 %select_select_fusion.9 = bf16[32,4,6144]{2,1,0:T(4,128)(2,1)} fusion(bf16[32,4,6144]{2,1,0:T(4,128)(2,1)} %get-tuple-element.788, pred[32,4]{1,0:T(8,128)(4,1)S(1)} %copy.210, pred[32,4]{1,0:T(8,128)(4,1)S(1)} %copy.211, bf16[32,6144]{1,0:T(8,128)(2,1)} %get-tuple-element.761, bf16[32,6144]{1,0:T(8,128)(2,1)} %get-tuple-element.762), kind=kLoop, calls=%fused_computation.6.clone.1 | loop fusion | flops 1572864 | bytes 3932416 | tf_op jit(solution)/shard_map/while/body/jit(_where)/select_n | solution.py:183
  199.0 0.9 slice.365
  200.0 1.6 squeeze.42
  201.6 2.2 add_convert_fusion.8
  203.8 5.3 %all-to-all-start.2 = ((bf16[16,2,6144]{2,1,0:T(2,128)(2,1)}), bf16[16,2,6144]{2,1,0:T(2,128)(2,1)S(1)}, u32[]{:S(2)}, u32[]{:S(2)}) async-start(bf16[16,2,6144]{2,1,0:T(2,128)(2,1)} %add_convert_fusion.8), calls=%async_computation.2 | async-start | bytes 786432 | tf_op jit(solution)/shard_map/while/body/all_to_all | solution.py:149
  209.3 8.2 %all-to-all-done.2 = bf16[16,2,6144]{2,1,0:T(2,128)(2,1)S(1)} async-done(((bf16[16,2,6144]{2,1,0:T(2,128)(2,1)}), bf16[16,2,6144]{2,1,0:T(2,128)(2,1)S(1)}, u32[]{:S(2)}, u32[]{:S(2)}) %all-to-all-start.2) | async-done | bytes 393248 | tf_op jit(solution)/shard_map/while/body/all_to_all | solution.py:149
  222.1 4.2 %all-to-all-start.8 = ((bf16[8,2,6144]{2,1,0:T(2,128)(2,1)}), bf16[8,2,6144]{2,1,0:T(2,128)(2,1)}, u32[]{:S(2)}, u32[]{:S(2)}) async-start(bf16[8,2,6144]{2,1,0:T(2,128)(2,1)} %broadcast_in_dim.631), calls=%async_computation.8 | async-start | bytes 393216 | tf_op jit(solution)/shard_map/all_to_all | solution.py:107
  226.4 3.0 %fusion.19 = bf16[1,168,6144]{2,1,0:T(8,128)(2,1)} fusion(bf16[128,168]{1,0:T(8,128)(2,1)} %reshape.795, bf16[128,6144]{1,0:T(8,128)(2,1)S(1)} %bitcast.152), kind=kOutput, calls=%fused_computation.53 | convolution fusion | flops 265273344 | bytes 3680256 | tf_op jit(solution)/shard_map/rh,rd->hd/dot_general | solution.py:233
  229.5 3.5 %fusion.20 = bf16[1,168,6144]{2,1,0:T(8,128)(2,1)} fusion(bf16[32,4,6144]{2,1,0:T(4,128)(2,1)S(1)} %copy-done.3, f32[32,4,168]{2,0,1:T(8,128)} %bitcast.161), kind=kOutput, calls=%fused_computation.54 | convolution fusion | flops 265380864 | bytes 3723264 | tf_op jit(solution)/shard_map/rh,rd->hd/dot_general | solution.py:225
  233.1 3.4 %all-to-all-done.8 = bf16[8,2,6144]{2,1,0:T(2,128)(2,1)} async-done(((bf16[8,2,6144]{2,1,0:T(2,128)(2,1)}), bf16[8,2,6144]{2,1,0:T(2,128)(2,1)}, u32[]{:S(2)}, u32[]{:S(2)}) %all-to-all-start.8) | async-done | bytes 196640 | tf_op jit(solution)/shard_map/all_to_all | solution.py:107
  236.4 1.4 fusion.67
  239.5 1.8 broadcast_in_dim.639
  241.3 1.7 broadcast_in_dim.633
  243.0 1.8 broadcast_in_dim.634
  244.9 2.9 %fusion.21 = bf16[128,6144]{1,0:T(8,128)(2,1)} fusion(bf16[128,6144]{1,0:T(8,128)(2,1)S(1)} %bitcast.156, pred[128]{0:T(512)(128)(4,1)S(1)} %copy-done.37, bf16[32,6144]{1,0:T(8,128)(2,1)} %broadcast_in_dim.634, bf16[32,6144]{1,0:T(8,128)(2,1)} %broadcast_in_dim.639, bf16[32,6144]{1,0:T(8,128)(2,1)S(1)} %get-tuple-element.289, ...), kind=kOutput, calls=%fused_computation.55 | convolution fusion | flops 52301824 | bytes 4391104 | tf_op jit(solution)/shard_map/dot_general | solution.py:239
  (218 shorter events, 37.3 us)
Async XLA Ops:
  0.6 225.7 %copy-start = (bf16[1,2,64,6144]{3,2,1,0:T(8,128)(2,1)S(1)}, bf16[1,2,64,6144]{3,2,1,0:T(8,128)(2,1)}, u32[]{:S(2)}) copy-start(bf16[1,2,64,6144]{3,2,1,0:T(8,128)(2,1)} %param.11) | copy-start | bytes 4718596
  1.5 37.1 %copy-start.20 = (s32[4]{0:T(128)}, s32[4]{0:T(128)S(1)}, u32[]{:S(2)}) copy-start(s32[4]{0:T(128)S(1)} %reshape_squeeze.12) | copy-start | bytes 52
  3.1 35.6 %copy-start.31 = (pred[4]{0:T(512)(128)(4,1)}, pred[4]{0:T(512)(128)(4,1)S(1)}, u32[]{:S(2)}) copy-start(pred[4]{0:T(512)(128)(4,1)S(1)} %lt.60) | copy-start | bytes 16
  3.1 84.9 %copy-start.30 = (f32[4]{0:T(128)}, f32[4]{0:T(128)S(1)}, u32[]{:S(2)}) copy-start(f32[4]{0:T(128)S(1)} %broadcast_select_fusion) | copy-start | bytes 52
  25.0 1.4 copy-start.24
  26.3 2.6 %collective-permute-start.5 = (bf16[16,4,6144]{2,0,1:T(8,128)(2,1)}, bf16[16,4,6144]{2,0,1:T(8,128)(2,1)}, u32[]{:S(2)}, u32[]{:S(2)}) collective-permute-start(bf16[16,4,6144]{2,0,1:T(8,128)(2,1)} %get-tuple-element.577), channel_id=1, source_target_pairs={{0,1},{1,0},{2,3},{3,2},{4,5},{5,4},{6,7},{7,6},{8,9},{9,8},{10,11... | collective-permute-start | bytes 2359304 | tf_op jit(solution)/shard_map/ppermute | solution.py:138
  26.3 3.8 %copy-start.1 = (bf16[1,168,6144]{2,1,0:T(8,128)(2,1)S(1)}, bf16[1,168,6144]{2,1,0:T(8,128)(2,1)}, u32[]{:S(2)}) copy-start(bf16[1,168,6144]{2,1,0:T(8,128)(2,1)} %param.14) | copy-start | bytes 6193156
  26.5 4.6 %copy-start.14 = (f32[2,16,2,2,168]{4,1,0,3,2:T(8,128)}, f32[2,16,2,2,168]{4,1,0,3,2:T(8,128)S(1)}, u32[]{:S(2)}) copy-start(f32[2,16,2,2,168]{4,1,0,3,2:T(8,128)S(1)} %copy.167) | copy-start | bytes 258052
  30.2 1.1 copy-start.10
  31.3 2.3 copy-start.18
  33.6 1.7 copy-start.4
  36.5 24.3 %collective-permute-start.6 = (bf16[16,4,6144]{2,1,0:T(4,128)(2,1)}, bf16[16,4,6144]{2,1,0:T(4,128)(2,1)}, u32[]{:S(2)}, u32[]{:S(2)}) collective-permute-start(bf16[16,4,6144]{2,1,0:T(4,128)(2,1)} %convert_element_type.210), channel_id=1, source_target_pairs={{0,1},{1,0},{2,3},{3,2},{4,5},{5,4},{6,7},{7,6},{8,9},{9,8},{10,11... | collective-permute-start | bytes 2359304 | tf_op jit(solution)/shard_map/ppermute | solution.py:147
  36.7 3.6 %collective-permute-start.2 = (s32[1,8]{1,0:T(1,128)S(1)}, s32[1,8]{1,0:T(1,128)S(1)}, u32[]{:S(2)}, u32[]{:S(2)}) collective-permute-start(s32[1,8]{1,0:T(1,128)S(1)} %add_bitcast_fusion.1), channel_id=1, source_target_pairs={{0,32},{32,0},{64,96},{96,64},{128,160},{160,128},{192,224},{224,1... | collective-permute-start | bytes 104 | tf_op jit(solution)/shard_map/ppermute | solution.py:117
  38.7 19.1 %copy-start.22 = (s32[4]{0:T(128)}, s32[4]{0:T(128)S(1)}, u32[]{:S(2)}) copy-start(s32[4]{0:T(128)S(1)} %and_select_fusion) | copy-start | bytes 52
  40.3 4.9 %collective-permute-start.3 = (s32[2,8]{1,0:T(2,128)S(1)}, s32[2,8]{1,0:T(2,128)S(1)}, u32[]{:S(2)}, u32[]{:S(2)}) collective-permute-start(s32[2,8]{1,0:T(2,128)S(1)} %pad_add_fusion.2), channel_id=1, source_target_pairs={{0,64},{32,96},{64,0},{96,32},{128,192},{160,224},{192,128},{224,1... | collective-permute-start | bytes 200 | tf_op jit(solution)/shard_map/ppermute | solution.py:117
  45.2 8.5 %collective-permute-start.4 = (s32[4,8]{1,0:T(4,128)S(1)}, s32[4,8]{1,0:T(4,128)S(1)}, u32[]{:S(2)}, u32[]{:S(2)}) collective-permute-start(s32[4,8]{1,0:T(4,128)S(1)} %pad_add_fusion.1), channel_id=1, source_target_pairs={{0,128},{32,160},{64,192},{96,224},{128,0},{160,32},{192,64},{224,... | collective-permute-start | bytes 392 | tf_op jit(solution)/shard_map/ppermute | solution.py:117
  57.2 11.8 %copy-start.38 = (s32[32]{0:T(128)}, s32[32]{0:T(128)S(1)}, u32[]{:S(2)}) copy-start(s32[32]{0:T(128)S(1)} %get-tuple-element.773) | copy-start | bytes 388
  57.2 31.0 %copy-start.34 = (s32[5]{0:T(128)}, s32[5]{0:T(128)S(1)}, u32[]{:S(2)}) copy-start(s32[5]{0:T(128)S(1)} %get-tuple-element.286) | copy-start | bytes 64
  57.8 1.4 slice-start
  63.7 15.7 %all-to-all-start.4 = ((bf16[16,4,6144]{2,1,0:T(4,128)(2,1)}), bf16[16,4,6144]{2,1,0:T(4,128)(2,1)S(1)}, u32[]{:S(2)}, u32[]{:S(2)}) async-start(bf16[16,4,6144]{2,1,0:T(4,128)(2,1)} %add_convert_fusion.2), calls=%async_computation.4 | async-start | bytes 1572864 | tf_op jit(solution)/shard_map/all_to_all | solution.py:149
  69.0 19.2 %copy-start.33 = (s32[4]{0:T(128)}, s32[4]{0:T(128)S(1)}, u32[]{:S(2)}) copy-start(s32[4]{0:T(128)S(1)} %get-tuple-element.771) | copy-start | bytes 52
  80.1 21.0 %copy-start.28 = (bf16[4,6144]{1,0:T(4,128)(2,1)}, bf16[4,6144]{1,0:T(4,128)(2,1)S(1)}, u32[]{:S(2)}) copy-start(bf16[4,6144]{1,0:T(4,128)(2,1)S(1)} %get-tuple-element.774) | copy-start | bytes 147460
  81.0 18.9 %all-to-all-start.5 = ((bf16[8,4,6144]{2,1,0:T(4,128)(2,1)}), bf16[8,4,6144]{2,1,0:T(4,128)(2,1)S(1)}, u32[]{:S(2)}, u32[]{:S(2)}) async-start(bf16[8,4,6144]{2,1,0:T(4,128)(2,1)} %broadcast_in_dim.596), calls=%async_computation.5 | async-start | bytes 786432 | tf_op jit(solution)/shard_map/all_to_all | solution.py:107
  100.0 13.6 %copy-start.15 = (f32[2,16,2,2,168]{4,1,0,3,2:T(8,128)S(1)}, f32[2,16,2,2,168]{4,1,0,3,2:T(8,128)}, u32[]{:S(2)}) copy-start(f32[2,16,2,2,168]{4,1,0,3,2:T(8,128)} %copy-done.14) | copy-start | bytes 258052
  100.1 15.2 %copy-start.17 = (s32[128,128]{1,0:T(8,128)S(1)}, s32[128,128]{1,0:T(8,128)}, u32[]{:S(2)}) copy-start(s32[128,128]{1,0:T(8,128)} %get-tuple-element.284) | copy-start | bytes 196612
  113.5 2.5 %collective-permute-start.7 = (bf16[16,2,6272]{2,0,1:T(8,128)(2,1)S(1)}, bf16[16,2,6272]{2,0,1:T(8,128)(2,1)S(1)}, u32[]{:S(2)}, u32[]{:S(2)}) collective-permute-start(bf16[16,2,6272]{2,0,1:T(8,128)(2,1)S(1)} %get-tuple-element.579), channel_id=1, source_target_pairs={{0,1},{1,0},{2,3},{3,2},{4,5},{5,4},{6,7},{7,6},{8,9},{9,8},{10,11... | collective-permute-start | bytes 1204232 | tf_op jit(solution)/shard_map/ppermute | solution.py:138
  121.3 0.6 copy-start.16
  124.2 1.1 copy-start.8
  126.4 6.0 %collective-permute-start.8 = (bf16[16,2,6144]{2,1,0:T(2,128)(2,1)}, bf16[16,2,6144]{2,1,0:T(2,128)(2,1)}, u32[]{:S(2)}, u32[]{:S(2)}) collective-permute-start(bf16[16,2,6144]{2,1,0:T(2,128)(2,1)} %convert_element_type.223), channel_id=1, source_target_pairs={{0,1},{1,0},{2,3},{3,2},{4,5},{5,4},{6,7},{7,6},{8,9},{9,8},{10,11... | collective-permute-start | bytes 1179656 | tf_op jit(solution)/shard_map/ppermute | solution.py:147
  126.9 2.1 copy-start.9
  134.8 14.6 %all-to-all-start.7 = ((bf16[16,2,6144]{2,1,0:T(2,128)(2,1)}), bf16[16,2,6144]{2,1,0:T(2,128)(2,1)}, u32[]{:S(2)}, u32[]{:S(2)}) async-start(bf16[16,2,6144]{2,1,0:T(2,128)(2,1)} %add_convert_fusion.3), calls=%async_computation.7 | async-start | bytes 786432 | tf_op jit(solution)/shard_map/all_to_all | solution.py:149
  142.4 2.4 copy-start.19
  142.4 2.4 copy-start.25
  142.4 2.4 copy-start.26
  142.4 2.4 copy-start.35
  142.5 2.4 copy-start.36
  153.1 13.5 %all-to-all-start = ((bf16[8,2,6144]{2,1,0:T(2,128)(2,1)}), bf16[8,2,6144]{2,1,0:T(2,128)(2,1)S(1)}, u32[]{:S(2)}, u32[]{:S(2)}) async-start(bf16[8,2,6144]{2,1,0:T(2,128)(2,1)} %broadcast_in_dim.820), calls=%async_computation | async-start | bytes 393216 | tf_op jit(solution)/shard_map/while/body/all_to_all | solution.py:107
  167.2 0.8 copy-start.29
  167.4 7.5 %copy-start.21 = (s32[4]{0:T(128)S(1)}, s32[4]{0:T(128)}, u32[]{:S(2)}) copy-start(s32[4]{0:T(128)} %get-tuple-element.821) | copy-start | bytes 52 | tf_op jit(solution)/shard_map/while
  167.4 7.5 %copy-start.23 = (s32[4]{0:T(128)S(1)}, s32[4]{0:T(128)}, u32[]{:S(2)}) copy-start(s32[4]{0:T(128)} %get-tuple-element.820) | copy-start | bytes 52 | tf_op jit(solution)/shard_map/while
  167.5 7.5 %copy-start.32 = (pred[4]{0:T(512)(128)(4,1)S(1)}, pred[4]{0:T(512)(128)(4,1)}, u32[]{:S(2)}) copy-start(pred[4]{0:T(512)(128)(4,1)} %get-tuple-element.822) | copy-start | bytes 16 | tf_op jit(solution)/shard_map/while
  169.7 12.7 %all-to-all-start.1 = ((bf16[16,2,6144]{2,1,0:T(2,128)(2,1)}), bf16[16,2,6144]{2,1,0:T(2,128)(2,1)S(1)}, u32[]{:S(2)}, u32[]{:S(2)}) async-start(bf16[16,2,6144]{2,1,0:T(2,128)(2,1)} %broadcast_in_dim.827), calls=%async_computation.1 | async-start | bytes 786432 | tf_op jit(solution)/shard_map/while/body/all_to_all | solution.py:107
  182.6 4.3 %collective-permute-start = (bf16[16,2,6144]{2,0,1:T(8,128)(2,1)S(1)}, bf16[16,2,6144]{2,0,1:T(8,128)(2,1)S(1)}, u32[]{:S(2)}, u32[]{:S(2)}) collective-permute-start(bf16[16,2,6144]{2,0,1:T(8,128)(2,1)S(1)} %get-tuple-element.756), channel_id=1, source_target_pairs={{0,1},{1,0},{2,3},{3,2},{4,5},{5,4},{6,7},{7,6},{8,9},{9,8},{10,11... | collective-permute-start | bytes 1179656 | tf_op jit(solution)/shard_map/while/body/ppermute | solution.py:138
  184.0 3.8 %copy-start.2 = (bf16[168,6144]{1,0:T(8,128)(2,1)S(1)}, bf16[168,6144]{1,0:T(8,128)(2,1)}, u32[]{:S(2)}) copy-start(bf16[168,6144]{1,0:T(8,128)(2,1)} %get-tuple-element.816) | copy-start | bytes 6193156 | tf_op jit(solution)/shard_map/while
  188.6 0.6 copy-start.5
  194.9 6.7 %collective-permute-start.1 = (bf16[16,2,6144]{2,1,0:T(2,128)(2,1)}, bf16[16,2,6144]{2,1,0:T(2,128)(2,1)}, u32[]{:S(2)}, u32[]{:S(2)}) collective-permute-start(bf16[16,2,6144]{2,1,0:T(2,128)(2,1)} %convert_element_type.321), channel_id=1, source_target_pairs={{0,1},{1,0},{2,3},{3,2},{4,5},{5,4},{6,7},{7,6},{8,9},{9,8},{10,11... | collective-permute-start | bytes 1179656 | tf_op jit(solution)/shard_map/while/body/ppermute | solution.py:147
  201.6 7.5 %copy-start.6 = (bf16[32,2,168]{2,0,1:T(8,128)(2,1)S(1)}, bf16[32,2,168]{2,0,1:T(8,128)(2,1)}, u32[]{:S(2)}) copy-start(bf16[32,2,168]{2,0,1:T(8,128)(2,1)} %copy-done.5) | copy-start | bytes 64516 | tf_op jit(solution)/shard_map/while
  201.6 7.6 %copy-start.11 = (bf16[32,4,168]{2,1,0:T(4,128)(2,1)S(1)}, bf16[32,4,168]{2,1,0:T(4,128)(2,1)}, u32[]{:S(2)}) copy-start(bf16[32,4,168]{2,1,0:T(4,128)(2,1)} %get-tuple-element.789) | copy-start | bytes 129028 | tf_op jit(solution)/shard_map/while
  201.6 16.4 %copy-start.13 = (f32[2,6144]{1,0:T(2,128)S(1)}, f32[2,6144]{1,0:T(2,128)}, u32[]{:S(2)}) copy-start(f32[2,6144]{1,0:T(2,128)} %get-tuple-element.749) | copy-start | bytes 147460 | tf_op jit(solution)/shard_map/while
  201.6 16.4 %copy-start.27 = (pred[2]{0:T(512)(128)(4,1)S(1)}, pred[2]{0:T(512)(128)(4,1)}, u32[]{:S(2)}) copy-start(pred[2]{0:T(512)(128)(4,1)} %get-tuple-element.750) | copy-start | bytes 10 | tf_op jit(solution)/shard_map/while
  203.8 13.8 %all-to-all-start.2 = ((bf16[16,2,6144]{2,1,0:T(2,128)(2,1)}), bf16[16,2,6144]{2,1,0:T(2,128)(2,1)S(1)}, u32[]{:S(2)}, u32[]{:S(2)}) async-start(bf16[16,2,6144]{2,1,0:T(2,128)(2,1)} %add_convert_fusion.8), calls=%async_computation.2 | async-start | bytes 786432 | tf_op jit(solution)/shard_map/while/body/all_to_all | solution.py:149
  209.3 8.8 %copy-start.12 = (bf16[32,4,168]{2,1,0:T(4,128)(2,1)}, bf16[32,4,168]{2,1,0:T(4,128)(2,1)S(1)}, u32[]{:S(2)}) copy-start(bf16[32,4,168]{2,1,0:T(4,128)(2,1)S(1)} %select_select_fusion.10) | copy-start | bytes 129028 | tf_op jit(solution)/shard_map/while
  222.1 14.4 %all-to-all-start.8 = ((bf16[8,2,6144]{2,1,0:T(2,128)(2,1)}), bf16[8,2,6144]{2,1,0:T(2,128)(2,1)}, u32[]{:S(2)}, u32[]{:S(2)}) async-start(bf16[8,2,6144]{2,1,0:T(2,128)(2,1)} %broadcast_in_dim.631), calls=%async_computation.8 | async-start | bytes 393216 | tf_op jit(solution)/shard_map/all_to_all | solution.py:107
  226.4 3.2 %copy-start.3 = (bf16[32,4,6144]{2,1,0:T(4,128)(2,1)S(1)}, bf16[32,4,6144]{2,1,0:T(4,128)(2,1)}, u32[]{:S(2)}) copy-start(bf16[32,4,6144]{2,1,0:T(4,128)(2,1)} %get-tuple-element.291) | copy-start | bytes 4718596
  237.8 7.0 %copy-start.7 = (bf16[2,64,6144]{2,1,0:T(8,128)(2,1)S(1)}, bf16[2,64,6144]{2,1,0:T(8,128)(2,1)}, u32[]{:S(2)}) copy-start(bf16[2,64,6144]{2,1,0:T(8,128)(2,1)} %param.10) | copy-start | bytes 4718596
  237.8 7.0 %copy-start.37 = (pred[128]{0:T(512)(128)(4,1)S(1)}, pred[128]{0:T(512)(128)(4,1)}, u32[]{:S(2)}) copy-start(pred[128]{0:T(512)(128)(4,1)} %fusion.47) | copy-start | bytes 388

commit v3 on v0

v3 whole, which is shorter than its diff:
```python
import functools

import jax
import jax.numpy as jnp
from jax import lax
from jax.experimental import pallas as pl
from jax.experimental.pallas import tpu as pltpu
from jax.sharding import PartitionSpec as P

BF = jnp.bfloat16
F32 = jnp.float32
I32 = jnp.int32
LANES = 128
LATE = 2
NT = (((1,), (1,)), ((), ()))
TN = (((0,), (0,)), ((), ()))
SMEM = pl.BlockSpec(memory_space=pltpu.SMEM)
VMEM = pl.BlockSpec(memory_space=pltpu.VMEM)


def call(kernel, ins, outs, out_specs, scratch=(), flops=1000000, size=1000000):
    return pl.pallas_call(
        kernel,
        in_specs=ins,
        out_specs=out_specs,
        out_shape=outs,
        scratch_shapes=list(scratch),
        compiler_params=pltpu.CompilerParams(vmem_limit_bytes=40 * 1024 * 1024),
        cost_estimate=pl.CostEstimate(flops=flops, bytes_accessed=size, transcendentals=0),
    )


def chunks(width):
    step = next(s for s in (1024, 768, 512, 384, 256, 128) if width % s == 0)
    return [pl.ds(at, step) for at in range(0, width, step)]


def dot(a, b, dims=None):
    if dims is None:
        return jnp.dot(a, b, preferred_element_type=F32)
    return lax.dot_general(a, b, dims, preferred_element_type=F32)


def iota(shape, axis):
    return lax.broadcasted_iota(I32, shape, axis)


def one_hot(flag):
    return jnp.where(flag, 1.0, 0.0).astype(BF)


def column(values, shape):
    rows = iota(shape, 0)
    out = jnp.full(shape, values[0])
    for i in range(1, len(values)):
        out = jnp.where(rows == i, values[i], out)
    return out


def first_kernel(token_ref, count_ref, gate_ref, grad_ref, sent_ref, first_ref, info_ref):
    micros, tok_rows, width = grad_ref.shape
    cap = token_ref.shape[2]
    slots = micros * cap
    tokens = [token_ref[0, i // cap, i % cap] for i in range(slots)]
    live = [jnp.where(i % cap < count_ref[0, i // cap, 0], 1, 0) for i in range(slots)]
    weights = [jnp.where(live[i] > 0, gate_ref[0, i // cap, i % cap], 0.0) for i in range(slots)]
    lane = iota((1, LANES), 1)
    info = jnp.zeros((1, LANES), I32)
    for i in range(slots):
        info = jnp.where(lane == i, tokens[i], info)
        info = jnp.where(lane == slots + i, live[i], info)
    info_ref[...] = info
    wanted = column([tokens[i] + (i // cap) * tok_rows for i in range(slots)], (8, micros * tok_rows))
    pick = one_hot(wanted == iota(wanted.shape, 1))
    weight = column(weights, (8, LANES))[:, :1]
    for part in chunks(width):
        rows = dot(pick, grad_ref[:, :, part].reshape(micros * tok_rows, part.size))
        first_ref[:, part] = rows[:slots].astype(BF)
        scaled = (weight * rows)[:slots].astype(BF)
        for chip in range(sent_ref.shape[0]):
            sent_ref[chip, :, part] = scaled


def plan_kernel(sections, cap, tok_rows, info_ref, place_ref, round_ref, own_ref, source_ref, ready_ref, last_ref):
    slots = 2 * cap
    place = place_ref[0]
    rows = 2 * tok_rows

    def clear(t, carry):
        ready_ref[t] = 1
        last_ref[t] = -1
        return carry

    lax.fori_loop(0, rows, clear, 0)
    row_ids = iota(source_ref.shape, 0)
    source_ref[...] = jnp.full(source_ref.shape, -1, I32)

    def layer_step(step, most):
        layer = sections - 1 - step
        at = layer ^ place
        token = [info_ref[at, i] + (i // cap) * tok_rows for i in range(slots)]
        live = [info_ref[at, slots + i] for i in range(slots)]
        own = layer == place
        for i in range(slots):
            prior = last_ref[token[i]]
            own_ref[i] = jnp.where(own, prior, own_ref[i])
        given = []
        for i in range(slots):
            twin_before = jnp.int32(0)
            twin_after = jnp.int32(0)
            for k in range((i // cap) * cap, (i // cap) * cap + cap):
                same = jnp.where((token[k] == token[i]) & (live[k] > 0), 1, 0)
                if k < i:
                    twin_before = jnp.maximum(twin_before, same * given[k])
                elif k > i:
                    twin_after = twin_after + same
            when = ready_ref[token[i]]
            size = 1 + twin_after
            for _ in range(slots - 1):
                taken = jnp.int32(0)
                for k in range(i):
                    taken = taken + jnp.where(given[k] == when, 1, 0)
                when = jnp.where((when >= 2) & (taken + size > LATE), when + 1, when)
            when = jnp.where(twin_before > 0, twin_before, when)
            when = jnp.where(live[i] > 0, when, 0)
            given.append(when)
        for i in range(slots):
            round_ref[layer * slots + i] = given[i]
            most = jnp.maximum(most, given[i])
            ready_ref[token[i]] = jnp.where(live[i] > 0, given[i] + 1, ready_ref[token[i]])
            last_ref[token[i]] = jnp.where(live[i] > 0, layer * slots + i, last_ref[token[i]])
            hit = (row_ids == token[i]) & ((live[i] > 0) & (layer >= place))
            source_ref[...] = jnp.where(hit, layer * slots + i, source_ref[...])
        return most

    for i in range(slots):
        own_ref[i] = -1
    own_ref[slots] = lax.fori_loop(0, sections, layer_step, jnp.int32(1))


def row_map(round_ref, sections, slots, now):
    found = []
    for layer in range(sections):
        rank = jnp.int32(0)
        for i in range(slots):
            hit = round_ref[layer * slots + i] == now
            found.append(jnp.where(hit, sections * slots + layer * LATE + rank, layer * slots + i))
            rank = rank + jnp.where(hit, 1, 0)
    return found


def own_picks(round_ref, place, slots, now):
    picks = [jnp.int32(-1)] * LATE
    rank = jnp.int32(0)
    for i in range(slots):
        hit = round_ref[place * slots + i] == now
        for c in range(LATE):
            picks[c] = jnp.where(hit & (rank == c), i, picks[c])
        rank = rank + jnp.where(hit, 1, 0)
    return picks


def send_kernel(fresh, note, cap, now_ref, place_ref, round_ref, own_ref, gate_ref, first_ref, table_ref, *refs):
    refs = list(refs)
    news_ref = refs.pop(0) if fresh else None
    sent_ref, row_in_ref = refs.pop(0), refs.pop(0)
    merged_ref = refs.pop(0) if fresh else None
    map_ref = refs.pop(0)
    sections, slots, width = table_ref.shape
    known = sections * slots
    now, place = now_ref[0], place_ref[0]
    if fresh:
        where_is = row_map(round_ref, sections, slots, now - 1)
    else:
        where_is = [jnp.int32(k) for k in range(known)]
    for k in range(known):
        map_ref[k] = where_is[k]
    wanted, from_first, weights = [], [], []
    for slot in own_picks(round_ref, place, slots, now):
        at = jnp.maximum(slot, 0)
        source = own_ref[at]
        wanted.append(jnp.where((slot >= 0) & (source >= 0), map_ref[jnp.maximum(source, 0)], -1))
        from_first.append(jnp.where((slot >= 0) & (source < 0), slot, -1))
        weights.append(jnp.where(slot >= 0, gate_ref[0, at // cap, at % cap], 0.0))
    weight = column(weights, (8, LANES))[:, :1]
    first_id = column(from_first + [jnp.int32(-1)], (8, LANES))
    in_first = [jnp.where(first_id == i, 1.0, 0.0)[:, :1] for i in range(slots)]
    old_ids = column(wanted + [jnp.int32(-1)], (8, known))
    pick_old = one_hot(old_ids == iota(old_ids.shape, 1))
    if fresh:
        extra = sections * LATE
        new_ids = column(wanted + [jnp.int32(-1)], (8, extra))
        pick_new = one_hot(new_ids == iota(new_ids.shape, 1) + known)
        keep_old = one_hot(column(where_is, (known, known)) == iota((known, known), 1))
        take_new = one_hot(column(where_is, (known, extra)) == iota((known, extra), 1) + known)
    for part in chunks(width):
        old = table_ref[:, :, part].reshape(known, part.size)
        rows = dot(pick_old, old)
        if fresh:
            new = news_ref[:, :, part].reshape(extra, part.size)
            rows = rows + dot(pick_new, new)
            merged = dot(keep_old, old) + dot(take_new, new)
            merged_ref[:, :, part] = merged.astype(BF).reshape(sections, slots, part.size)
        first = first_ref[:, part].astype(F32)
        for i in range(slots):
            rows = rows + in_first[i] * first[i : i + 1]
        row_in_ref[:, part] = rows[:LATE]
        scaled = (weight * rows)[:LATE].astype(BF)
        for chip in range(sent_ref.shape[0]):
            sent_ref[chip, :, part] = scaled
    if note:
        lane = iota((LATE, LANES), 1)
        word = jnp.zeros((LATE, LANES), I32)
        for i in range(slots):
            word = jnp.where(lane == i, round_ref[place * slots + i], word)
        word = jnp.where(lane == slots, own_ref[slots], word).astype(F32).astype(BF)
        for chip in range(sent_ref.shape[0]):
            sent_ref[chip, :, pl.ds(width, LANES)] = word


def places(count, chips, cap, tok_group, core, taken=None):
    total = 2 * chips * count
    row = iota((total, LANES), 0)
    half = row // (chips * count)
    chip = (row // count) % chips
    index = chip * 2 + (core ^ half)
    if taken is None:
        slot = row % count
        return (slot // cap) * tok_group + index * cap + slot % cap
    place = jnp.full((total, LANES), -1, I32)
    for i, flag in enumerate(taken):
        place = jnp.where(flag, (i // cap) * tok_group + index * cap + i % cap, place)
    return place


def pass_kernel(count, late, cap, core_ref, now_ref, saved_ref, down_ref, up_ref, own_ref, other_ref, *refs):
    refs = list(refs)
    note_in = refs.pop(0) if late == 2 else None
    mine_ref, theirs_ref, hidden_ref = refs[:3]
    chips = own_ref.shape[0]
    micros, group, hid = saved_ref.shape[1:]
    width = mine_ref.shape[2]
    half = chips * count
    core = core_ref[0]
    taken = None
    if late:
        if late == 1:
            perm_ref, note_ref, most_ref = refs[3:]
            word = jnp.concatenate(
                [own_ref[:, :, pl.ds(width, LANES)].reshape(half, LANES), other_ref[:, :, pl.ds(width, LANES)].reshape(half, LANES)]
            ).astype(F32)
            note_ref[...] = word
            most_ref[0] = jnp.max(word).astype(I32)
        else:
            (perm_ref,) = refs[3:]
            word = note_in[...]
        now = now_ref[0].astype(F32)
        position = (iota((2 * half, 1), 0) % count).astype(F32)
        rank = jnp.zeros((2 * half, 1), F32)
        taken = []
        for i in range(micros * cap):
            hit = jnp.where(word[:, i : i + 1] == now, 1.0, 0.0)
            flag = jnp.where(rank == position, hit, 0.0)
            taken.append(jnp.broadcast_to(flag, (2 * half, LANES)) > 0.5)
            rank = rank + hit
    place = places(count, chips, cap, group, core, taken)
    perm = one_hot(place == iota(place.shape, 1))
    if late:
        perm_ref[...] = perm
    v = dot(perm, saved_ref[0].reshape(micros * group, hid))
    s = 1.0 / (1.0 + jnp.exp(-v))
    slope = s * (1.0 + v * (1.0 - s))
    back = jnp.zeros((2 * half, hid), F32)
    for part in chunks(width):
        rows = jnp.concatenate(
            [own_ref[:, :, part].reshape(half, part.size), other_ref[:, :, part].reshape(half, part.size)]
        )
        back = back + dot(rows, down_ref[0, :, part], NT)
    hidden = (back * slope).astype(BF)
    hidden_ref[...] = hidden
    for part in chunks(width):
        partial = dot(hidden, up_ref[0, :, part])
        mine_ref[:, :, part] = partial[:half].reshape(chips, count, part.size)
        theirs_ref[:, :, part] = partial[half:].astype(BF).reshape(chips, count, part.size)


def news_kernel(late, cap, now_ref, place_ref, round_ref, token_ref, row_in_ref, swapped_ref, news_ref):
    chips, count, width = swapped_ref.shape
    slots = token_ref.shape[1] * cap
    ids = own_picks(round_ref, place_ref[0], slots, now_ref[0]) if late else list(range(count))
    micro, token = [], []
    for c, slot in enumerate(ids):
        at = jnp.maximum(slot, 0)
        micro.append(jnp.where(slot >= 0, at // cap, -1 - c))
        token.append(token_ref[0, at // cap, at % cap])
    twins = []
    for b in range(count):
        same = [
            jnp.where((micro[a] == micro[b]) & (token[a] == token[b]), 1.0, 0.0) if a != b else jnp.float32(0.0)
            for a in range(count)
        ]
        twins.append(column(same, (count, LANES))[:, :1])
    for part in chunks(width):
        own = swapped_ref[0, :, part].astype(F32)
        for chip in range(1, chips):
            own = own + swapped_ref[chip, :, part].astype(F32)
        total = own
        for b in range(count):
            total = total + twins[b] * own[b : b + 1]
        rows = (row_in_ref[:, part].astype(F32) + total).astype(BF)
        for section in range(news_ref.shape[0]):
            news_ref[section, :, part] = rows


def grads_kernel(cap, core_ref, saved_ref, saved_t_ref, x_ref, hid1, hid2, hid3, perm2, perm3, own1, other1, own2, other2, own3, other3, up_ref, down_ref):
    micros, group, hid = saved_ref.shape[1:]
    natural = micros * group
    chips, slots, width = own1.shape
    place = places(slots, chips, cap, group, core_ref[0])
    perm1 = one_hot(place == iota(place.shape, 1))
    late = jnp.concatenate([perm2[...], perm3[...]])
    later = dot(one_hot(iota((8, late.shape[0]), 0) >= 0), late)[:1]
    masked1 = jnp.where(later > 0.5, 0.0, perm1.astype(F32)).astype(BF)
    perms = jnp.concatenate([masked1, late])
    v = saved_t_ref[...].astype(F32)
    act = (v * (1.0 / (1.0 + jnp.exp(-v)))).astype(BF)
    act_rows = dot(act, perms, NT).astype(BF)
    hidden = jnp.concatenate([hid1[...], hid2[...], hid3[...]])
    hidden_t = dot(hidden, perms, TN).astype(BF)
    for part in chunks(width):
        rows = jnp.concatenate(
            [r[:, :, part].reshape(chips * r.shape[1], part.size) for r in (own1, other1, own2, other2, own3, other3)]
        )
        down_ref[0, :, part] = dot(act_rows, rows).astype(BF)
        up_ref[0, :, part] = dot(hidden_t, x_ref[0, :, :, part].reshape(natural, part.size)).astype(BF)


def output_kernel(last_ref, round_ref, source_ref, grad_ref, table_ref, news_ref, out_ref):
    sections, slots, width = table_ref.shape
    known, extra = sections * slots, sections * LATE
    micros, tok_rows, _ = grad_ref.shape
    where_is = row_map(round_ref, sections, slots, last_ref[0])
    keep_old = one_hot(column(where_is, (known, known)) == iota((known, known), 1))
    take_new = one_hot(column(where_is, (known, extra)) == iota((known, extra), 1) + known)
    source = source_ref[...]
    chosen = one_hot(source[:, :known] == iota((micros * tok_rows, known), 1))
    from_old = dot(chosen, keep_old).astype(BF)
    from_new = dot(chosen, take_new).astype(BF)
    still = jnp.where(source < 0, 1.0, 0.0)[:, :1]
    for part in chunks(width):
        moved = dot(from_old, table_ref[:, :, part].reshape(known, part.size))
        moved = moved + dot(from_new, news_ref[:, :, part].reshape(extra, part.size))
        kept = grad_ref[:, :, part].reshape(micros * tok_rows, part.size).astype(F32)
        rows = (moved + still * kept).astype(BF)
        out_ref[0, :, :, part] = rows.reshape(micros, tok_rows, part.size)


def per_device(out_grad, x_rows, saved_u, w_up_t, w_down, gate, route_tokens, route_count):
    sections = lax.axis_size("section")
    dp_count = lax.axis_size("dp")
    section_index = lax.axis_index("section")
    core = lax.axis_index("dp") % 2
    micros, tok_rows, width = out_grad.shape
    cap = gate.shape[2]
    hid = w_down.shape[1]
    chips = dp_count // 2
    slots = micros * cap
    same_core = [[2 * chip + c for chip in range(chips)] for c in range(2)]
    sibling = [(i, i ^ 1) for i in range(dp_count)]
    place = section_index.reshape(1).astype(I32)
    core_id = core.reshape(1).astype(I32)

    def shape(dims, dtype):
        return jax.ShapeDtypeStruct(dims, dtype)

    def swap(block, axis, groups=None):
        return lax.all_to_all(block, axis, 0, 0, tiled=True, axis_index_groups=groups)

    def hop_along(info, distance):
        arrived = lax.ppermute(info, "section", [(i, i ^ distance) for i in range(sections)])
        return jnp.concatenate([info, arrived])

    def send(now, fresh, note, table, news=None):
        wide = width + (LANES if note else 0)
        outs = [shape((chips, LATE, wide), BF), shape((LATE, width), F32)]
        outs += [shape(table.shape, BF)] if fresh else []
        return call(
            functools.partial(send_kernel, fresh, note, cap),
            [SMEM] * 5 + [VMEM] * (3 if fresh else 2),
            outs,
            [VMEM] * len(outs),
            [pltpu.SMEM((sections * slots,), I32)],
        )(now, place, rounds_of, own_plan, gate, first, table, *([news] if fresh else []))

    def one_pass(now, late, own, note=None, tie=None):
        other = lax.ppermute(own, "dp", sibling)
        count = own.shape[1]
        total = 2 * chips * count
        outs = [shape((chips, count, width), F32), shape((chips, count, width), BF), shape((total, hid), BF)]
        specs = [VMEM] * 3
        if late:
            outs.append(shape((total, LANES), BF))
            specs.append(VMEM)
        if late == 1:
            outs += [shape((total, LANES), F32), shape((1,), I32)]
            specs += [VMEM, SMEM]
        mine, theirs, *rest = call(
            functools.partial(pass_kernel, count, late, cap),
            [SMEM, SMEM] + [VMEM] * (5 + (late == 2)),
            outs,
            specs,
            flops=4 * total * hid * width,
            size=4 * hid * width + 8 * total * width,
        )(core_id, now, saved_u, w_down, w_up_t, own, other, *([note] if late == 2 else []))
        if tie is not None:
            theirs, tied = lax.optimization_barrier((theirs, tie))
            rest.append(tied)
        arrived = lax.ppermute(theirs, "dp", sibling)
        pair_sum = (mine + arrived.astype(F32)).astype(BF)
        return other, swap(pair_sum, "dp", same_core), rest

    def make_news(now, late, row_in, swapped):
        return call(
            functools.partial(news_kernel, late, cap),
            [SMEM] * 4 + [VMEM] * 2,
            shape((sections,) + swapped.shape[1:], BF),
            VMEM,
        )(now, place, rounds_of if late else place, route_tokens, row_in, swapped)

    def number(n):
        return jnp.full((1,), n, I32)

    sent, first, info = call(
        first_kernel,
        [SMEM] * 3 + [VMEM],
        [shape((chips, slots, width), BF), shape((slots, width), BF), shape((1, LANES), I32)],
        [VMEM] * 3,
    )(route_tokens, route_count, gate, out_grad)
    hops = [1 << k for k in range(sections.bit_length() - 1)]
    info = hop_along(info, hops[0])
    own1 = swap(sent, "dp", same_core)
    info = hop_along(info, hops[1])
    own1, info = lax.optimization_barrier((own1, info))
    for distance in hops[2:]:
        info = hop_along(info, distance)
    other1, swapped, (hid1, info) = one_pass(number(1), 0, own1, tie=info)
    rounds_of, own_plan, source = call(
        functools.partial(plan_kernel, sections, cap, tok_rows),
        [SMEM, SMEM],
        [shape((sections * slots,), I32), shape((slots + 1,), I32), shape((micros * tok_rows, LANES), I32)],
        [SMEM, SMEM, VMEM],
        [pltpu.SMEM((micros * tok_rows,), I32)] * 2,
    )(info, place)
    table = swap(make_news(number(1), False, first, swapped), "section")

    sent, row_in = send(number(2), False, True, table)
    own2 = swap(sent, "dp", same_core)
    other2, swapped, (hid2, perm2, note, most) = one_pass(number(2), 1, own2)
    news = swap(make_news(number(2), True, row_in, swapped), "section")

    sent, row_in, table = send(number(3), True, False, table, news)
    own3 = swap(sent, "dp", same_core)
    other3, swapped, (hid3, perm3) = one_pass(number(3), 2, own3, note)
    news = make_news(number(3), True, row_in, swapped)

    def more(state):
        return state[0] < most[0]

    def again(state):
        done, news, table, own1, other1, hid1 = state
        now = (done + 1).reshape(1)
        sent, row_in, table = send(now, True, False, table, swap(news, "section"))
        own = swap(sent, "dp", same_core)
        other, swapped, (hidden, _) = one_pass(now, 2, own, note)
        news = make_news(now, True, row_in, swapped)
        hit = note[::LATE, :slots] == now[0].astype(F32)
        rank = jnp.cumsum(hit.astype(I32), axis=1) - 1
        hid1 = hid1.reshape(dp_count, slots, hid)
        hidden = hidden.reshape(dp_count, LATE, hid)
        for c in range(LATE):
            taken = (hit & (rank == c))[:, :, None]
            own1 = jnp.where(taken[:chips], own[:, c : c + 1], own1)
            other1 = jnp.where(taken[chips:], other[:, c : c + 1], other1)
            hid1 = jnp.where(taken, hidden[:, c : c + 1], hid1)
        return done + 1, news, table, own1, other1, hid1.reshape(dp_count * slots, hid)

    done, news, table, own1, other1, hid1 = lax.while_loop(
        more, again, (jnp.int32(3), news, table, own1, other1, hid1)
    )
    news = swap(news, "section")

    grad_up, grad_down = call(
        functools.partial(grads_kernel, cap),
        [SMEM] + [VMEM] * 14,
        [shape((1, hid, width), BF)] * 2,
        [VMEM] * 2,
        flops=8 * dp_count * slots * hid * width,
        size=8 * hid * width,
    )(
        core_id, saved_u, saved_u.reshape(micros * dp_count * cap, hid).T, x_rows,
        hid1, hid2, hid3, perm2, perm3, own1, other1, own2[..., :width], other2[..., :width], own3, other3,
    )
    in_grad = call(
        output_kernel,
        [SMEM, SMEM] + [VMEM] * 4,
        shape((1, micros, tok_rows, width), BF),
        VMEM,
    )(done.reshape(1), rounds_of, source, out_grad, table, news)
    return (in_grad, grad_up, grad_down)


def solution(mesh):
    return jax.shard_map(
        per_device,
        mesh=mesh,
        in_specs=(
            P(None, "dp", None),
            P("section", None, None, None),
            P("section", None, None, "dp"),
            P("section", "dp", None),
            P("section", "dp", None),
            P("section", None, "dp"),
            P("section", None, "dp"),
            P("section", None, "dp"),
        ),
        out_specs=(
            P("section", None, "dp", None),
            P("section", "dp", None),
            P("section", "dp", None),
        ),
        check_vma=False,
    )
```

time: 821 us -> 185 us (0.23)
  waiting for transfers between devices: 318 us -> 53.3 us
  blocking collectives: 219 us -> 52.6 us
  matrix products: 94.3 us -> 0 us
  other arithmetic: 73.6 us -> 2.92 us
  local copies, waits for them, and re-layouts: 43.5 us -> 4.25 us
  Pallas kernels: 0 us -> 28.3 us
  starting transfers between devices: 62.3 us -> 41.5 us
    all_gather x9 -> x0, blocking collectives: 219 us -> none  [tick_step(): row_piece = lax.all_gather(scaled, 'dp', axis=0, tiled=True)]
    all_to_all x9 -> x5, waiting for transfers between devices: 190 us -> 39.6 us  [swap(): lax.all_to_all(block, axis, 0, 0, tiled=True, axis_index_groups=groups)]
    ppermute x9, waiting for transfers between devices: 128 us -> 13.6 us  [the longest x3 5.45 us: one_pass(): arrived = lax.ppermute(theirs, 'dp', sibling)]
    dot_general x36 -> x0, matrix products: 94.3 us -> none  [the longest x9 42.7 us: tick_step(): jnp.einsum('rh,rd->hd', hidden_grad, x_rows[0, micro_pick], preferred_ele...]
    all_to_all x0 -> x4, blocking collectives: none -> 52.6 us  [swap(): lax.all_to_all(block, axis, 0, 0, tiled=True, axis_index_groups=groups)]
    pallas_call x0 -> x12, Pallas kernels: none -> 28.3 us  [the longest x3 10.1 us: one_pass(): call(functools.partial(pass_kernel, count, late, cap), [SMEM, SMEM] + [VM...]
    reshape x9 -> x1, local copies, waits for them, and re-layouts: 28.1 us -> 0.11 us  [per_device(): saved_u.reshape(micros * dp_count * cap, hid)]
    select_n x27 -> x0, other arithmetic: 26.6 us -> none  [the longest x9 20.6 us: tick_step(): jnp.where(valid_tick, lax.dynamic_update_index_in_dim(in_grad, new_slab,...]
  transfers between devices with their start and end apart: 18 -> 14, of which waited for: 18 -> 13; matrix products, arithmetic and copies ran while one was open for 7% -> 0% of each run, Pallas kernels for 0% -> 4%
where the time goes in v3:
time: 185 us; the launch traced here: 184 us
  waiting for transfers between devices  53.3 us (29%)
  blocking collectives  52.6 us (28%)
  starting transfers between devices  41.5 us (22%)
  Pallas kernels  28.3 us (15%)
  local copies, waits for them, and re-layouts  4.25 us (2%)
  other arithmetic  2.92 us (2%)
    all_to_all x4, blocking collectives, swap(): lax.all_to_all(block, axis, 0, 0, tiled=True, axis_index_groups=groups)  52.6 us
    all_to_all x5, waiting for transfers between devices, swap(): lax.all_to_all(block, axis, 0, 0, tiled=True, axis_index_groups=groups)  39.6 us
    all_to_all x5, starting transfers between devices, swap(): lax.all_to_all(block, axis, 0, 0, tiled=True, axis_index_groups=groups)  28.5 us
    ppermute x3, starting transfers between devices, hop_along(): lax.ppermute(info, 'section', [(i, i ^ distance) for i in range(sections)])  12.4 us
    pallas_call x3, Pallas kernels, one_pass(): call(functools.partial(pass_kernel, count, late, cap), [SMEM, SMEM] + [VM...  10.1 us
    ppermute x3, waiting for transfers between devices, one_pass(): arrived = lax.ppermute(theirs, 'dp', sibling)  5.45 us
    pallas_call x1, Pallas kernels, per_device(): call(functools.partial(grads_kernel, cap), [SMEM] + [VMEM] * 14, [shape((...  4.98 us
    ppermute x3, waiting for transfers between devices, hop_along(): lax.ppermute(info, 'section', [(i, i ^ distance) for i in range(sections)])  4.73 us
  transfers between devices with their start and end apart: 14, of which 13 were waited for; matrix products, arithmetic and copies ran while one was open for 0% of the time, Pallas kernels for 4%

profile of v3, /device:TPU:8, one launch (start us, length us, event | category | flops | bytes accessed | tf_op | source)
XLA Modules:
  0.0 184.2 jit_solution(677519471015774644)
XLA Ops:
  0.6 0.7 copy.15.count_ref
  1.4 1.4 copy-done
  2.8 2.1 %shard_map.103 = (bf16[16,4,6144]{2,1,0:T(4,128)(2,1)}, bf16[4,6144]{1,0:T(4,128)(2,1)S(1)}, s32[1,128]{1,0:T(1,128)S(1)}) custom-call(s32[1,2,2]{2,1,0:T(2,128)} %token_ref.7, s32[1,2,1]{2,1,0:T(2,128)S(1)} %copy.15.count_ref, f32[1,2,2]{2,1,0:T(2,128)} %gate_ref.5, bf16[2,64,6144]{2,1,0:T(8,128)(2,1)S(1)} %copy-done), custom_call_target="tpu_custom_call" | custom-call | flops 1000000 | bytes 1000000 | tf_op jit(solution)/shard_map/pallas_call | solution.py:433
  4.9 7.4 %all-to-all-start.3 = ((bf16[16,4,6144]{2,1,0:T(4,128)(2,1)}), bf16[16,4,6144]{2,1,0:T(4,128)(2,1)}, u32[]{:S(2)}, u32[]{:S(2)}) async-start(bf16[16,4,6144]{2,1,0:T(4,128)(2,1)} %get-tuple-element.257), calls=%async_computation.3 | async-start | bytes 1572864 | tf_op jit(solution)/shard_map/all_to_all | solution.py:377
  12.3 1.9 %collective-permute-start.2 = (s32[1,128]{1,0:T(1,128)S(1)}, s32[1,128]{1,0:T(1,128)S(1)}, u32[]{:S(2)}, u32[]{:S(2)}) collective-permute-start(s32[1,128]{1,0:T(1,128)S(1)} %get-tuple-element.258), channel_id=1, source_target_pairs={{0,32},{32,0},{64,96},{96,64},{128,160},{160,128},{192,224},{224,1... | collective-permute-start | bytes 1544 | tf_op jit(solution)/shard_map/ppermute | solution.py:380
  14.2 1.6 collective-permute-done.2
  15.8 3.3 %collective-permute-start.3 = (s32[2,128]{1,0:T(2,128)S(1)}, s32[2,128]{1,0:T(2,128)S(1)}, u32[]{:S(2)}, u32[]{:S(2)}) collective-permute-start(s32[2,128]{1,0:T(2,128)S(1)} %pad_add_fusion.2), channel_id=1, source_target_pairs={{0,64},{32,96},{64,0},{96,32},{128,192},{160,224},{192,128},{224,1... | collective-permute-start | bytes 3080 | tf_op jit(solution)/shard_map/ppermute | solution.py:380
  19.1 1.5 collective-permute-done.3
  20.6 4.7 %all-to-all-done.3.own_ref = bf16[16,4,6144]{2,1,0:T(4,128)(2,1)} async-done(((bf16[16,4,6144]{2,1,0:T(4,128)(2,1)}), bf16[16,4,6144]{2,1,0:T(4,128)(2,1)}, u32[]{:S(2)}, u32[]{:S(2)}) %all-to-all-start.3) | async-done | bytes 786464 | tf_op jit(solution)/shard_map/all_to_all | solution.py:377
  25.4 0.0 collective-permute-start.4
  25.4 7.2 %collective-permute-start.5 = (s32[4,128]{1,0:T(4,128)S(1)}, s32[4,128]{1,0:T(4,128)S(1)}, u32[]{:S(2)}, u32[]{:S(2)}) collective-permute-start(s32[4,128]{1,0:T(4,128)S(1)} %pad_add_fusion.1), channel_id=1, source_target_pairs={{0,128},{32,160},{64,192},{96,224},{128,0},{160,32},{192,64},{224,... | collective-permute-start | bytes 6152 | tf_op jit(solution)/shard_map/ppermute | solution.py:380
  32.6 1.6 collective-permute-done.5
  34.1 0.0 collective-permute-done.4.other_ref
  34.1 0.0 copy-done.3
  34.1 0.0 copy-done.11
  34.2 4.1 %shard_map.104 = (f32[16,4,6144]{2,1,0:T(4,128)S(1)}, bf16[16,4,6144]{2,1,0:T(4,128)(2,1)S(1)}, bf16[128,168]{1,0:T(8,128)(2,1)S(1)}) custom-call(s32[1]{0:T(128)} %bitcast.5.core_ref, s32[1]{0:T(128)} %constant.46.clone.1.now_ref, bf16[1,2,64,168]{3,2,1,0:T(8,128)(2,1)S(1)} %copy-done.11, bf16[1,168,6144]{2,1,0:T(8,128)(2,1)S(1)} %copy-done.3, ...), custom_call_target="tpu_custom_call" | custom-call | flops 528482304 | bytes 10420224 | tf_op jit(solution)/shard_map/pallas_call | solution.py:407
  38.2 0.1 collective-permute-start.6
  38.3 2.3 %collective-permute-done.6 = bf16[16,4,6144]{2,1,0:T(4,128)(2,1)S(1)} collective-permute-done((bf16[16,4,6144]{2,1,0:T(4,128)(2,1)S(1)}, bf16[16,4,6144]{2,1,0:T(4,128)(2,1)S(1)}, u32[]{:S(2)}, u32[]{:S(2)}) %collective-permute-start.6) | collective-permute-done | bytes 786464 | tf_op jit(solution)/shard_map/ppermute | solution.py:418
  40.6 1.3 add_convert_fusion.1
  41.9 5.0 %all-to-all-start.4 = ((bf16[16,4,6144]{2,1,0:T(4,128)(2,1)}), bf16[16,4,6144]{2,1,0:T(4,128)(2,1)S(1)}, u32[]{:S(2)}, u32[]{:S(2)}) async-start(bf16[16,4,6144]{2,1,0:T(4,128)(2,1)} %add_convert_fusion.1), calls=%async_computation.4 | async-start | bytes 1572864 | tf_op jit(solution)/shard_map/all_to_all | solution.py:377
  46.9 13.9 %all-to-all-done.4.swapped_ref = bf16[16,4,6144]{2,1,0:T(4,128)(2,1)S(1)} async-done(((bf16[16,4,6144]{2,1,0:T(4,128)(2,1)}), bf16[16,4,6144]{2,1,0:T(4,128)(2,1)S(1)}, u32[]{:S(2)}, u32[]{:S(2)}) %all-to-all-start.4) | async-done | bytes 786464 | tf_op jit(solution)/shard_map/all_to_all | solution.py:377
  60.8 0.0 copy-done.12
  60.8 1.5 shard_map.106
  62.4 7.2 %all-to-all-start.5 = ((bf16[8,4,6144]{2,1,0:T(4,128)(2,1)}), bf16[8,4,6144]{2,1,0:T(4,128)(2,1)S(1)}, u32[]{:S(2)}, u32[]{:S(2)}) async-start(bf16[8,4,6144]{2,1,0:T(4,128)(2,1)} %shard_map.106), calls=%async_computation.5 | async-start | bytes 786432 | tf_op jit(solution)/shard_map/all_to_all | solution.py:377
  69.6 2.8 %shard_map.105 = (s32[32]{0:T(128)S(1)}, s32[5]{0:T(128)S(1)}, s32[128,128]{1,0:T(8,128)S(1)}) custom-call(s32[8,128]{1,0:T(8,128)S(1)} %pad_add_fusion.info_ref, s32[1]{0:T(128)} %bitcast.4.place_ref.round_ref), custom_call_target="tpu_custom_call" | custom-call | flops 1000000 | bytes 1000000 | tf_op jit(solution)/shard_map/pallas_call | solution.py:447
  72.4 9.8 %all-to-all-done.5.table_ref = bf16[8,4,6144]{2,1,0:T(4,128)(2,1)S(1)} async-done(((bf16[8,4,6144]{2,1,0:T(4,128)(2,1)}), bf16[8,4,6144]{2,1,0:T(4,128)(2,1)S(1)}, u32[]{:S(2)}, u32[]{:S(2)}) %all-to-all-start.5) | async-done | bytes 393248 | tf_op jit(solution)/shard_map/all_to_all | solution.py:377
  82.1 0.0 copy-done.13
  82.1 0.8 shard_map.107
  82.9 13.7 %all_to_all.63.own_ref = bf16[16,2,6272]{2,1,0:T(2,128)(2,1)S(1)} all-to-all(bf16[16,2,6272]{2,1,0:T(2,128)(2,1)S(1)} %get-tuple-element.269), channel_id=1, replica_groups={{0,2,4,6,8,10,12,14,16,18,20,22,24,26,28,30},{1,3,5,7,9,11,13,15,17,19,..., dimensions={0} | all-to-all | bytes 802816 | tf_op jit(solution)/shard_map/all_to_all | solution.py:377
  96.7 0.0 collective-permute-start.7
  96.7 1.7 collective-permute-done.7.other_ref
  98.4 4.4 %shard_map.108 = (f32[16,2,6144]{2,1,0:T(2,128)S(1)}, bf16[16,2,6144]{2,1,0:T(2,128)(2,1)S(1)}, bf16[64,168]{1,0:T(8,128)(2,1)S(1)}, bf16[64,128]{1,0:T(8,128)(2...) custom-call(s32[1]{0:T(128)} %bitcast.5.core_ref, s32[1]{0:T(128)} %constant.47.clone.1.now_ref, ...), custom_call_target="tpu_custom_call" | custom-call | flops 264241152 | bytes 7274496 | tf_op jit(solution)/shard_map/pallas_call | solution.py:407
  102.8 0.2 collective-permute-start.8
  103.0 1.6 collective-permute-done.8
  104.6 0.4 add_convert_fusion.3
  105.0 0.0 copy-start.4
  105.0 13.9 %all_to_all.64.swapped_ref = bf16[16,2,6144]{2,1,0:T(2,128)(2,1)S(1)} all-to-all(bf16[16,2,6144]{2,1,0:T(2,128)(2,1)S(1)} %add_convert_fusion.3), channel_id=1, replica_groups={{0,2,4,6,8,10,12,14,16,18,20,22,24,26,28,30},{1,3,5,7,9,11,13,15,17,19,..., dimensions={0} | all-to-all | bytes 786432 | tf_op jit(solution)/shard_map/all_to_all | solution.py:377
  118.9 0.7 shard_map.109
  119.6 12.5 %all_to_all.65.refs_0_ = bf16[8,2,6144]{2,1,0:T(2,128)(2,1)S(1)} all-to-all(bf16[8,2,6144]{2,1,0:T(2,128)(2,1)S(1)} %shard_map.109), channel_id=1, replica_groups=mesh['section'=8,'dp'=32] {'section'}, dimensions={0} | all-to-all | bytes 393216 | tf_op jit(solution)/shard_map/all_to_all | solution.py:377
  132.2 1.1 shard_map.110
  133.3 12.4 %all_to_all.66.own_ref.own3 = bf16[16,2,6144]{2,1,0:T(2,128)(2,1)S(1)} all-to-all(bf16[16,2,6144]{2,1,0:T(2,128)(2,1)S(1)} %get-tuple-element.273), channel_id=1, replica_groups={{0,2,4,6,8,10,12,14,16,18,20,22,24,26,28,30},{1,3,5,7,9,11,13,15,17,19,..., dimensions={0} | all-to-all | bytes 786432 | tf_op jit(solution)/shard_map/all_to_all | solution.py:377
  145.7 0.0 collective-permute-start.9
  145.7 1.7 collective-permute-done.9.other_ref.other3
  147.4 0.0 copy-done.6
  147.4 0.0 copy-done.4
  147.4 1.7 shard_map.111
  149.2 0.2 collective-permute-start.10
  149.4 1.6 collective-permute-done.10
  151.0 1.2 add_convert_fusion.2
  152.1 5.3 %all-to-all-start.10 = ((bf16[16,2,6144]{2,1,0:T(2,128)(2,1)}), bf16[16,2,6144]{2,1,0:T(2,128)(2,1)S(1)}, u32[]{:S(2)}, u32[]{:S(2)}) async-start(bf16[16,2,6144]{2,1,0:T(2,128)(2,1)} %add_convert_fusion.2), calls=%async_computation.10 | async-start | bytes 786432 | tf_op jit(solution)/shard_map/all_to_all | solution.py:377
  157.4 8.6 %all-to-all-done.10.swapped_ref = bf16[16,2,6144]{2,1,0:T(2,128)(2,1)S(1)} async-done(((bf16[16,2,6144]{2,1,0:T(2,128)(2,1)}), bf16[16,2,6144]{2,1,0:T(2,128)(2,1)S(1)}, u32[]{:S(2)}, u32[]{:S(2)}) %all-to-all-start.10) | async-done | bytes 393248 | tf_op jit(solution)/shard_map/all_to_all | solution.py:377
  166.0 1.4 shard_map.112
  167.4 0.6 while.20
  168.0 0.0 copy-start.9
  168.0 3.6 %all-to-all-start.11 = ((bf16[8,2,6144]{2,1,0:T(2,128)(2,1)}), bf16[8,2,6144]{2,1,0:T(2,128)(2,1)S(1)}, u32[]{:S(2)}, u32[]{:S(2)}) async-start(bf16[8,2,6144]{2,1,0:T(2,128)(2,1)} %get-tuple-element.283), calls=%async_computation.11 | async-start | bytes 393216 | tf_op jit(solution)/shard_map/all_to_all | solution.py:377
  171.6 0.1 copy.16
  171.8 0.3 slice.88.own2
  172.0 0.3 slice.89.other2
  172.3 0.0 copy-done.9
  172.3 0.0 copy-start.2
  172.3 1.4 copy-done.2
  173.7 5.0 %shard_map.114 = (bf16[1,168,6144]{2,1,0:T(8,128)(2,1)}, bf16[1,168,6144]{2,1,0:T(8,128)(2,1)}) custom-call(s32[1]{0:T(128)} %bitcast.5.core_ref, bf16[1,2,64,168]{3,2,1,0:T(8,128)(2,1)S(1)} %get-tuple-element.585, bf16[168,128]{1,0:T(8,128)(2,1)S(1)} %bitcast.36, bf16[1,2,64,6144]{3,2,1,0:T(8,128)(2,1)S(1)} %copy-done.2, ...), custom_call_target="tpu_custom_call" | custom-call | flops 1056964608 | bytes 8257536 | tf_op jit(solution)/shard_map/pallas_call | solution.py:492
  178.7 2.6 %all-to-all-done.11.news_ref = bf16[8,2,6144]{2,1,0:T(2,128)(2,1)S(1)} async-done(((bf16[8,2,6144]{2,1,0:T(2,128)(2,1)}), bf16[8,2,6144]{2,1,0:T(2,128)(2,1)S(1)}, u32[]{:S(2)}, u32[]{:S(2)}) %all-to-all-start.11) | async-done | bytes 196640 | tf_op jit(solution)/shard_map/all_to_all | solution.py:377
  181.4 2.8 %shard_map.113 = bf16[1,2,64,6144]{3,2,1,0:T(8,128)(2,1)} custom-call(s32[1]{0:T(128)} %bitcast.6.last_ref, s32[32]{0:T(128)S(1)} %get-tuple-element.591, s32[128,128]{1,0:T(8,128)S(1)} %get-tuple-element.281.source_ref, bf16[2,64,6144]{2,1,0:T(8,128)(2,1)S(1)} %copy-done.1, bf16[8,4,6144]{2,1,0:T(4,128)(2,1)S(1)} %copy-done.10, ...), custom_call_target="tpu_custom_call" | custom-call | flops 1000000 | bytes 1000000 | tf_op jit(solution)/shard_map/pallas_call | solution.py:503
  (13 shorter events, 0.0 us)
Async XLA Ops:
  1.4 1.4 copy-start
  2.8 31.4 %copy-start.3 = (bf16[1,168,6144]{2,1,0:T(8,128)(2,1)S(1)}, bf16[1,168,6144]{2,1,0:T(8,128)(2,1)}, u32[]{:S(2)}) copy-start(bf16[1,168,6144]{2,1,0:T(8,128)(2,1)} %down_ref.5) | copy-start | bytes 6193156
  2.8 31.4 %copy-start.11 = (bf16[1,2,64,168]{3,2,1,0:T(8,128)(2,1)S(1)}, bf16[1,2,64,168]{3,2,1,0:T(8,128)(2,1)}, u32[]{:S(2)}) copy-start(bf16[1,2,64,168]{3,2,1,0:T(8,128)(2,1)} %saved_ref.7) | copy-start | bytes 129028
  4.9 20.5 %all-to-all-start.3 = ((bf16[16,4,6144]{2,1,0:T(4,128)(2,1)}), bf16[16,4,6144]{2,1,0:T(4,128)(2,1)}, u32[]{:S(2)}, u32[]{:S(2)}) async-start(bf16[16,4,6144]{2,1,0:T(4,128)(2,1)} %get-tuple-element.257), calls=%async_computation.3 | async-start | bytes 1572864 | tf_op jit(solution)/shard_map/all_to_all | solution.py:377
  12.3 3.5 %collective-permute-start.2 = (s32[1,128]{1,0:T(1,128)S(1)}, s32[1,128]{1,0:T(1,128)S(1)}, u32[]{:S(2)}, u32[]{:S(2)}) collective-permute-start(s32[1,128]{1,0:T(1,128)S(1)} %get-tuple-element.258), channel_id=1, source_target_pairs={{0,32},{32,0},{64,96},{96,64},{128,160},{160,128},{192,224},{224,1... | collective-permute-start | bytes 1544 | tf_op jit(solution)/shard_map/ppermute | solution.py:380
  15.8 4.8 %collective-permute-start.3 = (s32[2,128]{1,0:T(2,128)S(1)}, s32[2,128]{1,0:T(2,128)S(1)}, u32[]{:S(2)}, u32[]{:S(2)}) collective-permute-start(s32[2,128]{1,0:T(2,128)S(1)} %pad_add_fusion.2), channel_id=1, source_target_pairs={{0,64},{32,96},{64,0},{96,32},{128,192},{160,224},{192,128},{224,1... | collective-permute-start | bytes 3080 | tf_op jit(solution)/shard_map/ppermute | solution.py:380
  25.4 8.8 %collective-permute-start.4 = (bf16[16,4,6144]{2,1,0:T(4,128)(2,1)}, bf16[16,4,6144]{2,1,0:T(4,128)(2,1)}, u32[]{:S(2)}, u32[]{:S(2)}) collective-permute-start(bf16[16,4,6144]{2,1,0:T(4,128)(2,1)} %all-to-all-done.3.own_ref), channel_id=1, source_target_pairs={{0,1},{1,0},{2,3},{3,2},{4,5},{5,4},{6,7},{7,6},{8,9},{9,8},{10,11... | collective-permute-start | bytes 2359304 | tf_op jit(solution)/shard_map/ppermute | solution.py:396
  25.4 8.8 %collective-permute-start.5 = (s32[4,128]{1,0:T(4,128)S(1)}, s32[4,128]{1,0:T(4,128)S(1)}, u32[]{:S(2)}, u32[]{:S(2)}) collective-permute-start(s32[4,128]{1,0:T(4,128)S(1)} %pad_add_fusion.1), channel_id=1, source_target_pairs={{0,128},{32,160},{64,192},{96,224},{128,0},{160,32},{192,64},{224,... | collective-permute-start | bytes 6152 | tf_op jit(solution)/shard_map/ppermute | solution.py:380
  38.2 2.4 %collective-permute-start.6 = (bf16[16,4,6144]{2,1,0:T(4,128)(2,1)S(1)}, bf16[16,4,6144]{2,1,0:T(4,128)(2,1)S(1)}, u32[]{:S(2)}, u32[]{:S(2)}) collective-permute-start(bf16[16,4,6144]{2,1,0:T(4,128)(2,1)S(1)} %get-tuple-element.267), channel_id=1, source_target_pairs={{0,1},{1,0},{2,3},{3,2},{4,5},{5,4},{6,7},{7,6},{8,9},{9,8},{10,11... | collective-permute-start | bytes 2359304 | tf_op jit(solution)/shard_map/ppermute | solution.py:418
  41.9 18.9 %copy-start.12 = (s32[1,2,2]{2,1,0:T(2,128)S(1)}, s32[1,2,2]{2,1,0:T(2,128)}, u32[]{:S(2)}) copy-start(s32[1,2,2]{2,1,0:T(2,128)} %token_ref.7) | copy-start | bytes 52
  41.9 40.2 %copy-start.13 = (f32[1,2,2]{2,1,0:T(2,128)S(1)}, f32[1,2,2]{2,1,0:T(2,128)}, u32[]{:S(2)}) copy-start(f32[1,2,2]{2,1,0:T(2,128)} %gate_ref.5) | copy-start | bytes 52
  41.9 18.9 %all-to-all-start.4 = ((bf16[16,4,6144]{2,1,0:T(4,128)(2,1)}), bf16[16,4,6144]{2,1,0:T(4,128)(2,1)S(1)}, u32[]{:S(2)}, u32[]{:S(2)}) async-start(bf16[16,4,6144]{2,1,0:T(4,128)(2,1)} %add_convert_fusion.1), calls=%async_computation.4 | async-start | bytes 1572864 | tf_op jit(solution)/shard_map/all_to_all | solution.py:377
  62.4 19.8 %all-to-all-start.5 = ((bf16[8,4,6144]{2,1,0:T(4,128)(2,1)}), bf16[8,4,6144]{2,1,0:T(4,128)(2,1)S(1)}, u32[]{:S(2)}, u32[]{:S(2)}) async-start(bf16[8,4,6144]{2,1,0:T(4,128)(2,1)} %shard_map.106), calls=%async_computation.5 | async-start | bytes 786432 | tf_op jit(solution)/shard_map/all_to_all | solution.py:377
  96.7 1.7 collective-permute-start.7
  102.8 1.8 collective-permute-start.8
  104.6 42.9 %copy-start.6 = (bf16[1,168,6144]{2,1,0:T(8,128)(2,1)S(1)}, bf16[1,168,6144]{2,1,0:T(8,128)(2,1)}, u32[]{:S(2)}) copy-start(bf16[1,168,6144]{2,1,0:T(8,128)(2,1)} %up_ref.5) | copy-start | bytes 6193156
  105.0 42.4 %copy-start.4 = (bf16[1,168,6144]{2,1,0:T(8,128)(2,1)S(1)}, bf16[1,168,6144]{2,1,0:T(8,128)(2,1)}, u32[]{:S(2)}) copy-start(bf16[1,168,6144]{2,1,0:T(8,128)(2,1)} %down_ref.5) | copy-start | bytes 6193156
  145.7 1.7 collective-permute-start.9
  149.2 1.8 collective-permute-start.10
  152.1 13.9 %all-to-all-start.10 = ((bf16[16,2,6144]{2,1,0:T(2,128)(2,1)}), bf16[16,2,6144]{2,1,0:T(2,128)(2,1)S(1)}, u32[]{:S(2)}, u32[]{:S(2)}) async-start(bf16[16,2,6144]{2,1,0:T(2,128)(2,1)} %add_convert_fusion.2), calls=%async_computation.10 | async-start | bytes 786432 | tf_op jit(solution)/shard_map/all_to_all | solution.py:377
  168.0 4.3 %copy-start.9 = (bf16[8,4,6144]{2,1,0:T(4,128)(2,1)}, bf16[8,4,6144]{2,1,0:T(4,128)(2,1)S(1)}, u32[]{:S(2)}) copy-start(bf16[8,4,6144]{2,1,0:T(4,128)(2,1)S(1)} %get-tuple-element.282.table_ref) | copy-start | bytes 1179652
  168.0 13.4 %all-to-all-start.11 = ((bf16[8,2,6144]{2,1,0:T(2,128)(2,1)}), bf16[8,2,6144]{2,1,0:T(2,128)(2,1)S(1)}, u32[]{:S(2)}, u32[]{:S(2)}) async-start(bf16[8,2,6144]{2,1,0:T(2,128)(2,1)} %get-tuple-element.283), calls=%async_computation.11 | async-start | bytes 393216 | tf_op jit(solution)/shard_map/all_to_all | solution.py:377
  172.3 1.4 copy-start.2
  173.7 7.6 %copy-start.1 = (bf16[2,64,6144]{2,1,0:T(8,128)(2,1)S(1)}, bf16[2,64,6144]{2,1,0:T(8,128)(2,1)}, u32[]{:S(2)}) copy-start(bf16[2,64,6144]{2,1,0:T(8,128)(2,1)} %grad_ref.3) | copy-start | bytes 4718596
  173.7 7.6 %copy-start.10 = (bf16[8,4,6144]{2,1,0:T(4,128)(2,1)S(1)}, bf16[8,4,6144]{2,1,0:T(4,128)(2,1)}, u32[]{:S(2)}) copy-start(bf16[8,4,6144]{2,1,0:T(4,128)(2,1)} %copy-done.9) | copy-start | bytes 1179652

commit v4 on v3

--- a/solution.py
+++ b/solution.py
@@ -25,7 +25,7 @@
         out_specs=out_specs,
         out_shape=outs,
         scratch_shapes=list(scratch),
-        compiler_params=pltpu.CompilerParams(vmem_limit_bytes=40 * 1024 * 1024),
+        compiler_params=pltpu.CompilerParams(vmem_limit_bytes=24 * 1024 * 1024),
         cost_estimate=pl.CostEstimate(flops=flops, bytes_accessed=size, transcendentals=0),
     )
 
@@ -392,7 +392,7 @@
             [pltpu.SMEM((sections * slots,), I32)],
         )(now, place, rounds_of, own_plan, gate, first, table, *([news] if fresh else []))
 
-    def one_pass(now, late, own, note=None, tie=None):
+    def one_pass(now, late, own, note=None, tie=None, beside=None):
         other = lax.ppermute(own, "dp", sibling)
         count = own.shape[1]
         total = 2 * chips * count
@@ -412,12 +412,13 @@
             flops=4 * total * hid * width,
             size=4 * hid * width + 8 * total * width,
         )(core_id, now, saved_u, w_down, w_up_t, own, other, *([note] if late == 2 else []))
-        if tie is not None:
-            theirs, tied = lax.optimization_barrier((theirs, tie))
-            rest.append(tied)
         arrived = lax.ppermute(theirs, "dp", sibling)
         pair_sum = (mine + arrived.astype(F32)).astype(BF)
-        return other, swap(pair_sum, "dp", same_core), rest
+        if beside is None:
+            return other, swap(pair_sum, "dp", same_core), rest
+        pair_sum, tie = lax.optimization_barrier((pair_sum, tie))
+        swapped, *done = lax.optimization_barrier((swap(pair_sum, "dp", same_core), *beside(tie)))
+        return other, swapped, rest, done
 
     def make_news(now, late, row_in, swapped):
         return call(
@@ -441,16 +442,19 @@
     own1 = swap(sent, "dp", same_core)
     info = hop_along(info, hops[1])
     own1, info = lax.optimization_barrier((own1, info))
-    for distance in hops[2:]:
-        info = hop_along(info, distance)
-    other1, swapped, (hid1, info) = one_pass(number(1), 0, own1, tie=info)
-    rounds_of, own_plan, source = call(
-        functools.partial(plan_kernel, sections, cap, tok_rows),
-        [SMEM, SMEM],
-        [shape((sections * slots,), I32), shape((slots + 1,), I32), shape((micros * tok_rows, LANES), I32)],
-        [SMEM, SMEM, VMEM],
-        [pltpu.SMEM((micros * tok_rows,), I32)] * 2,
-    )(info, place)
+
+    def plan(info):
+        for distance in hops[2:]:
+            info = hop_along(info, distance)
+        return call(
+            functools.partial(plan_kernel, sections, cap, tok_rows),
+            [SMEM, SMEM],
+            [shape((sections * slots,), I32), shape((slots + 1,), I32), shape((micros * tok_rows, LANES), I32)],
+            [SMEM, SMEM, VMEM],
+            [pltpu.SMEM((micros * tok_rows,), I32)] * 2,
+        )(info, place)
+
+    other1, swapped, (hid1,), (rounds_of, own_plan, source) = one_pass(number(1), 0, own1, tie=info, beside=plan)
     table = swap(make_news(number(1), False, first, swapped), "section")
 
     sent, row_in = send(number(2), False, True, table)
@@ -498,7 +502,7 @@
         size=8 * hid * width,
     )(
         core_id, saved_u, saved_u.reshape(micros * dp_count * cap, hid).T, x_rows,
-        hid1, hid2, hid3, perm2, perm3, own1, other1, own2[..., :width], other2[..., :width], own3, other3,
+        hid1, hid2, hid3, perm2, perm3, own1, other1, own2, other2, own3, other3,
     )
     in_grad = call(
         output_kernel,

time: 185 us -> 179 us (0.968)
  blocking collectives: 52.6 us -> 73.3 us
  waiting for transfers between devices: 53.3 us -> 34.7 us
  starting transfers between devices: 41.5 us -> 34 us
    all_to_all x5 -> x4, waiting for transfers between devices: 39.6 us -> 18.6 us  [swap(): lax.all_to_all(block, axis, 0, 0, tiled=True, axis_index_groups=groups)]
    all_to_all x4 -> x5, blocking collectives: 52.6 us -> 73.3 us  [swap(): lax.all_to_all(block, axis, 0, 0, tiled=True, axis_index_groups=groups)]
    all_to_all x5 -> x4, starting transfers between devices: 28.5 us -> 21 us  [swap(): lax.all_to_all(block, axis, 0, 0, tiled=True, axis_index_groups=groups)]
    ppermute x3, waiting for transfers between devices: 3.45 us -> 6.08 us  [one_pass(): other = lax.ppermute(own, 'dp', sibling)]
    pallas_call x3, Pallas kernels: 10.1 us -> 7.9 us  [one_pass(): call(functools.partial(pass_kernel, count, late, cap), [SMEM, SMEM] + [VM...]
    unnamed x23 -> x21, local copies, waits for them, and re-layouts: 3.59 us -> 4.3 us
  transfers between devices with their start and end apart: 14 -> 13, of which waited for: 13 -> 13; matrix products, arithmetic and copies ran while one was open for 0% -> 0% of each run, Pallas kernels for 4% -> 4%
where the time goes in v4:
time: 179 us; the launch traced here: 178 us
  blocking collectives  73.3 us (41%)
  waiting for transfers between devices  34.7 us (19%)
  starting transfers between devices  34 us (19%)
  Pallas kernels  26.9 us (15%)
  local copies, waits for them, and re-layouts  4.41 us (2%)
  other arithmetic  2.95 us (2%)
    all_to_all x5, blocking collectives, swap(): lax.all_to_all(block, axis, 0, 0, tiled=True, axis_index_groups=groups)  73.3 us
    all_to_all x4, starting transfers between devices, swap(): lax.all_to_all(block, axis, 0, 0, tiled=True, axis_index_groups=groups)  21 us
    all_to_all x4, waiting for transfers between devices, swap(): lax.all_to_all(block, axis, 0, 0, tiled=True, axis_index_groups=groups)  18.6 us
    ppermute x3, starting transfers between devices, hop_along(): lax.ppermute(info, 'section', [(i, i ^ distance) for i in range(sections)])  12.4 us
    pallas_call x3, Pallas kernels, one_pass(): call(functools.partial(pass_kernel, count, late, cap), [SMEM, SMEM] + [VM...  7.9 us
    ppermute x3, waiting for transfers between devices, one_pass(): other = lax.ppermute(own, 'dp', sibling)  6.08 us
    ppermute x3, waiting for transfers between devices, one_pass(): arrived = lax.ppermute(theirs, 'dp', sibling)  5.32 us
    pallas_call x1, Pallas kernels, per_device(): call(functools.partial(grads_kernel, cap), [SMEM] + [VMEM] * 14, [shape((...  5.02 us
  transfers between devices with their start and end apart: 13, of which 13 were waited for; matrix products, arithmetic and copies ran while one was open for 0% of the time, Pallas kernels for 4%

profile of v4, /device:TPU:8, one launch (start us, length us, event | category | flops | bytes accessed | tf_op | source)
XLA Modules:
  0.0 177.8 jit_solution(5595876954834391405)
XLA Ops:
  0.6 0.7 copy.15.count_ref
  1.4 0.0 copy-start
  1.4 1.4 copy-done
  2.8 2.1 %shard_map.103 = (bf16[16,4,6144]{2,1,0:T(4,128)(2,1)}, bf16[4,6144]{1,0:T(4,128)(2,1)}, s32[1,128]{1,0:T(1,128)S(1)}) custom-call(s32[1,2,2]{2,1,0:T(2,128)} %token_ref.7, s32[1,2,1]{2,1,0:T(2,128)S(1)} %copy.15.count_ref, f32[1,2,2]{2,1,0:T(2,128)} %gate_ref.5, bf16[2,64,6144]{2,1,0:T(8,128)(2,1)S(1)} %copy-done), custom_call_target="tpu_custom_call" | custom-call | flops 1000000 | bytes 1000000 | tf_op jit(solution)/shard_map/pallas_call | solution.py:434
  4.9 7.4 %all-to-all-start.3 = ((bf16[16,4,6144]{2,1,0:T(4,128)(2,1)}), bf16[16,4,6144]{2,1,0:T(4,128)(2,1)}, u32[]{:S(2)}, u32[]{:S(2)}) async-start(bf16[16,4,6144]{2,1,0:T(4,128)(2,1)} %get-tuple-element.261), calls=%async_computation.3 | async-start | bytes 1572864 | tf_op jit(solution)/shard_map/all_to_all | solution.py:377
  12.3 1.9 %collective-permute-start.2 = (s32[1,128]{1,0:T(1,128)S(1)}, s32[1,128]{1,0:T(1,128)S(1)}, u32[]{:S(2)}, u32[]{:S(2)}) collective-permute-start(s32[1,128]{1,0:T(1,128)S(1)} %get-tuple-element.262), channel_id=1, source_target_pairs={{0,32},{32,0},{64,96},{96,64},{128,160},{160,128},{192,224},{224,1... | collective-permute-start | bytes 1544 | tf_op jit(solution)/shard_map/ppermute | solution.py:380
  14.2 1.6 collective-permute-done.2
  15.8 3.3 %collective-permute-start.3 = (s32[2,128]{1,0:T(2,128)S(1)}, s32[2,128]{1,0:T(2,128)S(1)}, u32[]{:S(2)}, u32[]{:S(2)}) collective-permute-start(s32[2,128]{1,0:T(2,128)S(1)} %pad_add_fusion.2), channel_id=1, source_target_pairs={{0,64},{32,96},{64,0},{96,32},{128,192},{160,224},{192,128},{224,1... | collective-permute-start | bytes 3080 | tf_op jit(solution)/shard_map/ppermute | solution.py:380
  19.1 1.5 collective-permute-done.3
  20.6 4.7 %all-to-all-done.3.own_ref = bf16[16,4,6144]{2,1,0:T(4,128)(2,1)} async-done(((bf16[16,4,6144]{2,1,0:T(4,128)(2,1)}), bf16[16,4,6144]{2,1,0:T(4,128)(2,1)}, u32[]{:S(2)}, u32[]{:S(2)}) %all-to-all-start.3) | async-done | bytes 786464 | tf_op jit(solution)/shard_map/all_to_all | solution.py:377
  25.4 0.0 collective-permute-start.4
  25.4 2.6 %collective-permute-done.4.other_ref = bf16[16,4,6144]{2,1,0:T(4,128)(2,1)} collective-permute-done((bf16[16,4,6144]{2,1,0:T(4,128)(2,1)}, bf16[16,4,6144]{2,1,0:T(4,128)(2,1)}, u32[]{:S(2)}, u32[]{:S(2)}) %collective-permute-start.4) | collective-permute-done | bytes 786464 | tf_op jit(solution)/shard_map/ppermute | solution.py:396
  28.0 0.0 copy-done.5
  28.0 0.0 copy-done.11
  28.0 4.0 %shard_map.104 = (f32[16,4,6144]{2,1,0:T(4,128)S(1)}, bf16[16,4,6144]{2,1,0:T(4,128)(2,1)S(1)}, bf16[128,168]{1,0:T(8,128)(2,1)}) custom-call(s32[1]{0:T(128)} %bitcast.5.core_ref, s32[1]{0:T(128)} %constant.46.clone.1.now_ref, bf16[1,2,64,168]{3,2,1,0:T(8,128)(2,1)S(1)} %copy-done.11, bf16[1,168,6144]{2,1,0:T(8,128)(2,1)S(1)} %copy-done.5, ...), custom_call_target="tpu_custom_call" | custom-call | flops 528482304 | bytes 10420224 | tf_op jit(solution)/shard_map/pallas_call | solution.py:407
  32.1 0.2 collective-permute-start.5
  32.3 2.1 %collective-permute-done.5 = bf16[16,4,6144]{2,1,0:T(4,128)(2,1)S(1)} collective-permute-done((bf16[16,4,6144]{2,1,0:T(4,128)(2,1)S(1)}, bf16[16,4,6144]{2,1,0:T(4,128)(2,1)S(1)}, u32[]{:S(2)}, u32[]{:S(2)}) %collective-permute-start.5) | collective-permute-done | bytes 786464 | tf_op jit(solution)/shard_map/ppermute | solution.py:415
  34.4 1.4 add_convert_fusion.1
  35.8 4.9 %all-to-all-start.4 = ((bf16[16,4,6144]{2,1,0:T(4,128)(2,1)}), bf16[16,4,6144]{2,1,0:T(4,128)(2,1)S(1)}, u32[]{:S(2)}, u32[]{:S(2)}) async-start(bf16[16,4,6144]{2,1,0:T(4,128)(2,1)} %add_convert_fusion.1), calls=%async_computation.4 | async-start | bytes 1572864 | tf_op jit(solution)/shard_map/all_to_all | solution.py:377
  40.7 7.2 %collective-permute-start.6 = (s32[4,128]{1,0:T(4,128)S(1)}, s32[4,128]{1,0:T(4,128)S(1)}, u32[]{:S(2)}, u32[]{:S(2)}) collective-permute-start(s32[4,128]{1,0:T(4,128)S(1)} %pad_add_fusion.1), channel_id=1, source_target_pairs={{0,128},{32,160},{64,192},{96,224},{128,0},{160,32},{192,64},{224,... | collective-permute-start | bytes 6152 | tf_op jit(solution)/shard_map/ppermute | solution.py:380
  47.9 1.6 collective-permute-done.6
  49.4 2.7 %shard_map.105 = (s32[32]{0:T(128)}, s32[5]{0:T(128)}, s32[128,128]{1,0:T(8,128)S(1)}) custom-call(s32[8,128]{1,0:T(8,128)S(1)} %pad_add_fusion.info_ref, s32[1]{0:T(128)} %bitcast.4.place_ref.round_ref), custom_call_target="tpu_custom_call" | custom-call | flops 1000000 | bytes 1000000 | tf_op jit(solution)/shard_map/pallas_call | solution.py:449
  52.1 2.5 %all-to-all-done.4.swapped_ref = bf16[16,4,6144]{2,1,0:T(4,128)(2,1)S(1)} async-done(((bf16[16,4,6144]{2,1,0:T(4,128)(2,1)}), bf16[16,4,6144]{2,1,0:T(4,128)(2,1)S(1)}, u32[]{:S(2)}, u32[]{:S(2)}) %all-to-all-start.4) | async-done | bytes 786464 | tf_op jit(solution)/shard_map/all_to_all | solution.py:377
  54.6 1.2 shard_map.106
  55.8 20.8 %all_to_all.63.table_ref = bf16[8,4,6144]{2,1,0:T(4,128)(2,1)S(1)} all-to-all(bf16[8,4,6144]{2,1,0:T(4,128)(2,1)S(1)} %shard_map.106), channel_id=1, replica_groups=mesh['section'=8,'dp'=32] {'section'}, dimensions={0} | all-to-all | bytes 786432 | tf_op jit(solution)/shard_map/all_to_all | solution.py:377
  76.6 1.1 shard_map.107
  77.7 13.7 %all_to_all.64.own_ref.own2 = bf16[16,2,6272]{2,1,0:T(2,128)(2,1)S(1)} all-to-all(bf16[16,2,6272]{2,1,0:T(2,128)(2,1)S(1)} %get-tuple-element.277), channel_id=1, replica_groups={{0,2,4,6,8,10,12,14,16,18,20,22,24,26,28,30},{1,3,5,7,9,11,13,15,17,19,..., dimensions={0} | all-to-all | bytes 802816 | tf_op jit(solution)/shard_map/all_to_all | solution.py:377
  91.4 0.0 collective-permute-start.7
  91.4 1.7 collective-permute-done.7.other_ref.other2
  93.1 0.0 copy-done.8
  93.1 2.2 %shard_map.108 = (f32[16,2,6144]{2,1,0:T(2,128)S(1)}, bf16[16,2,6144]{2,1,0:T(2,128)(2,1)S(1)}, bf16[64,168]{1,0:T(8,128)(2,1)S(1)}, bf16[64,128]{1,0:T(8,128)(2...) custom-call(s32[1]{0:T(128)} %bitcast.5.core_ref, s32[1]{0:T(128)} %constant.47.clone.1.now_ref, ...), custom_call_target="tpu_custom_call" | custom-call | flops 264241152 | bytes 7274496 | tf_op jit(solution)/shard_map/pallas_call | solution.py:407
  95.3 0.2 collective-permute-start.8
  95.5 1.6 collective-permute-done.8
  97.1 0.4 add_convert_fusion.3
  97.5 0.0 copy-start.6
  97.5 13.8 %all_to_all.65.swapped_ref = bf16[16,2,6144]{2,1,0:T(2,128)(2,1)S(1)} all-to-all(bf16[16,2,6144]{2,1,0:T(2,128)(2,1)S(1)} %add_convert_fusion.3), channel_id=1, replica_groups={{0,2,4,6,8,10,12,14,16,18,20,22,24,26,28,30},{1,3,5,7,9,11,13,15,17,19,..., dimensions={0} | all-to-all | bytes 786432 | tf_op jit(solution)/shard_map/all_to_all | solution.py:377
  111.3 0.8 shard_map.109
  112.2 12.5 %all_to_all.66.refs_0_ = bf16[8,2,6144]{2,1,0:T(2,128)(2,1)S(1)} all-to-all(bf16[8,2,6144]{2,1,0:T(2,128)(2,1)S(1)} %shard_map.109), channel_id=1, replica_groups=mesh['section'=8,'dp'=32] {'section'}, dimensions={0} | all-to-all | bytes 393216 | tf_op jit(solution)/shard_map/all_to_all | solution.py:377
  124.7 1.4 shard_map.110
  126.1 12.4 %all_to_all.67.own_ref.own3 = bf16[16,2,6144]{2,1,0:T(2,128)(2,1)S(1)} all-to-all(bf16[16,2,6144]{2,1,0:T(2,128)(2,1)S(1)} %get-tuple-element.281), channel_id=1, replica_groups={{0,2,4,6,8,10,12,14,16,18,20,22,24,26,28,30},{1,3,5,7,9,11,13,15,17,19,..., dimensions={0} | all-to-all | bytes 786432 | tf_op jit(solution)/shard_map/all_to_all | solution.py:377
  138.5 0.0 collective-permute-start.9
  138.5 1.7 collective-permute-done.9.other_ref.other3
  140.2 0.0 copy-done.6
  140.2 1.7 shard_map.111
  141.9 0.0 copy-start.3
  141.9 0.2 collective-permute-start.10
  142.2 1.6 collective-permute-done.10
  143.7 1.2 add_convert_fusion.2
  144.9 5.3 %all-to-all-start.10 = ((bf16[16,2,6144]{2,1,0:T(2,128)(2,1)}), bf16[16,2,6144]{2,1,0:T(2,128)(2,1)S(1)}, u32[]{:S(2)}, u32[]{:S(2)}) async-start(bf16[16,2,6144]{2,1,0:T(2,128)(2,1)} %add_convert_fusion.2), calls=%async_computation.10 | async-start | bytes 786432 | tf_op jit(solution)/shard_map/all_to_all | solution.py:377
  150.2 8.6 %all-to-all-done.10.swapped_ref = bf16[16,2,6144]{2,1,0:T(2,128)(2,1)S(1)} async-done(((bf16[16,2,6144]{2,1,0:T(2,128)(2,1)}), bf16[16,2,6144]{2,1,0:T(2,128)(2,1)S(1)}, u32[]{:S(2)}, u32[]{:S(2)}) %all-to-all-start.10) | async-done | bytes 393248 | tf_op jit(solution)/shard_map/all_to_all | solution.py:377
  158.8 1.5 shard_map.112
  160.3 0.0 copy-done.3
  160.3 0.6 while.20
  161.0 0.0 copy-start.10
  161.0 3.4 %all-to-all-start.11 = ((bf16[8,2,6144]{2,1,0:T(2,128)(2,1)}), bf16[8,2,6144]{2,1,0:T(2,128)(2,1)S(1)}, u32[]{:S(2)}, u32[]{:S(2)}) async-start(bf16[8,2,6144]{2,1,0:T(2,128)(2,1)} %get-tuple-element.291), calls=%async_computation.11 | async-start | bytes 393216 | tf_op jit(solution)/shard_map/all_to_all | solution.py:377
  164.4 0.1 copy.16
  164.5 0.0 copy-done.10
  164.5 0.0 copy-start.2
  164.5 1.4 copy-done.2
  165.9 0.7 copy-done.4
  166.7 5.0 %shard_map.114 = (bf16[1,168,6144]{2,1,0:T(8,128)(2,1)}, bf16[1,168,6144]{2,1,0:T(8,128)(2,1)}) custom-call(s32[1]{0:T(128)} %bitcast.5.core_ref, bf16[1,2,64,168]{3,2,1,0:T(8,128)(2,1)} %saved_ref.7, bf16[168,128]{1,0:T(8,128)(2,1)S(1)} %bitcast.36, bf16[1,2,64,6144]{3,2,1,0:T(8,128)(2,1)S(1)} %copy-done.2, bf16[128,168]{1,0:T(8,128)(2,1)} %get-tuple-element.292.hid1, ...), custom_call_target="tpu_custom_call" | custom-call | flops 1056964608 | bytes 8257536 | tf_op jit(solution)/shard_map/pallas_call | solution.py:496
  171.7 2.8 %all-to-all-done.11.news_ref = bf16[8,2,6144]{2,1,0:T(2,128)(2,1)S(1)} async-done(((bf16[8,2,6144]{2,1,0:T(2,128)(2,1)}), bf16[8,2,6144]{2,1,0:T(2,128)(2,1)S(1)}, u32[]{:S(2)}, u32[]{:S(2)}) %all-to-all-start.11) | async-done | bytes 196640 | tf_op jit(solution)/shard_map/all_to_all | solution.py:377
  174.5 0.0 copy-done.1
  174.5 3.3 %shard_map.113 = bf16[1,2,64,6144]{3,2,1,0:T(8,128)(2,1)} custom-call(s32[1]{0:T(128)} %bitcast.6.last_ref, s32[32]{0:T(128)} %get-tuple-element.521.round_ref, s32[128,128]{1,0:T(8,128)S(1)} %get-tuple-element.289.source_ref, bf16[2,64,6144]{2,1,0:T(8,128)(2,1)S(1)} %copy-done.1, bf16[8,4,6144]{2,1,0:T(4,128)(2,1)} %copy-done.10, ...), custom_call_target="tpu_custom_call" | custom-call | flops 1000000 | bytes 1000000 | tf_op jit(solution)/shard_map/pallas_call | solution.py:507
  (8 shorter events, 0.0 us)
Async XLA Ops:
  1.4 1.4 copy-start
  2.8 25.2 %copy-start.5 = (bf16[1,168,6144]{2,1,0:T(8,128)(2,1)S(1)}, bf16[1,168,6144]{2,1,0:T(8,128)(2,1)}, u32[]{:S(2)}) copy-start(bf16[1,168,6144]{2,1,0:T(8,128)(2,1)} %down_ref.5) | copy-start | bytes 6193156
  2.8 25.2 %copy-start.11 = (bf16[1,2,64,168]{3,2,1,0:T(8,128)(2,1)S(1)}, bf16[1,2,64,168]{3,2,1,0:T(8,128)(2,1)}, u32[]{:S(2)}) copy-start(bf16[1,2,64,168]{3,2,1,0:T(8,128)(2,1)} %saved_ref.7) | copy-start | bytes 129028
  4.9 20.5 %all-to-all-start.3 = ((bf16[16,4,6144]{2,1,0:T(4,128)(2,1)}), bf16[16,4,6144]{2,1,0:T(4,128)(2,1)}, u32[]{:S(2)}, u32[]{:S(2)}) async-start(bf16[16,4,6144]{2,1,0:T(4,128)(2,1)} %get-tuple-element.261), calls=%async_computation.3 | async-start | bytes 1572864 | tf_op jit(solution)/shard_map/all_to_all | solution.py:377
  12.3 3.5 %collective-permute-start.2 = (s32[1,128]{1,0:T(1,128)S(1)}, s32[1,128]{1,0:T(1,128)S(1)}, u32[]{:S(2)}, u32[]{:S(2)}) collective-permute-start(s32[1,128]{1,0:T(1,128)S(1)} %get-tuple-element.262), channel_id=1, source_target_pairs={{0,32},{32,0},{64,96},{96,64},{128,160},{160,128},{192,224},{224,1... | collective-permute-start | bytes 1544 | tf_op jit(solution)/shard_map/ppermute | solution.py:380
  15.8 4.8 %collective-permute-start.3 = (s32[2,128]{1,0:T(2,128)S(1)}, s32[2,128]{1,0:T(2,128)S(1)}, u32[]{:S(2)}, u32[]{:S(2)}) collective-permute-start(s32[2,128]{1,0:T(2,128)S(1)} %pad_add_fusion.2), channel_id=1, source_target_pairs={{0,64},{32,96},{64,0},{96,32},{128,192},{160,224},{192,128},{224,1... | collective-permute-start | bytes 3080 | tf_op jit(solution)/shard_map/ppermute | solution.py:380
  25.4 2.6 %collective-permute-start.4 = (bf16[16,4,6144]{2,1,0:T(4,128)(2,1)}, bf16[16,4,6144]{2,1,0:T(4,128)(2,1)}, u32[]{:S(2)}, u32[]{:S(2)}) collective-permute-start(bf16[16,4,6144]{2,1,0:T(4,128)(2,1)} %all-to-all-done.3.own_ref), channel_id=1, source_target_pairs={{0,1},{1,0},{2,3},{3,2},{4,5},{5,4},{6,7},{7,6},{8,9},{9,8},{10,11... | collective-permute-start | bytes 2359304 | tf_op jit(solution)/shard_map/ppermute | solution.py:396
  32.1 2.4 %collective-permute-start.5 = (bf16[16,4,6144]{2,1,0:T(4,128)(2,1)S(1)}, bf16[16,4,6144]{2,1,0:T(4,128)(2,1)S(1)}, u32[]{:S(2)}, u32[]{:S(2)}) collective-permute-start(bf16[16,4,6144]{2,1,0:T(4,128)(2,1)S(1)} %get-tuple-element.265), channel_id=1, source_target_pairs={{0,1},{1,0},{2,3},{3,2},{4,5},{5,4},{6,7},{7,6},{8,9},{9,8},{10,11... | collective-permute-start | bytes 2359304 | tf_op jit(solution)/shard_map/ppermute | solution.py:415
  35.8 18.8 %all-to-all-start.4 = ((bf16[16,4,6144]{2,1,0:T(4,128)(2,1)}), bf16[16,4,6144]{2,1,0:T(4,128)(2,1)S(1)}, u32[]{:S(2)}, u32[]{:S(2)}) async-start(bf16[16,4,6144]{2,1,0:T(4,128)(2,1)} %add_convert_fusion.1), calls=%async_computation.4 | async-start | bytes 1572864 | tf_op jit(solution)/shard_map/all_to_all | solution.py:377
  40.7 8.8 %collective-permute-start.6 = (s32[4,128]{1,0:T(4,128)S(1)}, s32[4,128]{1,0:T(4,128)S(1)}, u32[]{:S(2)}, u32[]{:S(2)}) collective-permute-start(s32[4,128]{1,0:T(4,128)S(1)} %pad_add_fusion.1), channel_id=1, source_target_pairs={{0,128},{32,160},{64,192},{96,224},{128,0},{160,32},{192,64},{224,... | collective-permute-start | bytes 6152 | tf_op jit(solution)/shard_map/ppermute | solution.py:380
  54.6 38.6 %copy-start.8 = (bf16[1,168,6144]{2,1,0:T(8,128)(2,1)S(1)}, bf16[1,168,6144]{2,1,0:T(8,128)(2,1)}, u32[]{:S(2)}) copy-start(bf16[1,168,6144]{2,1,0:T(8,128)(2,1)} %up_ref.5) | copy-start | bytes 6193156
  91.4 1.7 collective-permute-start.7
  95.3 1.8 %collective-permute-start.8 = (bf16[16,2,6144]{2,1,0:T(2,128)(2,1)S(1)}, bf16[16,2,6144]{2,1,0:T(2,128)(2,1)S(1)}, u32[]{:S(2)}, u32[]{:S(2)}) collective-permute-start(bf16[16,2,6144]{2,1,0:T(2,128)(2,1)S(1)} %get-tuple-element.279), channel_id=1, source_target_pairs={{0,1},{1,0},{2,3},{3,2},{4,5},{5,4},{6,7},{7,6},{8,9},{9,8},{10,11... | collective-permute-start | bytes 1179656 | tf_op jit(solution)/shard_map/ppermute | solution.py:415
  97.5 42.7 %copy-start.6 = (bf16[1,168,6144]{2,1,0:T(8,128)(2,1)S(1)}, bf16[1,168,6144]{2,1,0:T(8,128)(2,1)}, u32[]{:S(2)}) copy-start(bf16[1,168,6144]{2,1,0:T(8,128)(2,1)} %down_ref.5) | copy-start | bytes 6193156
  138.5 1.7 collective-permute-start.9
  141.9 18.4 %copy-start.3 = (bf16[64,128]{1,0:T(8,128)(2,1)}, bf16[64,128]{1,0:T(8,128)(2,1)S(1)}, u32[]{:S(2)}) copy-start(bf16[64,128]{1,0:T(8,128)(2,1)S(1)} %get-tuple-element.296.perm3) | copy-start | bytes 49156
  141.9 1.8 %collective-permute-start.10 = (bf16[16,2,6144]{2,1,0:T(2,128)(2,1)S(1)}, bf16[16,2,6144]{2,1,0:T(2,128)(2,1)S(1)}, u32[]{:S(2)}, u32[]{:S(2)}) collective-permute-start(bf16[16,2,6144]{2,1,0:T(2,128)(2,1)S(1)} %get-tuple-element.284), channel_id=1, source_target_pairs={{0,1},{1,0},{2,3},{3,2},{4,5},{5,4},{6,7},{7,6},{8,9},{9,8},{10,11... | collective-permute-start | bytes 1179656 | tf_op jit(solution)/shard_map/ppermute | solution.py:415
  144.9 13.9 %all-to-all-start.10 = ((bf16[16,2,6144]{2,1,0:T(2,128)(2,1)}), bf16[16,2,6144]{2,1,0:T(2,128)(2,1)S(1)}, u32[]{:S(2)}, u32[]{:S(2)}) async-start(bf16[16,2,6144]{2,1,0:T(2,128)(2,1)} %add_convert_fusion.2), calls=%async_computation.10 | async-start | bytes 786432 | tf_op jit(solution)/shard_map/all_to_all | solution.py:377
  161.0 3.5 %copy-start.10 = (bf16[8,4,6144]{2,1,0:T(4,128)(2,1)}, bf16[8,4,6144]{2,1,0:T(4,128)(2,1)S(1)}, u32[]{:S(2)}) copy-start(bf16[8,4,6144]{2,1,0:T(4,128)(2,1)S(1)} %get-tuple-element.290.table_ref) | copy-start | bytes 1179652
  161.0 13.5 %all-to-all-start.11 = ((bf16[8,2,6144]{2,1,0:T(2,128)(2,1)}), bf16[8,2,6144]{2,1,0:T(2,128)(2,1)S(1)}, u32[]{:S(2)}, u32[]{:S(2)}) async-start(bf16[8,2,6144]{2,1,0:T(2,128)(2,1)} %get-tuple-element.291), calls=%async_computation.11 | async-start | bytes 393216 | tf_op jit(solution)/shard_map/all_to_all | solution.py:377
  164.5 1.4 copy-start.2
  165.9 0.7 copy-start.4
  166.6 7.9 %copy-start.1 = (bf16[2,64,6144]{2,1,0:T(8,128)(2,1)S(1)}, bf16[2,64,6144]{2,1,0:T(8,128)(2,1)}, u32[]{:S(2)}) copy-start(bf16[2,64,6144]{2,1,0:T(8,128)(2,1)} %grad_ref.3) | copy-start | bytes 4718596

commit v5 on v0

v5 whole, which is shorter than its diff:
```python
import functools

import jax
import jax.numpy as jnp
from jax import lax
from jax.experimental import pallas as pl
from jax.experimental.pallas import tpu as pltpu
from jax.sharding import PartitionSpec as P

BF = jnp.bfloat16
F32 = jnp.float32
I32 = jnp.int32
LANES = 128
ROOM = 2
UNROLLED = 3
NT = (((1,), (1,)), ((), ()))
TN = (((0,), (0,)), ((), ()))
SMEM = pl.BlockSpec(memory_space=pltpu.SMEM)
VMEM = pl.BlockSpec(memory_space=pltpu.VMEM)
ANY = pl.BlockSpec(memory_space=pl.ANY)


def call(kernel, ins, outs, out_specs, scratch=(), flops=1000000, size=1000000):
    return pl.pallas_call(
        kernel,
        in_specs=ins,
        out_specs=out_specs,
        out_shape=outs,
        scratch_shapes=list(scratch),
        compiler_params=pltpu.CompilerParams(vmem_limit_bytes=24 * 1024 * 1024),
        cost_estimate=pl.CostEstimate(flops=flops, bytes_accessed=size, transcendentals=0),
    )


def chunks(width):
    step = next(s for s in (1024, 768, 512, 384, 256, 128) if width % s == 0)
    return [pl.ds(at, step) for at in range(0, width, step)]


def dot(a, b, dims=None):
    if dims is None:
        return jnp.dot(a, b, preferred_element_type=F32)
    return lax.dot_general(a, b, dims, preferred_element_type=F32)


def iota(shape, axis):
    return lax.broadcasted_iota(I32, shape, axis)


def one_hot(flag):
    return jnp.where(flag, 1.0, 0.0).astype(BF)


def column(values, shape):
    rows = iota(shape, 0)
    out = jnp.full(shape, values[0])
    for i in range(1, len(values)):
        out = jnp.where(rows == i, values[i], out)
    return out


def info_kernel(token_ref, count_ref, info_ref):
    micros, cap = token_ref.shape[1:]
    slots = micros * cap
    lane = iota((1, LANES), 1)
    info = jnp.zeros((1, LANES), I32)
    for i in range(slots):
        live = jnp.where(i % cap < count_ref[0, 0, i // cap], 1, 0)
        info = jnp.where(lane == i, token_ref[0, i // cap, i % cap], info)
        info = jnp.where(lane == slots + i, live, info)
    for section in range(info_ref.shape[0]):
        info_ref[section] = info


def first_kernel(token_ref, grad_ref, first_ref):
    micros, tok_rows, width = grad_ref.shape
    cap = token_ref.shape[2]
    slots = micros * cap
    tokens = [token_ref[0, i // cap, i % cap] + (i // cap) * tok_rows for i in range(slots)]
    wanted = column(tokens, (8, micros * tok_rows))
    pick = one_hot(wanted == iota(wanted.shape, 1))
    for part in chunks(width):
        rows = dot(pick, grad_ref[:, :, part].reshape(micros * tok_rows, part.size))
        first_ref[:, part] = rows[:slots].astype(BF)


def plan_kernel(sections, cap, tok_rows, info_ref, place_ref, round_ref, own_ref, source_ref, round2_ref, own2_ref, ready_ref, last_ref, below_ref, height_ref):
    slots = 2 * cap
    place = place_ref[0]

    def routed(layer):
        token = [info_ref[layer, 0, i] + (i // cap) * tok_rows for i in range(slots)]
        live = [info_ref[layer, 0, slots + i] for i in range(slots)]
        return token, live

    def mates(i):
        return [k for k in range(i // cap * cap, i // cap * cap + cap) if k != i]

    def clear(layer, carry):
        for token in routed(layer)[0]:
            ready_ref[token] = 1
            last_ref[token] = -1
            below_ref[token] = 0
        return carry

    def climb(layer, carry):
        token, live = routed(layer)
        for i in range(slots):
            height_ref[layer * slots + i] = below_ref[token[i]]
        for i in range(slots):
            new = live[i]
            for k in mates(i):
                if k < i:
                    new = jnp.where((token[k] == token[i]) & (live[k] > 0), 0, new)
            below_ref[token[i]] = below_ref[token[i]] + new
        return carry

    def descend(step, most):
        layer = sections - 1 - step
        token, live = routed(layer)
        own = layer == place
        for i in range(slots):
            own_ref[i] = jnp.where(own, last_ref[token[i]], own_ref[i])
        height = [height_ref[layer * slots + i] for i in range(slots)]
        ready = [ready_ref[token[i]] for i in range(slots)]
        twin = [
            [(k, (token[k] == token[i]) & (live[k] > 0)) for k in mates(i)] for i in range(slots)
        ]
        given = [jnp.int32(0)] * slots
        for awaited in (True, False):
            for i in range(slots):
                wanted = (height[i] > 0) if awaited else (height[i] == 0)
                wanted = wanted & (live[i] > 0) & (given[i] == 0)
                size = jnp.int32(1)
                for _, same in twin[i]:
                    size = size + jnp.where(same, 1, 0)
                when = ready[i]
                for _ in range(slots - ROOM):
                    taken = jnp.int32(0)
                    for k in range(slots):
                        taken = taken + jnp.where(given[k] == when, 1, 0)
                    when = when + jnp.where(taken + size > ROOM, 1, 0)
                for k, same in twin[i]:
                    given[k] = jnp.where(wanted & same, when, given[k])
                given[i] = jnp.where(wanted, when, given[i])
        source = source_ref[...]
        lane = iota(source.shape, 1)
        for i in range(slots):
            here = layer * slots + i
            round_ref[here] = given[i]
            round2_ref[here] = given[i]
            most = jnp.maximum(most, given[i])
            ready_ref[token[i]] = jnp.where(live[i] > 0, given[i] + 1, ready_ref[token[i]])
            last_ref[token[i]] = jnp.where(live[i] > 0, here, last_ref[token[i]])
            source = jnp.where((lane == token[i]) & ((live[i] > 0) & (layer >= place)), here, source)
        source_ref[...] = source
        return most

    for i in range(slots):
        own_ref[i] = -1
    source_ref[...] = jnp.full(source_ref.shape, -1, I32)
    lax.fori_loop(0, sections, clear, 0)
    lax.fori_loop(0, sections, climb, 0)
    own_ref[slots] = lax.fori_loop(0, sections, descend, jnp.int32(1))
    for i in range(slots + 1):
        own2_ref[i] = own_ref[i]


def row_map(round_ref, sections, slots, start, news, table=False):
    block = sections * ROOM
    found = []
    for layer in range(sections):
        ranks = [jnp.int32(0)] * news
        for i in range(slots):
            k = layer * slots + i
            at = jnp.int32(start + news * block + k if table else -1)
            for b in range(news):
                hit = round_ref[k] == b + 1
                at = jnp.where(hit, start + b * block + layer * ROOM + ranks[b], at)
                ranks[b] = ranks[b] + jnp.where(hit, 1, 0)
            found.append(at)
    return found


def own_picks(round_ref, place, slots, now):
    picks = [jnp.int32(-1)] * ROOM
    rank = jnp.int32(0)
    for i in range(slots):
        hit = round_ref[place * slots + i] == now
        for c in range(ROOM):
            picks[c] = jnp.where(hit & (rank == c), i, picks[c])
        rank = rank + jnp.where(hit, 1, 0)
    return picks


def stacked(refs, part):
    rows = [r[:, :, part].reshape(r.shape[0] * r.shape[1], part.size) for r in refs]
    return jnp.concatenate(rows) if len(rows) > 1 else rows[0]


def send_kernel(sections, news, table, note, now_ref, place_ref, round_ref, own_ref, gate_ref, first_ref, *refs):
    held = refs[: news + table]
    sent_ref, row_in_ref, map_ref = refs[news + table :]
    cap = gate_ref.shape[2]
    slots, width = first_ref.shape
    now, place = now_ref[0], place_ref[0]
    for k, at in enumerate(row_map(round_ref, sections, slots, 0, news, table)):
        map_ref[k] = at
    wanted, from_first, weights = [], [], []
    for slot in own_picks(round_ref, place, slots, now):
        at = jnp.maximum(slot, 0)
        source = own_ref[at]
        wanted.append(jnp.where((slot >= 0) & (source >= 0), map_ref[jnp.maximum(source, 0)], -1))
        from_first.append(jnp.where((slot >= 0) & (source < 0), slot, -1))
        weights.append(jnp.where(slot >= 0, gate_ref[0, at // cap, at % cap], 0.0))
    weight = column(weights, (8, LANES))[:, :1]
    first_id = column(from_first, (8, LANES))
    in_first = [jnp.where(first_id == i, 1.0, 0.0)[:, :1] for i in range(slots)]
    if held:
        total = sum(r.shape[0] * r.shape[1] for r in held)
        ids = column(wanted, (8, total))
        pick = one_hot(ids == iota(ids.shape, 1))
    for part in chunks(width):
        first = first_ref[:, part].astype(F32)
        rows = dot(pick, stacked(held, part)) if held else jnp.zeros((8, part.size), F32)
        for i in range(slots):
            rows = rows + in_first[i] * first[i : i + 1]
        row_in_ref[:, part] = rows[:ROOM]
        scaled = (weight * rows)[:ROOM].astype(BF)
        for chip in range(sent_ref.shape[0]):
            sent_ref[chip, :, part] = scaled
    if note:
        lane = iota((ROOM, LANES), 1)
        word = jnp.zeros((ROOM, LANES), I32)
        for i in range(slots):
            word = jnp.where(lane == i, round_ref[place * slots + i], word)
        word = jnp.where(lane == slots, own_ref[slots], word).astype(F32).astype(BF)
        for chip in range(sent_ref.shape[0]):
            sent_ref[chip, :, pl.ds(width, LANES)] = word


def merge_kernel(now_ref, round_ref, table_ref, news_ref, merged_ref):
    sections, slots, width = table_ref.shape
    known, total = sections * slots, sections * (slots + ROOM)
    where_is = []
    for layer in range(sections):
        rank = jnp.int32(0)
        for i in range(slots):
            hit = round_ref[layer * slots + i] == now_ref[0]
            where_is.append(jnp.where(hit, known + layer * ROOM + rank, layer * slots + i))
            rank = rank + jnp.where(hit, 1, 0)
    pick = one_hot(column(where_is, (known, total)) == iota((known, total), 1))
    for part in chunks(width):
        rows = dot(pick, stacked([table_ref, news_ref], part))
        merged_ref[:, :, part] = rows.astype(BF).reshape(sections, slots, part.size)


def places(count, chips, cap, tok_group, core, taken):
    total = 2 * chips * count
    row = iota((total, LANES), 0)
    half = row // (chips * count)
    index = (row // count) % chips * 2 + (core ^ half)
    place = jnp.full((total, LANES), -1, I32)
    for i, flag in enumerate(taken):
        place = jnp.where(flag, (i // cap) * tok_group + index * cap + i % cap, place)
    return place


def pass_kernel(count, late, cap, core_ref, now_ref, saved_ref, down_ref, up_ref, own_ref, other_ref, *refs):
    refs = list(refs)
    note_in = refs.pop(0) if late == 2 else None
    mine_ref, theirs_ref, hidden_ref = refs[:3]
    chips = own_ref.shape[0]
    micros, group, hid = saved_ref.shape[1:]
    width = mine_ref.shape[2]
    half = chips * count
    core = core_ref[0]
    if late == 1:
        perm_ref, note_ref, later_ref, most_ref = refs[3:]
        lanes = pl.ds(width, LANES)
        word = jnp.concatenate([r[:, :, lanes].reshape(half, LANES) for r in (own_ref, other_ref)]).astype(F32)
        note_ref[...] = word
        later_ref[...] = word
        most_ref[0] = jnp.max(word).astype(I32)
    else:
        (perm_ref,) = refs[3:]
        word = note_in[...]
    now = now_ref[0].astype(F32)
    position = (iota((2 * half, 1), 0) % count).astype(F32)
    rank = jnp.zeros((2 * half, 1), F32)
    taken = []
    for i in range(micros * cap):
        hit = jnp.where(word[:, i : i + 1] == now, 1.0, 0.0)
        flag = jnp.where(rank == position, hit, 0.0)
        taken.append(jnp.broadcast_to(flag, (2 * half, LANES)) > 0.5)
        rank = rank + hit
    place = places(count, chips, cap, group, core, taken)
    perm = one_hot(place == iota(place.shape, 1))
    perm_ref[...] = perm
    v = dot(perm, saved_ref[0].reshape(micros * group, hid))
    s = 1.0 / (1.0 + jnp.exp(-v))
    slope = s * (1.0 + v * (1.0 - s))
    back = jnp.zeros((2 * half, hid), F32)
    for part in chunks(width):
        rows = jnp.concatenate(
            [own_ref[:, :, part].reshape(half, part.size), other_ref[:, :, part].reshape(half, part.size)]
        )
        back = back + dot(rows, down_ref[0, :, part], NT)
    hidden = (back * slope).astype(BF)
    hidden_ref[...] = hidden
    for part in chunks(width):
        partial = dot(hidden, up_ref[0, :, part])
        mine_ref[:, :, part] = partial[:half].reshape(chips, count, part.size)
        theirs_ref[:, :, part] = partial[half:].astype(BF).reshape(chips, count, part.size)


def news_kernel(now_ref, place_ref, round_ref, token_ref, row_in_ref, swapped_ref, news_ref):
    chips, count, width = swapped_ref.shape
    micros, cap = token_ref.shape[1:]
    ids = own_picks(round_ref, place_ref[0], micros * cap, now_ref[0])
    micro, token = [], []
    for c, slot in enumerate(ids):
        at = jnp.maximum(slot, 0)
        micro.append(jnp.where(slot >= 0, at // cap, -1 - c))
        token.append(token_ref[0, at // cap, at % cap])
    twins = []
    for b in range(count):
        same = [
            jnp.where((micro[a] == micro[b]) & (token[a] == token[b]), 1.0, 0.0) if a != b else jnp.float32(0.0)
            for a in range(count)
        ]
        twins.append(column(same, (count, LANES))[:, :1])
    for part in chunks(width):
        own = swapped_ref[0, :, part].astype(F32)
        for chip in range(1, chips):
            own = own + swapped_ref[chip, :, part].astype(F32)
        total = own
        for b in range(count):
            total = total + twins[b] * own[b : b + 1]
        rows = (row_in_ref[:, part] + total).astype(BF)
        for section in range(news_ref.shape[0]):
            news_ref[section, :, part] = rows


def grads_kernel(rounds, saved_t_ref, x_any, *refs):
    up_any, down_any, x_ref, up_ref, down_ref, sems = refs[-6:]
    hids, perms, owns, others = (refs[i : 4 * rounds : 4] for i in range(4))
    so_far = refs[4 * rounds : -6]
    natural = saved_t_ref.shape[1]
    width = x_ref.shape[2]
    parts = chunks(width)
    arriving = [
        pltpu.make_async_copy(x_any.at[0, :, :, part], x_ref.at[:, :, part], sems.at[n]) for n, part in enumerate(parts)
    ]
    for copy in arriving:
        copy.start()
    perm = jnp.concatenate([p[...] for p in perms])
    v = saved_t_ref[...].astype(F32)
    act = (v * (1.0 / (1.0 + jnp.exp(-v)))).astype(BF)
    act_rows = dot(act, perm, NT).astype(BF)
    hidden_t = dot(jnp.concatenate([h[...] for h in hids]), perm, TN).astype(BF)
    held = [r for pair in zip(owns, others) for r in pair]
    leaving = []
    for n, part in enumerate(parts):
        down = dot(act_rows, stacked(held, part))
        arriving[n].wait()
        up = dot(hidden_t, x_ref[:, :, part].reshape(natural, part.size))
        if so_far:
            up = up + so_far[0][0, :, part].astype(F32)
            down = down + so_far[1][0, :, part].astype(F32)
        down_ref[:, part] = down.astype(BF)
        up_ref[:, part] = up.astype(BF)
        for i, (a, b) in enumerate(((up_ref, up_any), (down_ref, down_any))):
            at = len(parts) * (1 + i) + n
            leaving.append(pltpu.make_async_copy(a.at[:, part], b.at[0, :, part], sems.at[at]))
            leaving[-1].start()
    for copy in leaving:
        copy.wait()


def output_kernel(round_ref, source_ref, grad_ref, *refs):
    held = [grad_ref, *refs[: UNROLLED + 1]]
    out_any, out_ref, sems = refs[UNROLLED + 1 :]
    sections, slots, width = held[-1].shape
    micros, tok_rows, _ = grad_ref.shape
    natural = micros * tok_rows
    source = source_ref[...]
    at = iota(source.shape, 1)
    for k, where_is in enumerate(row_map(round_ref, sections, slots, natural, UNROLLED, True)):
        at = jnp.where(source == k, where_is, at)
    total = sum(r.shape[0] * r.shape[1] for r in held)
    pick = one_hot(iota((total, natural), 0) == at)
    copies = []
    for n, part in enumerate(chunks(width)):
        out_ref[:, :, part] = dot(pick, stacked(held, part), TN).astype(BF).reshape(micros, tok_rows, part.size)
        copies.append(pltpu.make_async_copy(out_ref.at[:, :, part], out_any.at[0, :, :, part], sems.at[n]))
        copies[n].start()
    for copy in copies:
        copy.wait()


def per_device(out_grad, x_rows, saved_u, w_up_t, w_down, gate, route_tokens, route_count):
    sections = lax.axis_size("section")
    dp_count = lax.axis_size("dp")
    section_index = lax.axis_index("section")
    core = lax.axis_index("dp") % 2
    micros, tok_rows, width = out_grad.shape
    cap = gate.shape[2]
    hid = w_down.shape[1]
    chips = dp_count // 2
    slots = micros * cap
    same_core = [[2 * chip + c for chip in range(chips)] for c in range(2)]
    sibling = [(i, i ^ 1) for i in range(dp_count)]
    place = section_index.reshape(1).astype(I32)
    core_id = core.reshape(1).astype(I32)

    def shape(dims, dtype):
        return jax.ShapeDtypeStruct(dims, dtype)

    def swap(block, axis, groups=None):
        return lax.all_to_all(block, axis, 0, 0, tiled=True, axis_index_groups=groups)

    def number(n):
        return jnp.full((1,), n, I32)

    def in_vmem(block):
        return pltpu.with_memory_space_constraint(block, pltpu.VMEM)

    def send(now, note, rounds_of, own_plan, *held):
        news = min(len(held), UNROLLED)
        return call(
            functools.partial(send_kernel, sections, news, len(held) - news, note),
            [SMEM] * 5 + [VMEM] * (1 + len(held)),
            [shape((chips, ROOM, width + LANES * note), BF), shape((ROOM, width), F32)],
            [VMEM] * 2,
            [pltpu.SMEM((sections * slots,), I32)],
        )(now, place, rounds_of, own_plan, gate, first, *held)

    def one_pass(now, late, own, note=None):
        other = lax.ppermute(own, "dp", sibling)
        total = 2 * chips * ROOM
        outs = [shape((chips, ROOM, width), F32), shape((chips, ROOM, width), BF), shape((total, hid), BF)]
        outs.append(shape((total, LANES), BF))
        outs += [shape((total, LANES), F32)] * 2 + [shape((1,), I32)] if late == 1 else []
        mine, theirs, hidden, perm, *rest = call(
            functools.partial(pass_kernel, ROOM, late, cap),
            [SMEM, SMEM] + [VMEM] * (5 + (late == 2)),
            outs,
            [VMEM] * 4 + ([VMEM, VMEM, SMEM] if late == 1 else []),
            flops=4 * total * hid * width,
            size=4 * hid * width + 8 * total * width,
        )(core_id, now, saved_here, w_down, w_up_t, own, other, *([note] if late == 2 else []))
        arrived = lax.ppermute(theirs, "dp", sibling)
        pair_sum = (mine + arrived.astype(F32)).astype(BF)
        return swap(pair_sum, "dp", same_core), [hidden, perm, own, other], rest

    def make_news(now, rounds_of, row_in, swapped):
        return call(
            news_kernel,
            [SMEM] * 4 + [VMEM] * 2,
            shape((sections,) + swapped.shape[1:], BF),
            VMEM,
        )(now, place, rounds_of, route_tokens, row_in, swapped)

    def gradients(kept, so_far=()):
        return call(
            functools.partial(grads_kernel, len(kept)),
            [VMEM, ANY] + [VMEM] * (4 * len(kept) + len(so_far)),
            [shape((1, hid, width), BF)] * 2,
            [ANY] * 2,
            [pltpu.VMEM(x_rows.shape[1:], BF)]
            + [pltpu.VMEM((hid, width), BF)] * 2
            + [pltpu.SemaphoreType.DMA((3 * len(chunks(width)),))],
            flops=8 * dp_count * slots * hid * width,
            size=8 * hid * width,
        )(saved_t, pltpu.with_memory_space_constraint(x_rows, pltpu.HBM), *[a for one in kept for a in one], *so_far)

    info = call(info_kernel, [SMEM] * 2, shape((sections, 1, LANES), I32), VMEM)(
        route_tokens, route_count.transpose(0, 2, 1)
    )
    first = call(first_kernel, [SMEM, VMEM], shape((slots, width), BF), VMEM)(route_tokens, out_grad)
    info, first = lax.optimization_barrier((swap(info, "section"), first))
    rounds_of, own_plan, source, *again_plan = call(
        functools.partial(plan_kernel, sections, cap, tok_rows),
        [SMEM, SMEM],
        [shape((sections * slots,), I32), shape((slots + 1,), I32), shape((1, micros * tok_rows), I32)]
        + [shape((sections * slots,), I32), shape((slots + 1,), I32)],
        [SMEM, SMEM, VMEM, SMEM, SMEM],
        [pltpu.SMEM((micros * tok_rows,), I32)] * 3 + [pltpu.SMEM((sections * slots,), I32)],
    )(info, place)
    saved_t = saved_u.reshape(micros * dp_count * cap, hid).T
    saved_here = in_vmem(saved_u)

    sent, row_in = send(number(1), True, rounds_of, own_plan)
    swapped, kept1, (note, note_later, most) = one_pass(number(1), 1, swap(sent, "dp", same_core))
    news1 = swap(make_news(number(1), rounds_of, row_in, swapped), "section")
    sent, row_in = send(number(2), False, rounds_of, own_plan, news1)
    swapped, kept2, _ = one_pass(number(2), 2, swap(sent, "dp", same_core), note)
    news2 = swap(make_news(number(2), rounds_of, row_in, swapped), "section")
    sent, row_in = send(number(3), False, rounds_of, own_plan, news1, news2)
    swapped, kept3, _ = one_pass(number(3), 2, swap(sent, "dp", same_core), note)
    news3 = make_news(number(3), rounds_of, row_in, swapped)
    news3, *grads = lax.optimization_barrier((swap(news3, "section"), *gradients([kept1, kept2, kept3])))

    def more(state):
        return state[0] < most[0]

    def again(state):
        done, table, *grads = state
        now = (done + 1).reshape(1)
        sent, row_in = send(now, False, *again_plan, news1, news2, news3, table)
        swapped, kept, _ = one_pass(now, 2, swap(sent, "dp", same_core), note_later)
        news = swap(make_news(now, again_plan[0], row_in, swapped), "section")
        table = call(merge_kernel, [SMEM] * 2 + [VMEM] * 2, shape(table.shape, BF), VMEM)(now, again_plan[0], table, news)
        return done + 1, table, *gradients([kept], grads)

    table = jnp.zeros((sections, slots, width), BF)
    _, table, grad_up, grad_down = lax.while_loop(more, again, (jnp.int32(UNROLLED), table, *grads))
    in_grad = call(
        output_kernel,
        [SMEM] + [VMEM] * (3 + UNROLLED),
        shape((1, micros, tok_rows, width), BF),
        ANY,
        [pltpu.VMEM(out_grad.shape, BF), pltpu.SemaphoreType.DMA((len(chunks(width)),))],
    )(again_plan[0], source, out_grad, news1, news2, news3, table)
    return (in_grad, grad_up, grad_down)


def solution(mesh):
    return jax.shard_map(
        per_device,
        mesh=mesh,
        in_specs=(
            P(None, "dp", None),
            P("section", None, None, None),
            P("section", None, None, "dp"),
            P("section", "dp", None),
            P("section", "dp", None),
            P("section", None, "dp"),
            P("section", None, "dp"),
            P("section", None, "dp"),
        ),
        out_specs=(
            P("section", None, "dp", None),
            P("section", "dp", None),
            P("section", "dp", None),
        ),
        check_vma=False,
    )
```

time: 821 us -> 174 us (0.21)
  waiting for transfers between devices: 318 us -> 21.1 us
  blocking collectives: 219 us -> 107 us
  matrix products: 94.3 us -> 0 us
  other arithmetic: 73.6 us -> 1.3 us
  starting transfers between devices: 62.3 us -> 13.2 us
  local copies, waits for them, and re-layouts: 43.5 us -> 2.99 us
  Pallas kernels: 0 us -> 25.8 us
    all_gather x9 -> x0, blocking collectives: 219 us -> none  [tick_step(): row_piece = lax.all_gather(scaled, 'dp', axis=0, tiled=True)]
    all_to_all x9 -> x2, waiting for transfers between devices: 190 us -> 11.2 us  [swap(): lax.all_to_all(block, axis, 0, 0, tiled=True, axis_index_groups=groups)]
    ppermute x9 -> x6, waiting for transfers between devices: 128 us -> 9.93 us  [the longest x3 5.17 us: one_pass(): other = lax.ppermute(own, 'dp', sibling)]
    all_to_all x0 -> x8, blocking collectives: none -> 107 us  [swap(): lax.all_to_all(block, axis, 0, 0, tiled=True, axis_index_groups=groups)]
    dot_general x36 -> x0, matrix products: 94.3 us -> none  [the longest x9 42.7 us: tick_step(): jnp.einsum('rh,rd->hd', hidden_grad, x_rows[0, micro_pick], preferred_ele...]
    all_to_all x9 -> x2, starting transfers between devices: 50.8 us -> 12.5 us  [swap(): lax.all_to_all(block, axis, 0, 0, tiled=True, axis_index_groups=groups)]
    reshape x9 -> x1, local copies, waits for them, and re-layouts: 28.1 us -> 0.11 us  [per_device(): saved_t = saved_u.reshape(micros * dp_count * cap, hid).T]
    select_n x27 -> x0, other arithmetic: 26.6 us -> none  [the longest x9 20.6 us: tick_step(): jnp.where(valid_tick, lax.dynamic_update_index_in_dim(in_grad, new_slab,...]
  transfers between devices with their start and end apart: 18 -> 8, of which waited for: 18 -> 8; matrix products, arithmetic and copies ran while one was open for 7% -> 0% of each run, Pallas kernels for 0% -> 3%
where the time goes in v5:
time: 174 us; the launch traced here: 173 us
  blocking collectives  107 us (61%)
  Pallas kernels  25.8 us (15%)
  waiting for transfers between devices  21.1 us (12%)
  starting transfers between devices  13.2 us (8%)
  local copies, waits for them, and re-layouts  2.99 us (2%)
    all_to_all x8, blocking collectives, swap(): lax.all_to_all(block, axis, 0, 0, tiled=True, axis_index_groups=groups)  107 us
    all_to_all x2, starting transfers between devices, swap(): lax.all_to_all(block, axis, 0, 0, tiled=True, axis_index_groups=groups)  12.5 us
    all_to_all x2, waiting for transfers between devices, swap(): lax.all_to_all(block, axis, 0, 0, tiled=True, axis_index_groups=groups)  11.2 us
    pallas_call x3, Pallas kernels, one_pass(): call(functools.partial(pass_kernel, ROOM, late, cap), [SMEM, SMEM] + [VME...  7.12 us
    ppermute x3, waiting for transfers between devices, one_pass(): other = lax.ppermute(own, 'dp', sibling)  5.17 us
    ppermute x3, waiting for transfers between devices, one_pass(): arrived = lax.ppermute(theirs, 'dp', sibling)  4.76 us
    pallas_call x1, Pallas kernels, gradients(): call(functools.partial(grads_kernel, len(kept)), [VMEM, ANY] + [VMEM] * (...  3.92 us
    pallas_call x3, Pallas kernels, send(): call(functools.partial(send_kernel, sections, news, len(held) - news, not...  3.49 us
  transfers between devices with their start and end apart: 8, of which 8 were waited for; matrix products, arithmetic and copies ran while one was open for 0% of the time, Pallas kernels for 3%

profile of v5, /device:TPU:8, one launch (start us, length us, event | category | flops | bytes accessed | tf_op | source)
XLA Modules:
  0.0 173.1 jit_solution(6366652355586254667)
XLA Ops:
  0.6 0.0 copy-start.3
  0.6 0.6 copy-done.3
  1.3 1.3 shard_map.103
  2.6 8.5 %all-to-all-start.3 = ((s32[8,1,128]{2,1,0:T(1,128)}), s32[8,1,128]{2,1,0:T(1,128)S(1)}, u32[]{:S(2)}, u32[]{:S(2)}) async-start(s32[8,1,128]{2,1,0:T(1,128)} %shard_map.103), calls=%async_computation.3 | async-start | bytes 8192 | tf_op jit(solution)/shard_map/all_to_all | solution.py:421
  11.0 0.0 copy-start
  11.0 1.4 copy-done
  12.5 0.0 copy-start.2
  12.5 0.0 copy-start.4
  12.5 1.1 shard_map.104.first_ref
  13.6 5.1 %all-to-all-done.3.info_ref = s32[8,1,128]{2,1,0:T(1,128)S(1)} async-done(((s32[8,1,128]{2,1,0:T(1,128)}), s32[8,1,128]{2,1,0:T(1,128)S(1)}, u32[]{:S(2)}, u32[]{:S(2)}) %all-to-all-start.3) | async-done | bytes 4128 | tf_op jit(solution)/shard_map/all_to_all | solution.py:421
  18.6 2.9 %shard_map.105 = (s32[32]{0:T(128)S(1)}, s32[5]{0:T(128)S(1)}, s32[1,128]{1,0:T(1,128)S(1)}, s32[32]{0:T(128)}, s32[5]{0:T(128)}) custom-call(s32[8,1,128]{2,1,0:T(1,128)S(1)} %all-to-all-done.3.info_ref, s32[1]{0:T(128)} %bitcast.3.place_ref), custom_call_target="tpu_custom_call" | custom-call | flops 1000000 | bytes 1000000 | tf_op jit(solution)/shard_map/pallas_call | solution.py:483
  21.5 0.9 shard_map.106
  22.4 14.7 %all_to_all.68.own_ref.refs_2_ = bf16[16,2,6272]{2,1,0:T(2,128)(2,1)S(1)} all-to-all(bf16[16,2,6272]{2,1,0:T(2,128)(2,1)S(1)} %get-tuple-element.161), channel_id=1, replica_groups={{0,2,4,6,8,10,12,14,16,18,20,22,24,26,28,30},{1,3,5,7,9,11,13,15,17,19,..., dimensions={0} | all-to-all | bytes 802816 | tf_op jit(solution)/shard_map/all_to_all | solution.py:421
  37.1 0.0 collective-permute-start.2
  37.1 1.7 %collective-permute-done.2.other_ref.refs_3_ = bf16[16,2,6272]{2,1,0:T(2,128)(2,1)S(1)} collective-permute-done((bf16[16,2,6272]{2,1,0:T(2,128)(2,1)S(1)}, bf16[16,2,6272]{2,1,0:T(2,128)(2,1)S(1)}, u32[]{:S(2)}, u32[]{:S(2)}) %collective-permute-start.2) | collective-permute-done | bytes 401440 | tf_op jit(solution)/shard_map/ppermute | solution.py:440
  38.9 0.0 copy-done.2
  38.9 0.0 copy-done.4
  38.9 3.7 %shard_map.107 = (f32[16,2,6144]{2,1,0:T(2,128)S(1)}, bf16[16,2,6144]{2,1,0:T(2,128)(2,1)S(1)}, bf16[64,168]{1,0:T(8,128)(2,1)S(1)}, bf16[64,128]{1,0:T(8,128)(2...) custom-call(s32[1]{0:T(128)} %bitcast.4.core_ref, s32[1]{0:T(128)} %constant.25.clone.1.now_ref, ...), custom_call_target="tpu_custom_call" | custom-call | flops 264241152 | bytes 7274496 | tf_op jit(solution)/shard_map/pallas_call | solution.py:445
  42.6 0.2 collective-permute-start.3
  42.8 1.6 collective-permute-done.3
  44.4 0.0 copy-start.5
  44.4 0.0 copy-start.6
  44.4 0.4 add_convert_fusion.3
  44.9 13.9 %all_to_all.69.swapped_ref = bf16[16,2,6144]{2,1,0:T(2,128)(2,1)S(1)} all-to-all(bf16[16,2,6144]{2,1,0:T(2,128)(2,1)S(1)} %add_convert_fusion.3), channel_id=1, replica_groups={{0,2,4,6,8,10,12,14,16,18,20,22,24,26,28,30},{1,3,5,7,9,11,13,15,17,19,..., dimensions={0} | all-to-all | bytes 786432 | tf_op jit(solution)/shard_map/all_to_all | solution.py:421
  58.8 0.8 shard_map.108
  59.6 13.2 %all_to_all.70.refs_0_ = bf16[8,2,6144]{2,1,0:T(2,128)(2,1)} all-to-all(bf16[8,2,6144]{2,1,0:T(2,128)(2,1)S(1)} %shard_map.108), channel_id=1, replica_groups=mesh['section'=8,'dp'=32] {'section'}, dimensions={0} | all-to-all | bytes 393216 | tf_op jit(solution)/shard_map/all_to_all | solution.py:421
  72.8 1.2 shard_map.109
  74.1 12.4 %all_to_all.71.own_ref.refs_6_ = bf16[16,2,6144]{2,1,0:T(2,128)(2,1)S(1)} all-to-all(bf16[16,2,6144]{2,1,0:T(2,128)(2,1)S(1)} %get-tuple-element.165), channel_id=1, replica_groups={{0,2,4,6,8,10,12,14,16,18,20,22,24,26,28,30},{1,3,5,7,9,11,13,15,17,19,..., dimensions={0} | all-to-all | bytes 786432 | tf_op jit(solution)/shard_map/all_to_all | solution.py:421
  86.5 0.0 collective-permute-start.4
  86.5 1.7 collective-permute-done.4.other_ref.refs_7_
  88.2 0.0 copy-done.5
  88.2 0.0 copy-done.6
  88.2 1.7 shard_map.110
  89.9 0.2 collective-permute-start.5
  90.2 1.6 collective-permute-done.5
  91.8 0.4 add_convert_fusion.2
  92.2 13.6 %all_to_all.72.swapped_ref = bf16[16,2,6144]{2,1,0:T(2,128)(2,1)S(1)} all-to-all(bf16[16,2,6144]{2,1,0:T(2,128)(2,1)S(1)} %add_convert_fusion.2), channel_id=1, replica_groups={{0,2,4,6,8,10,12,14,16,18,20,22,24,26,28,30},{1,3,5,7,9,11,13,15,17,19,..., dimensions={0} | all-to-all | bytes 786432 | tf_op jit(solution)/shard_map/all_to_all | solution.py:421
  105.8 0.8 shard_map.111
  106.7 13.2 %all_to_all.73.refs_1_ = bf16[8,2,6144]{2,1,0:T(2,128)(2,1)} all-to-all(bf16[8,2,6144]{2,1,0:T(2,128)(2,1)S(1)} %shard_map.111), channel_id=1, replica_groups=mesh['section'=8,'dp'=32] {'section'}, dimensions={0} | all-to-all | bytes 393216 | tf_op jit(solution)/shard_map/all_to_all | solution.py:421
  119.9 1.4 shard_map.112
  121.3 12.4 %all_to_all.74.own_ref.refs_10_ = bf16[16,2,6144]{2,1,0:T(2,128)(2,1)S(1)} all-to-all(bf16[16,2,6144]{2,1,0:T(2,128)(2,1)S(1)} %get-tuple-element.170), channel_id=1, replica_groups={{0,2,4,6,8,10,12,14,16,18,20,22,24,26,28,30},{1,3,5,7,9,11,13,15,17,19,..., dimensions={0} | all-to-all | bytes 786432 | tf_op jit(solution)/shard_map/all_to_all | solution.py:421
  133.7 0.0 collective-permute-start.6
  133.7 1.7 collective-permute-done.6.other_ref.refs_11_
  135.4 1.7 shard_map.113
  137.1 0.2 collective-permute-start.7
  137.3 1.6 collective-permute-done.7
  138.9 0.4 add_convert_fusion.1
  139.4 13.6 %all_to_all.75.swapped_ref = bf16[16,2,6144]{2,1,0:T(2,128)(2,1)S(1)} all-to-all(bf16[16,2,6144]{2,1,0:T(2,128)(2,1)S(1)} %add_convert_fusion.1), channel_id=1, replica_groups={{0,2,4,6,8,10,12,14,16,18,20,22,24,26,28,30},{1,3,5,7,9,11,13,15,17,19,..., dimensions={0} | all-to-all | bytes 786432 | tf_op jit(solution)/shard_map/all_to_all | solution.py:421
  153.0 1.5 shard_map.114
  154.5 4.0 %all-to-all-start.12 = ((bf16[8,2,6144]{2,1,0:T(2,128)(2,1)}), bf16[8,2,6144]{2,1,0:T(2,128)(2,1)}, u32[]{:S(2)}, u32[]{:S(2)}) async-start(bf16[8,2,6144]{2,1,0:T(2,128)(2,1)} %shard_map.114), calls=%async_computation.12 | async-start | bytes 393216 | tf_op jit(solution)/shard_map/all_to_all | solution.py:421
  158.5 0.1 copy.12
  158.6 3.9 %shard_map.115 = (bf16[1,168,6144]{2,1,0:T(8,128)(2,1)}, bf16[1,168,6144]{2,1,0:T(8,128)(2,1)}) custom-call(bf16[168,128]{1,0:T(8,128)(2,1)S(1)} %bitcast.12, bf16[1,2,64,6144]{3,2,1,0:T(8,128)(2,1)} %x_any.1, bf16[64,168]{1,0:T(8,128)(2,1)S(1)} %get-tuple-element.173.refs_0_, bf16[64,128]{1,0:T(8,128)(2,1)S(1)} %get-tuple-element.174.refs_1_, ...), custom_call_target="tpu_custom_call" | custom-call | flops 1056964608 | bytes 8257536 | tf_op jit(solution)/shard_map/pallas_call | solution.py:466
  162.6 6.1 %all-to-all-done.12.refs_2_ = bf16[8,2,6144]{2,1,0:T(2,128)(2,1)} async-done(((bf16[8,2,6144]{2,1,0:T(2,128)(2,1)}), bf16[8,2,6144]{2,1,0:T(2,128)(2,1)}, u32[]{:S(2)}, u32[]{:S(2)}) %all-to-all-start.12) | async-done | bytes 196640 | tf_op jit(solution)/shard_map/all_to_all | solution.py:421
  168.7 0.1 broadcast_in_dim.3
  168.8 0.0 copy-start.1
  168.8 0.7 while.14
  169.5 0.7 copy-done.1
  170.2 2.7 %shard_map.116 = bf16[1,2,64,6144]{3,2,1,0:T(8,128)(2,1)} custom-call(s32[32]{0:T(128)} %get-tuple-element.382.round_ref, s32[1,128]{1,0:T(1,128)S(1)} %get-tuple-element.156.source_ref, bf16[2,64,6144]{2,1,0:T(8,128)(2,1)S(1)} %copy-done.1, bf16[8,2,6144]{2,1,0:T(2,128)(2,1)} %all_to_all.70.refs_0_, bf16[8,2,6144]{2,1,0:T(2,128)(2,1)} %all_to_all.73.refs_1_, ...), custom_call_target="tpu_custom_call" | custom-call | flops 1000000 | bytes 1000000 | tf_op jit(solution)/shard_map/pallas_call | solution.py:519
Async XLA Ops:
  0.6 0.7 copy-start.3
  2.6 16.1 %all-to-all-start.3 = ((s32[8,1,128]{2,1,0:T(1,128)}), s32[8,1,128]{2,1,0:T(1,128)S(1)}, u32[]{:S(2)}, u32[]{:S(2)}) async-start(s32[8,1,128]{2,1,0:T(1,128)} %shard_map.103), calls=%async_computation.3 | async-start | bytes 8192 | tf_op jit(solution)/shard_map/all_to_all | solution.py:421
  11.0 1.4 copy-start
  12.5 26.4 %copy-start.2 = (bf16[1,2,64,168]{3,2,1,0:T(8,128)(2,1)S(1)}, bf16[1,2,64,168]{3,2,1,0:T(8,128)(2,1)}, u32[]{:S(2)}) copy-start(bf16[1,2,64,168]{3,2,1,0:T(8,128)(2,1)} %saved_ref.5) | copy-start | bytes 129028
  12.5 26.4 %copy-start.4 = (bf16[1,168,6144]{2,1,0:T(8,128)(2,1)S(1)}, bf16[1,168,6144]{2,1,0:T(8,128)(2,1)}, u32[]{:S(2)}) copy-start(bf16[1,168,6144]{2,1,0:T(8,128)(2,1)} %down_ref.5) | copy-start | bytes 6193156
  37.1 1.7 %collective-permute-start.2 = (bf16[16,2,6272]{2,1,0:T(2,128)(2,1)S(1)}, bf16[16,2,6272]{2,1,0:T(2,128)(2,1)S(1)}, u32[]{:S(2)}, u32[]{:S(2)}) collective-permute-start(bf16[16,2,6272]{2,1,0:T(2,128)(2,1)S(1)} %all_to_all.68.own_ref.refs_2_), channel_id=1, source_target_pairs={{0,1},{1,0},{2,3},{3,2},{4,5},{5,4},{6,7},{7,6},{8,9},{9,8},{10,11... | collective-permute-start | bytes 1204232 | tf_op jit(solution)/shard_map/ppermute | solution.py:440
  42.6 1.8 %collective-permute-start.3 = (bf16[16,2,6144]{2,1,0:T(2,128)(2,1)S(1)}, bf16[16,2,6144]{2,1,0:T(2,128)(2,1)S(1)}, u32[]{:S(2)}, u32[]{:S(2)}) collective-permute-start(bf16[16,2,6144]{2,1,0:T(2,128)(2,1)S(1)} %get-tuple-element.163), channel_id=1, source_target_pairs={{0,1},{1,0},{2,3},{3,2},{4,5},{5,4},{6,7},{7,6},{8,9},{9,8},{10,11... | collective-permute-start | bytes 1179656 | tf_op jit(solution)/shard_map/ppermute | solution.py:453
  44.4 43.8 %copy-start.5 = (bf16[1,168,6144]{2,1,0:T(8,128)(2,1)S(1)}, bf16[1,168,6144]{2,1,0:T(8,128)(2,1)}, u32[]{:S(2)}) copy-start(bf16[1,168,6144]{2,1,0:T(8,128)(2,1)} %down_ref.5) | copy-start | bytes 6193156
  44.4 43.8 %copy-start.6 = (bf16[1,168,6144]{2,1,0:T(8,128)(2,1)S(1)}, bf16[1,168,6144]{2,1,0:T(8,128)(2,1)}, u32[]{:S(2)}) copy-start(bf16[1,168,6144]{2,1,0:T(8,128)(2,1)} %up_ref.5) | copy-start | bytes 6193156
  86.5 1.7 collective-permute-start.4
  89.9 1.8 %collective-permute-start.5 = (bf16[16,2,6144]{2,1,0:T(2,128)(2,1)S(1)}, bf16[16,2,6144]{2,1,0:T(2,128)(2,1)S(1)}, u32[]{:S(2)}, u32[]{:S(2)}) collective-permute-start(bf16[16,2,6144]{2,1,0:T(2,128)(2,1)S(1)} %get-tuple-element.168), channel_id=1, source_target_pairs={{0,1},{1,0},{2,3},{3,2},{4,5},{5,4},{6,7},{7,6},{8,9},{9,8},{10,11... | collective-permute-start | bytes 1179656 | tf_op jit(solution)/shard_map/ppermute | solution.py:453
  133.7 1.7 collective-permute-start.6
  137.1 1.8 %collective-permute-start.7 = (bf16[16,2,6144]{2,1,0:T(2,128)(2,1)S(1)}, bf16[16,2,6144]{2,1,0:T(2,128)(2,1)S(1)}, u32[]{:S(2)}, u32[]{:S(2)}) collective-permute-start(bf16[16,2,6144]{2,1,0:T(2,128)(2,1)S(1)} %get-tuple-element.172), channel_id=1, source_target_pairs={{0,1},{1,0},{2,3},{3,2},{4,5},{5,4},{6,7},{7,6},{8,9},{9,8},{10,11... | collective-permute-start | bytes 1179656 | tf_op jit(solution)/shard_map/ppermute | solution.py:453
  154.5 14.2 %all-to-all-start.12 = ((bf16[8,2,6144]{2,1,0:T(2,128)(2,1)}), bf16[8,2,6144]{2,1,0:T(2,128)(2,1)}, u32[]{:S(2)}, u32[]{:S(2)}) async-start(bf16[8,2,6144]{2,1,0:T(2,128)(2,1)} %shard_map.114), calls=%async_computation.12 | async-start | bytes 393216 | tf_op jit(solution)/shard_map/all_to_all | solution.py:421
  168.8 1.4 copy-start.1
